TPU v7x, 32 devices: a whole 2x2x4 slice. The times are simulated.
32 devices in a mesh: dp: 4 (over x, core), seq: 8 (over z, y).
Axes of the slice: x: 2, y: 2, z: 4, core: 2. Of those that a mesh axis runs over, the one named last changes fastest.
Arguments:
- inputs: bfloat16 [4, 1024, 2048], P('dp', 'seq'), may hold values from -6 to 6
- doc_lengths: int32 [4, 8], P('dp'), may hold values from 1 to 960, 1024 in all within a row
- w_query: bfloat16 [2048, 2048], P(('dp', 'seq')), may hold values from -0.125 to 0.125
- w_key: bfloat16 [2048, 2048], P(('dp', 'seq')), may hold values from -0.125 to 0.125
- w_value: bfloat16 [2048, 2048], P(('dp', 'seq')), may hold values from -0.125 to 0.125
- w_out: bfloat16 [2048, 2048], P(('dp', 'seq')), may hold values from -0.125 to 0.125
- gain_query: bfloat16 [2048], P(('dp', 'seq')), may hold values from 0.25 to 1.75
- gain_key: bfloat16 [2048], P(('dp', 'seq')), may hold values from 0.25 to 1.75
- gain_attn: bfloat16 [2048], P(('dp', 'seq')), may hold values from 0.25 to 1.75
- w_gate: bfloat16 [2048, 8192], P(('dp', 'seq')), may hold values from -0.125 to 0.125
- w_up: bfloat16 [2048, 8192], P(('dp', 'seq')), may hold values from -0.125 to 0.125
- w_down: bfloat16 [8192, 2048], P(None, ('dp', 'seq')), may hold values from -0.0625 to 0.0625
- gain_ffn: bfloat16 [2048], P(('dp', 'seq')), may hold values from 0.25 to 1.75
- cotangent: bfloat16 [4, 1024, 2048], P('dp', 'seq'), may hold values from -6 to 6
Outputs:
- out: bfloat16 [4, 1024, 2048], P('dp', 'seq')
- grad_inputs: float32 [4, 1024, 2048], P('dp', 'seq')
- grad_w_query: float32 [2048, 2048], P(('dp', 'seq'))
- grad_w_key: float32 [2048, 2048], P(('dp', 'seq'))
- grad_w_value: float32 [2048, 2048], P(('dp', 'seq'))
- grad_w_out: float32 [2048, 2048], P(('dp', 'seq'))
- grad_gain_query: float32 [2048], P(('dp', 'seq'))
- grad_gain_key: float32 [2048], P(('dp', 'seq'))
- grad_gain_attn: float32 [2048], P(('dp', 'seq'))
- grad_w_gate: float32 [2048, 8192], P(('dp', 'seq'))
- grad_w_up: float32 [2048, 8192], P(('dp', 'seq'))
- grad_w_down: float32 [8192, 2048], P(None, ('dp', 'seq'))
- grad_gain_ffn: float32 [2048], P(('dp', 'seq'))
Inputs may be any that keep to these rules, and one draw needn't show every extreme that they name: `doc_lengths`: each row's lengths sum to 1024, and one of them is 960.
All inputs are finite; a program needn't handle non-finite values.
Results may differ from a plain program's by a relative error of at most 0.019.
Values may be sent and summed in bfloat16 or wider, within the bound.
No kernel may reach another device: no remote copies, remote signals or barrier semaphores. Data moves between devices by JAX's collectives and lax.ppermute only.
A program may use at most 832 MiB of HBM per device.

v0:
```python
import math

import jax
import jax.numpy as jnp
from jax import lax
from jax.sharding import PartitionSpec as P

HEADS = 16
HEAD_DIM = 128


NORM_EPS = 1e-06
ROPE_BASE = 500000.0
MASK_FILL = -1e30


def matmul(left_mat, right_mat):
    return jnp.dot(left_mat, right_mat, preferred_element_type=jnp.float32)


def dot_right_t(left_mat, right_mat):
    return lax.dot_general(
        left_mat, right_mat, (((1,), (1,)), ((), ())), preferred_element_type=jnp.float32
    )


def dot_left_t(left_mat, right_mat):
    return lax.dot_general(
        left_mat, right_mat, (((0,), (0,)), ((), ())), preferred_element_type=jnp.float32
    )


def norm_apply(array_in, gain_vec):
    factor = lax.rsqrt(jnp.mean(array_in * array_in, axis=-1, keepdims=True) + NORM_EPS)
    return (array_in * factor * gain_vec, factor)


def norm_back(array_in, factor, gain_vec, grad_in):
    gain_term = jnp.sum(grad_in * array_in * factor, axis=0)
    scaled = grad_in * gain_vec
    grad_out = factor * scaled - array_in * (factor * factor * factor) * jnp.mean(
        scaled * array_in, axis=-1, keepdims=True
    )
    return (grad_out, gain_term)


def rotation(first_pos, tok_count):
    half_dim = HEAD_DIM // 2
    position = (first_pos + jnp.arange(tok_count)).astype(jnp.float32)
    inverse = jnp.exp(-(jnp.arange(half_dim).astype(jnp.float32) / half_dim) * math.log(ROPE_BASE))
    angles = position[:, None] * inverse[None, :]
    return (jnp.cos(angles)[None, :, None, :], jnp.sin(angles)[None, :, None, :])


def rotate(array_in, cosine, sine_t, turn_sign):
    half_dim = array_in.shape[-1] // 2
    first_half = array_in[..., :half_dim]
    second_half = array_in[..., half_dim:]
    return jnp.concatenate(
        [
            first_half * cosine - turn_sign * second_half * sine_t,
            second_half * cosine + turn_sign * first_half * sine_t,
        ],
        axis=-1,
    )


def body(
    inputs,
    doc_lengths,
    w_query,
    w_key,
    w_value,
    w_out,
    gain_query,
    gain_key,
    gain_attn,
    w_gate,
    w_up,
    w_down,
    gain_ffn,
    cotangent,
):
    row_count, tok_count, model_width = inputs.shape
    length = tok_count * lax.axis_size("seq")
    first_pos = lax.axis_index("seq") * tok_count
    score_scale = 1.0 / math.sqrt(HEAD_DIM)
    tokens = inputs.reshape(row_count * tok_count, model_width)

    def heads_first(array_in):
        return array_in.reshape(row_count, tok_count, HEADS, HEAD_DIM).transpose(2, 0, 1, 3)

    def heads_last(array_in):
        return array_in.transpose(1, 2, 0, 3).reshape(row_count * tok_count, HEADS * HEAD_DIM)

    full_q, full_k, full_v, full_o, full_gq, full_gk, full_ga = (
        lax.all_gather(w_query, ("dp", "seq"), axis=0, tiled=True),
        lax.all_gather(w_key, ("dp", "seq"), axis=0, tiled=True),
        lax.all_gather(w_value, ("dp", "seq"), axis=0, tiled=True),
        lax.all_gather(w_out, ("dp", "seq"), axis=0, tiled=True),
        lax.all_gather(gain_query, ("dp", "seq"), axis=0, tiled=True),
        lax.all_gather(gain_key, ("dp", "seq"), axis=0, tiled=True),
        lax.all_gather(gain_attn, ("dp", "seq"), axis=0, tiled=True),
    )
    cosine, sine_t = rotation(first_pos, tok_count)
    q_lin = matmul(tokens, full_q)
    k_lin = matmul(tokens, full_k)
    v_lin = matmul(tokens, full_v)
    q_norm, q_factor = norm_apply(q_lin, full_gq.astype(jnp.float32))
    k_norm, k_factor = norm_apply(k_lin, full_gk.astype(jnp.float32))
    queries = (
        rotate(q_norm.reshape(row_count, tok_count, HEADS, HEAD_DIM), cosine, sine_t, 1.0)
        .astype(jnp.bfloat16)
        .transpose(2, 0, 1, 3)
    )
    keys_mine = (
        rotate(k_norm.reshape(row_count, tok_count, HEADS, HEAD_DIM), cosine, sine_t, 1.0)
        .astype(jnp.bfloat16)
        .transpose(2, 0, 1, 3)
    )
    values_mine = heads_first(v_lin.astype(jnp.bfloat16))
    keys_all, values_all = (
        lax.all_gather(keys_mine, "seq", axis=2, tiled=True),
        lax.all_gather(values_mine, "seq", axis=2, tiled=True),
    )
    doc_ends = jnp.cumsum(doc_lengths, axis=1)
    position = jnp.arange(length)
    doc_ids = jnp.sum((position[None, :, None] >= doc_ends[:, None, :]).astype(jnp.int32), axis=2)
    my_pos = first_pos + jnp.arange(tok_count)
    docs_mine = lax.dynamic_slice_in_dim(doc_ids, first_pos, tok_count, 1)
    allowed = (position[None, None, :] <= my_pos[None, :, None]) & (
        doc_ids[:, None, :] == docs_mine[:, :, None]
    )

    def scores_of(q_head, k_head):
        raw_scores = (
            jnp.einsum("rtd,rkd->rtk", q_head, k_head, preferred_element_type=jnp.float32)
            * score_scale
        )
        return jnp.where(allowed, raw_scores, MASK_FILL)

    def attend(head_item):
        q_head, k_head, v_head = head_item
        scores = scores_of(q_head, k_head)
        row_max = jnp.max(scores, axis=-1, keepdims=True)
        row_total = row_max + jnp.log(jnp.sum(jnp.exp(scores - row_max), axis=-1, keepdims=True))
        attn_probs = jnp.exp(scores - row_total).astype(jnp.bfloat16)
        head_out = jnp.einsum(
            "rtk,rkd->rtd", attn_probs, v_head, preferred_element_type=jnp.float32
        )
        return (head_out, row_total[..., 0])

    attn_mixed, totals = lax.map(attend, (queries, keys_all, values_all))
    attended = heads_last(attn_mixed.astype(jnp.bfloat16))
    branch = matmul(attended, full_o)
    branch_norm, branch_factor = norm_apply(branch, full_ga.astype(jnp.float32))
    hidden = tokens.astype(jnp.float32) + branch_norm
    hidden_low = hidden.astype(jnp.bfloat16)
    gate_full, up_full, down_full, ffn_gain_full = (
        lax.all_gather(w_gate, ("dp", "seq"), axis=0, tiled=True),
        lax.all_gather(w_up, ("dp", "seq"), axis=0, tiled=True),
        lax.all_gather(w_down, ("dp", "seq"), axis=1, tiled=True),
        lax.all_gather(gain_ffn, ("dp", "seq"), axis=0, tiled=True),
    )
    gate_act = matmul(hidden_low, gate_full)
    upward = matmul(hidden_low, up_full)
    gate_sig = jax.nn.sigmoid(gate_act)
    active = (gate_act * gate_sig * upward).astype(jnp.bfloat16)
    result = matmul(active, down_full)
    result_norm, result_factor = norm_apply(result, ffn_gain_full.astype(jnp.float32))
    output = (hidden + result_norm).astype(jnp.bfloat16).reshape(row_count, tok_count, model_width)
    grad_top = cotangent.reshape(row_count * tok_count, model_width).astype(jnp.float32)
    grad_result, ffn_gain_term = norm_back(
        result, result_factor, ffn_gain_full.astype(jnp.float32), grad_top
    )
    grad_result = grad_result.astype(jnp.bfloat16)
    grad_active = dot_right_t(grad_result, down_full)
    grad_gate = (grad_active * upward * gate_sig * (1.0 + gate_act * (1.0 - gate_sig))).astype(
        jnp.bfloat16
    )
    grad_up = (grad_active * gate_act * gate_sig).astype(jnp.bfloat16)
    grad_hidden = grad_top + dot_right_t(grad_gate, gate_full) + dot_right_t(grad_up, up_full)
    feedforward_grads = lax.psum_scatter(
        jnp.concatenate(
            [
                dot_left_t(hidden_low, grad_gate),
                dot_left_t(hidden_low, grad_up),
                dot_left_t(grad_result, active),
            ],
            axis=1,
        ),
        ("dp", "seq"),
        scatter_dimension=0,
        tiled=True,
    )
    grad_branch, attn_gain_term = norm_back(
        branch, branch_factor, full_ga.astype(jnp.float32), grad_hidden
    )
    grad_branch = grad_branch.astype(jnp.bfloat16)
    back_q, back_k, back_v, back_o, back_gq, back_gk = (
        lax.all_gather(w_query, ("dp", "seq"), axis=0, tiled=True),
        lax.all_gather(w_key, ("dp", "seq"), axis=0, tiled=True),
        lax.all_gather(w_value, ("dp", "seq"), axis=0, tiled=True),
        lax.all_gather(w_out, ("dp", "seq"), axis=0, tiled=True),
        lax.all_gather(gain_query, ("dp", "seq"), axis=0, tiled=True),
        lax.all_gather(gain_key, ("dp", "seq"), axis=0, tiled=True),
    )
    grad_attended = dot_right_t(grad_branch, back_o).astype(jnp.bfloat16)
    grad_w_out_term = dot_left_t(attended, grad_branch)
    grad_mixed = heads_first(grad_attended)

    def head_back(head_item):
        q_head, k_head, v_head, g_head, t_head = head_item
        prob_full = jnp.exp(scores_of(q_head, k_head) - t_head[..., None])
        grad_probs = jnp.einsum("rtd,rkd->rtk", g_head, v_head, preferred_element_type=jnp.float32)
        offsets = jnp.sum(prob_full * grad_probs, axis=-1, keepdims=True)
        grad_scores = (prob_full * (grad_probs - offsets)).astype(jnp.bfloat16)
        grad_q = (
            jnp.einsum("rtk,rkd->rtd", grad_scores, k_head, preferred_element_type=jnp.float32)
            * score_scale
        )
        grad_k = (
            jnp.einsum("rtk,rtd->rkd", grad_scores, q_head, preferred_element_type=jnp.float32)
            * score_scale
        )
        grad_v = jnp.einsum(
            "rtk,rtd->rkd",
            prob_full.astype(jnp.bfloat16),
            g_head,
            preferred_element_type=jnp.float32,
        )
        return (grad_q, grad_k, grad_v)

    grad_queries, key_terms, value_terms = lax.map(
        head_back, (queries, keys_all, values_all, grad_mixed, totals)
    )
    grad_keys, grad_values = (
        lax.psum_scatter(
            key_terms.astype(jnp.bfloat16), "seq", scatter_dimension=2, tiled=True
        ).astype(jnp.float32),
        lax.psum_scatter(
            value_terms.astype(jnp.bfloat16), "seq", scatter_dimension=2, tiled=True
        ).astype(jnp.float32),
    )
    grad_q_norm = rotate(grad_queries.transpose(1, 2, 0, 3), cosine, sine_t, -1.0).reshape(
        row_count * tok_count, model_width
    )
    grad_k_norm = rotate(grad_keys.transpose(1, 2, 0, 3), cosine, sine_t, -1.0).reshape(
        row_count * tok_count, model_width
    )
    grad_q_lin, query_gain_term = norm_back(
        q_lin, q_factor, back_gq.astype(jnp.float32), grad_q_norm
    )
    grad_k_lin, key_gain_term = norm_back(k_lin, k_factor, back_gk.astype(jnp.float32), grad_k_norm)
    grad_q_lin = grad_q_lin.astype(jnp.bfloat16)
    grad_k_lin = grad_k_lin.astype(jnp.bfloat16)
    grad_v_lin = heads_last(grad_values).astype(jnp.bfloat16)
    grad_input = (
        grad_hidden
        + dot_right_t(grad_q_lin, back_q)
        + dot_right_t(grad_k_lin, back_k)
        + dot_right_t(grad_v_lin, back_v)
    )
    attention_grads = (
        lax.psum_scatter(
            dot_left_t(tokens, grad_q_lin), ("dp", "seq"), scatter_dimension=0, tiled=True
        ),
        lax.psum_scatter(
            dot_left_t(tokens, grad_k_lin), ("dp", "seq"), scatter_dimension=0, tiled=True
        ),
        lax.psum_scatter(
            dot_left_t(tokens, grad_v_lin), ("dp", "seq"), scatter_dimension=0, tiled=True
        ),
        lax.psum_scatter(grad_w_out_term, ("dp", "seq"), scatter_dimension=0, tiled=True),
        lax.psum_scatter(query_gain_term, ("dp", "seq"), scatter_dimension=0, tiled=True),
        lax.psum_scatter(key_gain_term, ("dp", "seq"), scatter_dimension=0, tiled=True),
        lax.psum_scatter(attn_gain_term, ("dp", "seq"), scatter_dimension=0, tiled=True),
        lax.psum_scatter(ffn_gain_term, ("dp", "seq"), scatter_dimension=0, tiled=True),
    )
    feed_width = w_gate.shape[1]
    grad_w_gate = feedforward_grads[:, :feed_width]
    grad_w_up = feedforward_grads[:, feed_width : 2 * feed_width]
    grad_w_down = feedforward_grads[:, 2 * feed_width :].T
    return (
        output,
        grad_input.reshape(row_count, tok_count, model_width),
        attention_grads[0],
        attention_grads[1],
        attention_grads[2],
        attention_grads[3],
        attention_grads[4],
        attention_grads[5],
        attention_grads[6],
        grad_w_gate,
        grad_w_up,
        grad_w_down,
        attention_grads[7],
    )


def solution(mesh):
    return jax.shard_map(
        body,
        mesh=mesh,
        in_specs=(
            P("dp", "seq", None),
            P("dp", None),
            P(("dp", "seq"), None),
            P(("dp", "seq"), None),
            P(("dp", "seq"), None),
            P(("dp", "seq"), None),
            P(("dp", "seq")),
            P(("dp", "seq")),
            P(("dp", "seq")),
            P(("dp", "seq"), None),
            P(("dp", "seq"), None),
            P(None, ("dp", "seq")),
            P(("dp", "seq")),
            P("dp", "seq", None),
        ),
        out_specs=(
            P("dp", "seq", None),
            P("dp", "seq", None),
            P(("dp", "seq"), None),
            P(("dp", "seq"), None),
            P(("dp", "seq"), None),
            P(("dp", "seq"), None),
            P(("dp", "seq")),
            P(("dp", "seq")),
            P(("dp", "seq")),
            P(("dp", "seq"), None),
            P(("dp", "seq"), None),
            P(None, ("dp", "seq")),
            P(("dp", "seq")),
        ),
        check_vma=False,
    )
```

profile of v0, /device:TPU:25, one launch (start us, length us, event | category | flops | bytes accessed | tf_op | source)
XLA Modules:
  0.0 4514.1 jit_solution(14314143053071231867)
XLA Ops:
  9.5 78.9 %all-gather.16.cloned.1.call-done = bf16[2048,2048]{1,0:T(8,128)(2,1)} async-done(((bf16[64,2048]{1,0:T(8,128)(2,1)}), bf16[2048,2048]{1,0:T(8,128)(2,1)}) %all-gather.16.cloned.1.call-update) | async-done | bytes 8388624 | tf_op jit(solution)/shard_map/all_gather | solution.py:99
  88.4 4.8 fusion.52
  95.4 39.4 all-reduce.9
  135.8 31.8 all-gather.12.cloned.1.call-done
  167.7 4.7 multiply_reduce_fusion.7
  173.7 72.9 %all-gather.10.cloned.1.call-done = bf16[2048,2048]{1,0:T(8,128)(2,1)} async-done(((bf16[64,2048]{1,0:T(8,128)(2,1)}), bf16[2048,2048]{1,0:T(8,128)(2,1)}) %all-gather.10.cloned.1.call-update) | async-done | bytes 8388624 | tf_op jit(solution)/shard_map/all_gather | solution.py:97
  246.7 4.7 multiply_reduce_fusion.8
  259.5 61.2 %all-gather.18.cloned.1.call-done = bf16[16,1,1024,128]{3,2,1,0:T(8,128)(2,1)} async-done(((bf16[16,1,128,128]{3,2,1,0:T(8,128)(2,1)}), bf16[16,1,1024,128]{3,2,1,0:T(8,128)(2,1)}) %all-gather.18.cloned.1.call-update) | async-done | bytes 4194320 | tf_op jit(solution)/shard_map/all_gather | solution.py:124
  320.7 74.3 %all-gather.14.cloned.1.call-done = bf16[16,1,1024,128]{3,2,1,0:T(8,128)(2,1)} async-done(((bf16[16,1,128,128]{3,2,1,0:T(8,128)(2,1)}), bf16[16,1,1024,128]{3,2,1,0:T(8,128)(2,1)}) %all-gather.14.cloned.1.call-update) | async-done | bytes 4194320 | tf_op jit(solution)/shard_map/all_gather | solution.py:123
  395.0 46.2 %while.28 = (s32[]{:T(128)}, bf16[16,1,128,128]{2,3,0,1:T(8,128)(2,1)S(1)}, f32[16,1,128]{2,1,0:T(1,128)S(1)}, bf16[16,1,128,128]{3,2,1,0:T(8,128)(2,1)S(1)}, bf...) while((s32[]{:T(128)}, ...), condition=%wide.region_7.8_spmd.clone, body=%wide.region_4.7_spmd.clone.sunk | while | flops 68419456 | bytes 2206833 | solution.py:153
  441.2 33.2 all-gather.20.cloned.1.call-done
  474.4 4.7 multiply_reduce_fusion.6
  479.4 190.9 %all-gather.22.cloned.1.call-done = bf16[2048,8192]{1,0:T(8,128)(2,1)} async-done(((bf16[64,8192]{1,0:T(8,128)(2,1)}), bf16[2048,8192]{1,0:T(8,128)(2,1)}) %all-gather.22.cloned.1.call-update) | async-done | bytes 33554448 | tf_op jit(solution)/shard_map/all_gather | solution.py:160
  670.3 17.1 fusion.80
  687.4 178.9 %all-gather.24.cloned.1.call-done = bf16[2048,8192]{1,0:T(8,128)(2,1)} async-done(((bf16[64,8192]{1,0:T(8,128)(2,1)}), bf16[2048,8192]{1,0:T(8,128)(2,1)}) %all-gather.24.cloned.1.call-update) | async-done | bytes 33554448 | tf_op jit(solution)/shard_map/all_gather | solution.py:161
  866.3 19.9 multiply_convert_fusion.3
  886.2 176.1 %all-gather.26.cloned.1.call-done = bf16[8192,2048]{0,1:T(8,128)(2,1)} async-done(((bf16[8192,64]{0,1:T(8,128)(2,1)}), bf16[8192,2048]{0,1:T(8,128)(2,1)}) %all-gather.26.cloned.1.call-update) | async-done | bytes 33554448 | tf_op jit(solution)/shard_map/all_gather | solution.py:162
  1062.3 16.6 multiply_reduce_fusion.5
  1079.9 18.6 multiply_convert_fusion.1
  1098.4 17.4 convolution_add_fusion.1
  1115.8 17.7 multiply_reduce_fusion.1
  1134.9 6.5 fusion.53
  1141.7 105.4 %while.29 = (s32[]{:T(128)}, f32[16,1,128,128]{3,2,1,0:T(8,128)S(1)}, bf16[16,1,1024,128]{3,2,1,0:T(8,128)(2,1)}, bf16[16,1,1024,128]{2,3,0,1:T(8,128)(2,1)}, bf...) while((s32[]{:T(128)}, ...), condition=%wide.region_14.15_spmd.clone, body=%wide.region_12.14_spmd.clone.sunk | while | flops 169492352 | bytes 5976713 | solution.py:234
  1247.1 7.3 copy.77
  1254.4 6.3 copy.130
  1260.8 26.0 fusion.83
  1286.8 25.7 fusion.82
  1312.5 23.7 fusion.77
  1336.3 133.4 %pad_maximum_fusion = f32[2048,24576]{1,0:T(8,128)} fusion(f32[2048,8192]{1,0:T(8,128)} %fusion.77, f32[2048,8192]{1,0:T(8,128)} %fusion.83, f32[2048,8192]{1,0:T(8,128)} %fusion.82), kind=kLoop, calls=%fused_computation.62 | loop fusion | flops 100663296 | bytes 402653184 | tf_op jit(solution)/shard_map/concatenate | solution.py:184
  1470.9 11.0 fusion.81
  1484.1 11.7 convolution_bitcast_fusion.2
  1495.8 19.7 copy.83
  1517.2 2.0 multiply_subtract_fusion
  1521.6 11.6 convolution_bitcast_fusion.3
  1533.3 19.7 copy.81
  1553.3 2.5 pad_maximum_fusion.1
  1557.6 11.6 convolution_bitcast_fusion.4
  1569.2 19.7 copy.79
  1589.6 37.8 all-reduce.8
  1629.8 8.1 convolution_add_fusion.4
  1637.9 8.1 convolution_add_fusion.3
  1646.0 3.9 fusion.49
  1649.8 1416.9 %reduce-scatter.20.cloned.1.call-done = f32[64,24576]{1,0:T(8,128)} async-done(((f32[2048,24576]{1,0:T(8,128)}), f32[64,24576]{1,0:T(8,128)}) %reduce-scatter.20.cloned.1.call-update) | async-done | bytes 6291472 | tf_op jit(solution)/shard_map/reduce_scatter | solution.py:183
  3066.8 5.7 slice_bitcast_fusion
  3072.5 354.7 %reduce-scatter.18.cloned.1.call-done = f32[64,2048]{1,0:T(8,128)} async-done(((f32[2048,2048]{1,0:T(8,128)}), f32[64,2048]{1,0:T(8,128)}) %reduce-scatter.18.cloned.1.call-update) | async-done | bytes 524304 | tf_op jit(solution)/shard_map/reduce_scatter | solution.py:274
  3427.1 360.1 %reduce-scatter.28.cloned.1.call-done = f32[64,2048]{1,0:T(8,128)} async-done(((f32[2048,2048]{1,0:T(8,128)}), f32[64,2048]{1,0:T(8,128)}) %reduce-scatter.28.cloned.1.call-update) | async-done | bytes 524304
  3787.2 360.1 %reduce-scatter.26.cloned.1.call-done = f32[64,2048]{1,0:T(8,128)} async-done(((f32[2048,2048]{1,0:T(8,128)}), f32[64,2048]{1,0:T(8,128)}) %reduce-scatter.26.cloned.1.call-update) | async-done | bytes 524304
  4147.3 360.1 %reduce-scatter.24.cloned.1.call-done = f32[64,2048]{1,0:T(8,128)} async-done(((f32[2048,2048]{1,0:T(8,128)}), f32[64,2048]{1,0:T(8,128)}) %reduce-scatter.24.cloned.1.call-update) | async-done | bytes 524304
  (354 shorter events, 180.3 us)
Async XLA Ops:
  7.2 81.2 %all-gather.16.cloned.1.call-start = ((), (), s32[]{:S(2)}) async-start(), calls=%async_computation.10 | async-start | bytes 8650752 | tf_op jit(solution)/shard_map/all_gather | solution.py:99
  7.9 159.8 %all-gather.12.cloned.1.call-start = ((), (), s32[]{:S(2)}) async-start(), calls=%async_computation.8 | async-start | bytes 8650752 | tf_op jit(solution)/shard_map/all_gather | solution.py:98
  8.7 238.0 %all-gather.10.cloned.1.call-start = ((), (), s32[]{:S(2)}) async-start(), calls=%async_computation.7 | async-start | bytes 8650752 | tf_op jit(solution)/shard_map/all_gather | solution.py:97
  9.4 85.0 %copy-start.34 = (bf16[64]{0:T(256)(128)(2,1)S(1)}, bf16[64]{0:T(256)(128)(2,1)}, u32[]{:S(2)}) copy-start(bf16[64]{0:T(256)(128)(2,1)} %param.26) | copy-start | bytes 388
  9.4 85.3 %copy-start.35 = (bf16[64]{0:T(256)(128)(2,1)S(1)}, bf16[64]{0:T(256)(128)(2,1)}, u32[]{:S(2)}) copy-start(bf16[64]{0:T(256)(128)(2,1)} %param.25) | copy-start | bytes 388
  9.4 85.5 %copy-start.36 = (bf16[64]{0:T(256)(128)(2,1)S(1)}, bf16[64]{0:T(256)(128)(2,1)}, u32[]{:S(2)}) copy-start(bf16[64]{0:T(256)(128)(2,1)} %param.24) | copy-start | bytes 388
  9.4 85.7 %copy-start.37 = (bf16[64]{0:T(256)(128)(2,1)S(1)}, bf16[64]{0:T(256)(128)(2,1)}, u32[]{:S(2)}) copy-start(bf16[64]{0:T(256)(128)(2,1)} %param.30) | copy-start | bytes 388
  9.4 158.2 %copy-start = (bf16[1,128,2048]{2,1,0:T(8,128)(2,1)S(1)}, bf16[1,128,2048]{2,1,0:T(8,128)(2,1)}, u32[]{:S(2)}) copy-start(bf16[1,128,2048]{2,1,0:T(8,128)(2,1)} %param.18) | copy-start | bytes 1572868
  9.4 311.3 %all-gather.18.cloned.1.call-start = ((), (), s32[]{:S(2)}) async-start(), calls=%async_computation.11 | async-start | bytes 4718592 | tf_op jit(solution)/shard_map/all_gather | solution.py:124
  94.3 300.7 %all-gather.14.cloned.1.call-start = ((), (), s32[]{:S(2)}) async-start(), calls=%async_computation.9 | async-start | bytes 4718592 | tf_op jit(solution)/shard_map/all_gather | solution.py:123
  134.8 117.2 %copy-start.22 = (f32[2048]{0:T(1024)}, f32[2048]{0:T(1024)S(1)}, u32[]{:S(2)}) copy-start(f32[2048]{0:T(1024)S(1)} %convert_element_type.135) | copy-start | bytes 24580
  134.8 38.1 copy-start.24
  135.8 117.6 %copy-start.19 = (f32[128,64]{1,0:T(8,128)}, f32[128,64]{1,0:T(8,128)S(1)}, u32[]{:S(2)}) copy-start(f32[128,64]{1,0:T(8,128)S(1)} %get-tuple-element.303) | copy-start | bytes 98308
  173.0 78.4 %copy-start.30 = (f32[128]{0:T(128)}, f32[128]{0:T(128)S(1)}, u32[]{:S(2)}) copy-start(f32[128]{0:T(128)S(1)} %get-tuple-element.305) | copy-start | bytes 1540
  252.0 1.5 copy-start.28
  254.8 4.0 copy-start.38
  256.0 218.4 %all-gather.20.cloned.1.call-start = ((), (), s32[]{:S(2)}) async-start(), calls=%async_computation.12 | async-start | bytes 8650752 | tf_op jit(solution)/shard_map/all_gather | solution.py:100
  256.5 413.8 %all-gather.22.cloned.1.call-start = ((), (), s32[]{:S(2)}) async-start(), calls=%async_computation.13 | async-start | bytes 34603008 | tf_op jit(solution)/shard_map/all_gather | solution.py:160
  257.3 609.0 %all-gather.24.cloned.1.call-start = ((), (), s32[]{:S(2)}) async-start(), calls=%async_computation.14 | async-start | bytes 34603008 | tf_op jit(solution)/shard_map/all_gather | solution.py:161
  258.0 804.2 %all-gather.26.cloned.1.call-start = ((), (), s32[]{:S(2)}) async-start(), calls=%async_computation.15 | async-start | bytes 34603008 | tf_op jit(solution)/shard_map/all_gather | solution.py:162
  258.8 1223.7 %reduce-scatter.22.cloned.1.call-start = ((), (), s32[]{:S(2)}) async-start(), calls=%async_computation.19 | async-start | bytes 4718592
  441.2 33.2 copy-start.18
  441.2 37.9 copy-start.16
  1062.3 16.7 copy-start.11
  1133.5 7.9 copy-start.7
  1134.9 6.6 copy-start.9
  1134.9 6.8 copy-start.13
  1247.1 7.3 copy-start.14
  1260.8 254.9 %reduce-scatter.16.cloned.1.call-start = ((), (), s32[]{:S(2)}) async-start(), calls=%async_computation.16 | async-start | bytes 4718592 | tf_op jit(solution)/shard_map/reduce_scatter | solution.py:238
  1286.8 25.7 copy-start.6
  1286.8 25.7 copy-start.12
  1336.3 1730.5 %reduce-scatter.20.cloned.1.call-start = ((), (), s32[]{:S(2)}) async-start(), calls=%async_computation.18 | async-start | bytes 207618048 | tf_op jit(solution)/shard_map/reduce_scatter | solution.py:183
  1469.7 1957.4 %reduce-scatter.18.cloned.1.call-start = ((), (), s32[]{:S(2)}) async-start(), calls=%async_computation.17 | async-start | bytes 17301504 | tf_op jit(solution)/shard_map/reduce_scatter | solution.py:274
  1481.9 2.2 copy-start.1
  1481.9 2305.3 %reduce-scatter.28.cloned.1.call-start = ((), (), s32[]{:S(2)}) async-start(), calls=%async_computation.22 | async-start | bytes 17301504
  1515.5 1.7 copy-start.15
  1515.5 1.7 copy-start.20
  1515.5 1.7 copy-start.21
  1515.5 2631.8 %reduce-scatter.26.cloned.1.call-start = ((), (), s32[]{:S(2)}) async-start(), calls=%async_computation.21 | async-start | bytes 17301504
  1519.2 1.9 copy-start.33
  1553.0 3.4 copy-start.3
  1553.0 3.4 copy-start.23
  1553.0 3.4 copy-start.29
  1553.0 4.0 copy-start.32
  1553.0 2954.3 %reduce-scatter.24.cloned.1.call-start = ((), (), s32[]{:S(2)}) async-start(), calls=%async_computation.20 | async-start | bytes 17301504
  1588.9 40.9 copy-start.8
  1629.8 16.2 slice-start
  1637.9 8.1 slice-start.1
  (9 other events, 9.7 us)
Sparse Core Ops, SparseCore 0:
  11.0 77.3 all-gather.15
  91.4 76.2 all-gather.11
  170.7 75.9 all-gather.9
  249.3 71.3 all-gather.17
  323.3 71.6 all-gather.13
  397.8 76.5 all-gather.19
  477.4 192.8 all-gather.21
  673.3 192.9 all-gather.23
  869.3 192.9 all-gather.25
  1260.9 86.5 reduce-scatter.21
  1351.5 88.2 reduce-scatter.15
  1469.8 1596.8 reduce-scatter.19
  3069.6 357.4 reduce-scatter.17
  3429.8 357.3 reduce-scatter.27
  3789.9 357.3 reduce-scatter.25
  4150.0 357.3 reduce-scatter.23
where the time goes:
time: 4530 us; the launch traced here: 4510 us
  waiting for transfers between devices  3750 us (83%)
  matrix products  419 us (9%)
  other arithmetic  156 us (3%)
  local copies, waits for them, and re-layouts  90.5 us (2%)
  blocking collectives  77.2 us (2%)
    reduce_scatter x1, waiting for transfers between devices, body(): lax.psum_scatter(jnp.concatenate([dot_left_t(hidden_low, grad_gate), dot_...  1420 us
    unnamed x20, waiting for transfers between devices  1090 us
    reduce_scatter x1, waiting for transfers between devices, body(): lax.psum_scatter(grad_w_out_term, ('dp', 'seq'), scatter_dimension=0, til...  355 us
    all_gather x1, waiting for transfers between devices, body(): lax.all_gather(w_gate, ('dp', 'seq'), axis=0, tiled=True)  191 us
    all_gather x1, waiting for transfers between devices, body(): lax.all_gather(w_up, ('dp', 'seq'), axis=0, tiled=True)  179 us
    all_gather x1, waiting for transfers between devices, body(): lax.all_gather(w_down, ('dp', 'seq'), axis=1, tiled=True)  176 us
    concatenate x1, other arithmetic, body(): jnp.concatenate([dot_left_t(hidden_low, grad_gate), dot_left_t(hidden_low...  133 us
    dot_general x7, matrix products, dot_left_t(): lax.dot_general(left_mat, right_mat, (((0,), (0,)), ((), ())), preferred_...  121 us
  transfers between devices with their start and end apart: 16, of which 14 were waited for; matrix products, arithmetic and copies ran while one was open for 10% of the time, Pallas kernels for 0%

commit v1 on v0

--- a/solution.py
+++ b/solution.py
@@ -3,6 +3,7 @@
 import jax
 import jax.numpy as jnp
 from jax import lax
+from jax.sharding import Mesh
 from jax.sharding import PartitionSpec as P
 
 HEADS = 16
@@ -13,20 +14,29 @@
 ROPE_BASE = 500000.0
 MASK_FILL = -1e30
 
+SEQ = ("z", "y")
+DP = ("x", "core")
+FEED = ("core", "z")
+REST = ("x", "y")
+ALL = ("x", "core", "z", "y")
+SWAP = [(0, 1), (1, 0)]
+F32 = jnp.float32
+BF16 = jnp.bfloat16
+
 
 def matmul(left_mat, right_mat):
-    return jnp.dot(left_mat, right_mat, preferred_element_type=jnp.float32)
+    return jnp.dot(left_mat, right_mat, preferred_element_type=F32)
 
 
 def dot_right_t(left_mat, right_mat):
     return lax.dot_general(
-        left_mat, right_mat, (((1,), (1,)), ((), ())), preferred_element_type=jnp.float32
+        left_mat, right_mat, (((1,), (1,)), ((), ())), preferred_element_type=F32
     )
 
 
 def dot_left_t(left_mat, right_mat):
     return lax.dot_general(
-        left_mat, right_mat, (((0,), (0,)), ((), ())), preferred_element_type=jnp.float32
+        left_mat, right_mat, (((0,), (0,)), ((), ())), preferred_element_type=F32
     )
 
 
@@ -46,10 +56,10 @@
 
 def rotation(first_pos, tok_count):
     half_dim = HEAD_DIM // 2
-    position = (first_pos + jnp.arange(tok_count)).astype(jnp.float32)
-    inverse = jnp.exp(-(jnp.arange(half_dim).astype(jnp.float32) / half_dim) * math.log(ROPE_BASE))
+    position = (first_pos + jnp.arange(tok_count)).astype(F32)
+    inverse = jnp.exp(-(jnp.arange(half_dim).astype(F32) / half_dim) * math.log(ROPE_BASE))
     angles = position[:, None] * inverse[None, :]
-    return (jnp.cos(angles)[None, :, None, :], jnp.sin(angles)[None, :, None, :])
+    return (jnp.cos(angles)[:, None, :], jnp.sin(angles)[:, None, :])
 
 
 def rotate(array_in, cosine, sine_t, turn_sign):
@@ -65,7 +75,261 @@
     )
 
 
+def exchange(array_in, axes):
+    return lax.all_to_all(array_in, axes, split_axis=0, concat_axis=0, tiled=True)
+
+
+def spread(array_in, axes):
+    count = lax.axis_size(axes)
+    return exchange(jnp.broadcast_to(array_in[None], (count,) + array_in.shape), axes)
+
+
+def ring_pairs(count):
+    order = [0] + list(range(1, count, 2)) + [v for v in range(count - 1, 0, -1) if v % 2 == 0]
+    return [(order[i], order[(i + 1) % count]) for i in range(count)]
+
+
+def core_swap(array_in):
+    return lax.ppermute(array_in, "core", SWAP)
+
+
 def body(
+    inputs,
+    doc_lengths,
+    w_query,
+    w_key,
+    w_value,
+    w_out,
+    gain_query,
+    gain_key,
+    gain_attn,
+    w_gate,
+    w_up,
+    w_down,
+    gain_ffn,
+    cotangent,
+):
+    _, tok_count, model_width = inputs.shape
+    n_x, n_core, n_z, n_y = (lax.axis_size(a) for a in ALL)
+    n_seq, n_dp, n_all = n_z * n_y, n_x * n_core, n_x * n_core * n_z * n_y
+    seq_at = lax.axis_index(SEQ)
+    length = tok_count * n_seq
+    score_scale = 1.0 / math.sqrt(HEAD_DIM)
+    own_rows = w_query.shape[0]
+    own_width = model_width // n_seq
+    own_heads = own_width // HEAD_DIM
+    feed_width = w_gate.shape[1]
+    n_feed = n_core * n_z
+    own_feed = feed_width // n_feed
+    ring = ring_pairs(n_z)
+    tokens = inputs[0]
+
+    gains = spread(jnp.stack([gain_query, gain_key, gain_attn, gain_ffn]), ALL)
+    gains = gains.transpose(1, 0, 2).reshape(4, model_width).astype(F32)
+    my_gq = lax.dynamic_slice_in_dim(gains[0], seq_at * own_width, own_width)
+    my_gk = lax.dynamic_slice_in_dim(gains[1], seq_at * own_width, own_width)
+    gain_a, gain_f = gains[2], gains[3]
+
+    w_heads = jnp.stack([w_query, w_key, w_value])
+    w_heads = w_heads.reshape(3, own_rows, n_seq, own_width).transpose(2, 1, 0, 3)
+    w_heads = exchange(w_heads.reshape(n_seq, own_rows, 3 * own_width), SEQ)
+    w_heads = lax.all_gather(w_heads, DP, axis=0, tiled=True).reshape(model_width, 3 * own_width)
+    x_row = lax.all_gather(tokens, SEQ, axis=0, tiled=True)
+    full_o = lax.all_gather(w_out, ALL, axis=0, tiled=True)
+
+    w_feed = jnp.stack([w_gate, w_up, w_down.T])
+    w_feed = w_feed.reshape(3, own_rows, n_feed, own_feed).transpose(2, 0, 1, 3)
+    w_feed = exchange(w_feed, FEED)
+    w_feed = lax.all_gather(w_feed, REST, axis=0, tiled=False)
+    w_feed = w_feed.reshape(n_x, n_y, n_core, n_z, 3, own_rows, own_feed)
+    w_feed = w_feed.transpose(4, 0, 2, 3, 1, 5, 6).reshape(3, model_width, own_feed)
+    w_g, w_u, w_d = w_feed[0], w_feed[1], w_feed[2]
+
+    qkv = matmul(x_row, w_heads)
+    q_lin, k_lin, v_lin = (
+        qkv[:, :own_width],
+        qkv[:, own_width : 2 * own_width],
+        qkv[:, 2 * own_width :],
+    )
+    squares = jnp.stack([jnp.sum(q_lin * q_lin, axis=1), jnp.sum(k_lin * k_lin, axis=1)])
+    squares = jnp.sum(spread(squares, SEQ), axis=0) / model_width
+    factors = lax.rsqrt(squares + NORM_EPS)
+    q_factor, k_factor = factors[0][:, None], factors[1][:, None]
+    cosine, sine_t = rotation(0, length)
+
+    def to_heads(array_in, turn_sign):
+        heads = rotate(array_in.reshape(length, own_heads, HEAD_DIM), cosine, sine_t, turn_sign)
+        return heads.astype(BF16).transpose(1, 0, 2)
+
+    def from_heads(array_in):
+        return array_in.transpose(1, 0, 2).reshape(length, own_width)
+
+    queries = to_heads(q_lin * q_factor * my_gq, 1.0)
+    keys = to_heads(k_lin * k_factor * my_gk, 1.0)
+    values = v_lin.astype(BF16).reshape(length, own_heads, HEAD_DIM).transpose(1, 0, 2)
+
+    position = jnp.arange(length)
+    doc_ends = jnp.cumsum(doc_lengths[0])
+    doc_ids = jnp.sum((position[:, None] >= doc_ends[None, :]).astype(jnp.int32), axis=1)
+    allowed = (position[None, :] <= position[:, None]) & (doc_ids[None, :] == doc_ids[:, None])
+    scores = jnp.einsum("htd,hkd->htk", queries, keys, preferred_element_type=F32) * score_scale
+    scores = jnp.where(allowed[None], scores, MASK_FILL)
+    row_max = jnp.max(scores, axis=-1, keepdims=True)
+    totals = row_max + jnp.log(jnp.sum(jnp.exp(scores - row_max), axis=-1, keepdims=True))
+    prob_full = jnp.exp(scores - totals)
+    probs = prob_full.astype(BF16)
+    mixed = jnp.einsum("htk,hkd->htd", probs, values, preferred_element_type=F32)
+    attended = from_heads(mixed).astype(BF16)
+
+    att_tok = exchange(attended.reshape(n_seq, tok_count, own_width), SEQ)
+    att_tok = att_tok.transpose(1, 0, 2).reshape(tok_count, model_width)
+    branch = matmul(att_tok, full_o)
+    branch_norm, branch_factor = norm_apply(branch, gain_a)
+    hidden = tokens.astype(F32) + branch_norm
+    hidden_low = hidden.astype(BF16)
+
+    def ring_gather(own):
+        held = [own]
+        for _ in range(n_z - 1):
+            held.append(lax.ppermute(held[-1], "z", ring))
+        return [jnp.concatenate([part, core_swap(part)], axis=0) for part in held]
+
+    def ring_sum(parts):
+        total = None
+        for step in list(range(1, n_z)) + [0]:
+            part = parts[step]
+            mine = part[:tok_count] + core_swap(part[tok_count:].astype(BF16)).astype(F32)
+            if total is not None:
+                mine = mine + lax.ppermute(total.astype(BF16), "z", ring).astype(F32)
+            total = mine
+        return total
+
+    hid = ring_gather(hidden_low)
+    gate = [matmul(part, w_g) for part in hid]
+    upward = [matmul(part, w_u) for part in hid]
+    sig = [jax.nn.sigmoid(part) for part in gate]
+    active = [(g * s * u).astype(BF16) for g, s, u in zip(gate, sig, upward)]
+    result = ring_sum([dot_right_t(part, w_d) for part in active])
+    result_norm, result_factor = norm_apply(result, gain_f)
+    output = (hidden + result_norm).astype(BF16)
+
+    grad_top = cotangent[0].astype(F32)
+    grad_result, ffn_gain_term = norm_back(result, result_factor, gain_f, grad_top)
+    g_res = ring_gather(grad_result.astype(BF16))
+    g_act = [matmul(part, w_d) for part in g_res]
+    g_gate = [
+        (a * u * s * (1.0 + g * (1.0 - s))).astype(BF16)
+        for a, u, s, g in zip(g_act, upward, sig, gate)
+    ]
+    g_up = [(a * g * s).astype(BF16) for a, g, s in zip(g_act, gate, sig)]
+    grad_hidden = grad_top + ring_sum(
+        [dot_right_t(a, w_g) + dot_right_t(b, w_u) for a, b in zip(g_gate, g_up)]
+    )
+
+    def feed_grad(left, right):
+        term = dot_left_t(jnp.concatenate(left, axis=0), jnp.concatenate(right, axis=0))
+        term = term.astype(BF16).reshape(n_x, n_core, n_z, n_y, own_rows, own_feed)
+        term = term.transpose(0, 3, 1, 2, 4, 5).reshape(n_x * n_y, n_feed, own_rows, own_feed)
+        term = jnp.sum(exchange(term, REST).astype(F32), axis=0)
+        term = exchange(term.astype(BF16), FEED)
+        return term.transpose(1, 0, 2).reshape(own_rows, feed_width).astype(F32)
+
+    grad_w_down = feed_grad(g_res, active).T
+    grad_w_gate = feed_grad(hid, g_gate)
+    grad_w_up = feed_grad(hid, g_up)
+
+    grad_branch, attn_gain_term = norm_back(branch, branch_factor, gain_a, grad_hidden)
+    grad_branch = grad_branch.astype(BF16)
+    grad_attended = dot_right_t(grad_branch, full_o).astype(BF16)
+    g_att = grad_attended.reshape(tok_count, n_seq, own_width).transpose(1, 0, 2)
+    g_att = exchange(g_att, SEQ).reshape(length, own_heads, HEAD_DIM).transpose(1, 0, 2)
+
+    branch_row = lax.all_gather(grad_branch, SEQ, axis=0, tiled=True)
+    grad_w_out = dot_left_t(attended, branch_row).astype(BF16)
+    grad_w_out = grad_w_out.reshape(n_dp, own_rows, model_width)
+    grad_w_out = jnp.sum(exchange(grad_w_out, DP).astype(F32), axis=0)
+    home = [(d * n_seq + s, s * n_dp + d) for d in range(n_dp) for s in range(n_seq)]
+    grad_w_out = lax.ppermute(grad_w_out.astype(BF16), ALL, home).astype(F32)
+
+    grad_probs = jnp.einsum("htd,hkd->htk", g_att, values, preferred_element_type=F32)
+    offsets = jnp.sum(prob_full * grad_probs, axis=-1, keepdims=True)
+    grad_scores = (prob_full * (grad_probs - offsets)).astype(BF16)
+    grad_q = (
+        jnp.einsum("htk,hkd->htd", grad_scores, keys, preferred_element_type=F32) * score_scale
+    )
+    grad_k = (
+        jnp.einsum("htk,htd->hkd", grad_scores, queries, preferred_element_type=F32) * score_scale
+    )
+    grad_v = jnp.einsum("htk,htd->hkd", probs, g_att, preferred_element_type=F32)
+
+    def turn_back(array_in):
+        heads = rotate(array_in.transpose(1, 0, 2), cosine, sine_t, -1.0)
+        return heads.reshape(length, own_width)
+
+    grad_q, grad_k = turn_back(grad_q), turn_back(grad_k)
+    dots = jnp.stack(
+        [jnp.sum(grad_q * my_gq * q_lin, axis=1), jnp.sum(grad_k * my_gk * k_lin, axis=1)]
+    )
+    dots = jnp.sum(spread(dots, SEQ), axis=0) / model_width
+
+    def lin_back(grad_in, lin, factor, gain_vec, mean_dot):
+        gain_term = jnp.sum(grad_in * lin * factor, axis=0)
+        grad_out = factor * (grad_in * gain_vec) - lin * (factor * factor * factor) * mean_dot
+        return grad_out.astype(BF16), gain_term
+
+    grad_q_lin, query_gain_term = lin_back(grad_q, q_lin, q_factor, my_gq, dots[0][:, None])
+    grad_k_lin, key_gain_term = lin_back(grad_k, k_lin, k_factor, my_gk, dots[1][:, None])
+    grad_lin = jnp.concatenate([grad_q_lin, grad_k_lin, from_heads(grad_v).astype(BF16)], axis=1)
+
+    grad_row = dot_right_t(grad_lin, w_heads).astype(BF16)
+    grad_input = grad_hidden + lax.psum_scatter(
+        grad_row, SEQ, scatter_dimension=0, tiled=True
+    ).astype(F32)
+
+    grad_heads = dot_left_t(x_row, grad_lin).astype(BF16)
+    grad_heads = grad_heads.reshape(n_dp, n_seq * own_rows, 3 * own_width)
+    grad_heads = jnp.sum(exchange(grad_heads, DP).astype(F32), axis=0).astype(BF16)
+    grad_heads = exchange(grad_heads.reshape(n_seq, own_rows, 3 * own_width), SEQ)
+    grad_heads = grad_heads.reshape(n_seq, own_rows, 3, own_width).transpose(2, 1, 0, 3)
+    grad_heads = grad_heads.reshape(3, own_rows, model_width).astype(F32)
+
+    def place(term):
+        return lax.dynamic_update_slice(
+            jnp.zeros((model_width,), F32), term, (seq_at * own_width,)
+        )
+
+    gain_terms = jnp.stack(
+        [place(query_gain_term), place(key_gain_term), attn_gain_term, ffn_gain_term]
+    )
+    gain_terms = gain_terms.reshape(4, n_all, own_rows).transpose(1, 0, 2)
+    gain_grads = jnp.sum(exchange(gain_terms, ALL), axis=0)
+
+    return (
+        output[None],
+        grad_input[None],
+        grad_heads[0],
+        grad_heads[1],
+        grad_heads[2],
+        grad_w_out,
+        gain_grads[0],
+        gain_grads[1],
+        gain_grads[2],
+        grad_w_gate,
+        grad_w_up,
+        grad_w_down,
+        gain_grads[3],
+    )
+
+
+def plain_rotation(first_pos, tok_count):
+    half_dim = HEAD_DIM // 2
+    position = (first_pos + jnp.arange(tok_count)).astype(jnp.float32)
+    inverse = jnp.exp(-(jnp.arange(half_dim).astype(jnp.float32) / half_dim) * math.log(ROPE_BASE))
+    angles = position[:, None] * inverse[None, :]
+    return (jnp.cos(angles)[None, :, None, :], jnp.sin(angles)[None, :, None, :])
+
+
+def plain_body(
     inputs,
     doc_lengths,
     w_query,
@@ -102,7 +366,7 @@
         lax.all_gather(gain_key, ("dp", "seq"), axis=0, tiled=True),
         lax.all_gather(gain_attn, ("dp", "seq"), axis=0, tiled=True),
     )
-    cosine, sine_t = rotation(first_pos, tok_count)
+    cosine, sine_t = plain_rotation(first_pos, tok_count)
     q_lin = matmul(tokens, full_q)
     k_lin = matmul(tokens, full_k)
     v_lin = matmul(tokens, full_v)
@@ -299,39 +563,23 @@
 
 
 def solution(mesh):
+    n_dp, n_seq = mesh.shape["dp"], mesh.shape["seq"]
+    if HEADS % n_seq == 0 and n_dp % 2 == 0 and n_seq % 2 == 0:
+        grid = Mesh(mesh.devices.reshape(n_dp // 2, 2, n_seq // 2, 2), ALL)
+        layer, dp, seq = body, DP, SEQ
+    else:
+        grid, layer, dp, seq = mesh, plain_body, ("dp",), ("seq",)
+    rows = P(dp, seq, None)
+    split = P(dp + seq, None)
+    vector = P(dp + seq)
+    down = P(None, dp + seq)
     return jax.shard_map(
-        body,
-        mesh=mesh,
-        in_specs=(
-            P("dp", "seq", None),
-            P("dp", None),
-            P(("dp", "seq"), None),
-            P(("dp", "seq"), None),
-            P(("dp", "seq"), None),
-            P(("dp", "seq"), None),
-            P(("dp", "seq")),
-            P(("dp", "seq")),
-            P(("dp", "seq")),
-            P(("dp", "seq"), None),
-            P(("dp", "seq"), None),
-            P(None, ("dp", "seq")),
-            P(("dp", "seq")),
-            P("dp", "seq", None),
-        ),
-        out_specs=(
-            P("dp", "seq", None),
-            P("dp", "seq", None),
-            P(("dp", "seq"), None),
-            P(("dp", "seq"), None),
-            P(("dp", "seq"), None),
-            P(("dp", "seq"), None),
-            P(("dp", "seq")),
-            P(("dp", "seq")),
-            P(("dp", "seq")),
-            P(("dp", "seq"), None),
-            P(("dp", "seq"), None),
-            P(None, ("dp", "seq")),
-            P(("dp", "seq")),
-        ),
+        layer,
+        mesh=grid,
+        in_specs=(rows, P(dp, None))
+        + (split,) * 4
+        + (vector,) * 3
+        + (split, split, down, vector, rows),
+        out_specs=(rows, rows) + (split,) * 4 + (vector,) * 3 + (split, split, down, vector),
         check_vma=False,
     )

time: 4530 us -> 1050 us (0.23)
  waiting for transfers between devices: 3750 us -> 478 us
  matrix products: 419 us -> 120 us
  starting transfers between devices: 1.27 us -> 137 us
  other arithmetic: 156 us -> 62.1 us
  blocking collectives: 77.2 us -> 131 us
    reduce_scatter x3 -> x1, waiting for transfers between devices: 1770 us -> 0.01 us  [body(): lax.psum_scatter(grad_row, SEQ, scatter_dimension=0, tiled=True).astype(F32)]
    unnamed x20 -> x6, waiting for transfers between devices: 1090 us -> 1.56 us
    all_gather x9 -> x5, waiting for transfers between devices: 898 us -> 86.9 us  [the longest x1 71.9 us: body(): w_feed = lax.all_gather(w_feed, REST, axis=0, tiled=False)]
    all_to_all x0 -> x15, waiting for transfers between devices: none -> 261 us  [exchange(): lax.all_to_all(array_in, axes, split_axis=0, concat_axis=0, tiled=True)]
    dot_general x119 -> x20, matrix products: 217 us -> 59.5 us  [the longest x14 39.2 us: matmul(): return jnp.dot(left_mat, right_mat, preferred_element_type=F32)]
    concatenate x1 -> x0, other arithmetic: 133 us -> none  [body(): jnp.concatenate([dot_left_t(hidden_low, grad_gate), dot_left_t(hidden_low...]
    all_to_all x0 -> x2, blocking collectives: none -> 131 us  [exchange(): lax.all_to_all(array_in, axes, split_axis=0, concat_axis=0, tiled=True)]
    ppermute x0 -> x29, waiting for transfers between devices: none -> 129 us  [the longest x6 63.1 us: ring_gather(): held.append(lax.ppermute(held[-1], 'z', ring))]
  transfers between devices with their start and end apart: 16 -> 50, of which waited for: 14 -> 30; matrix products, arithmetic and copies ran while one was open for 10% -> 19% of each run, Pallas kernels for 0% -> 0%
where the time goes in v1:
time: 1050 us; the launch traced here: 1040 us
  waiting for transfers between devices  478 us (46%)
  starting transfers between devices  137 us (13%)
  blocking collectives  131 us (12%)
  matrix products  120 us (11%)
  local copies, waits for them, and re-layouts  91.3 us (9%)
  other arithmetic  62.1 us (6%)
  between operations  16.1 us (2%)
    all_to_all x15, waiting for transfers between devices, exchange(): lax.all_to_all(array_in, axes, split_axis=0, concat_axis=0, tiled=True)  261 us
    all_to_all x2, blocking collectives, exchange(): lax.all_to_all(array_in, axes, split_axis=0, concat_axis=0, tiled=True)  131 us
    all_to_all x15, starting transfers between devices, exchange(): lax.all_to_all(array_in, axes, split_axis=0, concat_axis=0, tiled=True)  110 us
    all_gather x1, waiting for transfers between devices, body(): w_feed = lax.all_gather(w_feed, REST, axis=0, tiled=False)  71.9 us
    ppermute x6, waiting for transfers between devices, ring_gather(): held.append(lax.ppermute(held[-1], 'z', ring))  63.1 us
    ppermute x6, waiting for transfers between devices, ring_sum(): mine = mine + lax.ppermute(total.astype(BF16), 'z', ring).astype(F32)  57.6 us
    unnamed x172, local copies, waits for them, and re-layouts  40.3 us
    dot_general x14, matrix products, matmul(): return jnp.dot(left_mat, right_mat, preferred_element_type=F32)  39.2 us
  transfers between devices with their start and end apart: 50, of which 30 were waited for; matrix products, arithmetic and copies ran while one was open for 19% of the time, Pallas kernels for 0%

profile of v1, /device:TPU:25, one launch (start us, length us, event | category | flops | bytes accessed | tf_op | source)
XLA Modules:
  0.0 1036.3 jit_solution(5283686863519687810)
XLA Ops:
  14.3 22.9 %all_to_all.85 = bf16[8,64,768]{2,1,0:T(8,128)(2,1)} all-to-all(bf16[8,64,768]{2,1,0:T(8,128)(2,1)S(1)} %reshape.365), channel_id=1, replica_groups=mesh['x'=2,'core'=2,'z'=4,'y'=2] {'z','y'}, dimensions={0} | all-to-all | bytes 1572864 | tf_op jit(solution)/shard_map/all_to_all | solution.py:79
  44.0 107.9 %all_to_all.86 = bf16[8,3,64,1024]{3,2,1,0:T(8,128)(2,1)} all-to-all(bf16[8,3,64,1024]{3,2,1,0:T(8,128)(2,1)S(1)} %copy.294), channel_id=1, replica_groups=mesh['x'=2,'core'=2,'z'=4,'y'=2] {'core','z'}, dimensions={0} | all-to-all | bytes 6291456 | tf_op jit(solution)/shard_map/all_to_all | solution.py:79
  152.6 10.5 %all-to-all-start.2 = ((bf16[32,2,128]{2,1,0:T(2,128)(2,1)}), bf16[32,2,128]{2,1,0:T(2,128)(2,1)S(1)}, u32[]{:S(2)}, u32[]{:S(2)}) async-start(bf16[32,2,128]{2,1,0:T(2,128)(2,1)} %reshape.430), calls=%async_computation.2 | async-start | bytes 32768 | tf_op jit(solution)/shard_map/all_to_all | solution.py:79
  171.4 6.2 fusion.31
  180.2 5.3 all-to-all-start.1
  215.8 6.4 all-to-all-start.3
  222.3 26.8 %all-to-all-done.3 = bf16[8,128,256]{1,2,0:T(8,128)(2,1)S(1)} async-done(((bf16[8,128,256]{1,2,0:T(8,128)(2,1)}), bf16[8,128,256]{1,2,0:T(8,128)(2,1)S(1)}, u32[]{:S(2)}, u32[]{:S(2)}) %all-to-all-start.3) | async-done | bytes 524320 | tf_op jit(solution)/shard_map/all_to_all | solution.py:79
  249.1 10.8 %all-gather.10.cloned.1.call-done = bf16[2048,2048]{1,0:T(8,128)(2,1)} async-done(((bf16[64,2048]{1,0:T(8,128)(2,1)}), bf16[2048,2048]{1,0:T(8,128)(2,1)}) %all-gather.10.cloned.1.call-update) | async-done | bytes 8388624 | tf_op jit(solution)/shard_map/all_gather | solution.py:138
  265.7 14.2 %collective-permute-done.2 = bf16[128,2048]{1,0:T(8,128)(2,1)S(1)} collective-permute-done((bf16[128,2048]{1,0:T(8,128)(2,1)S(1)}, bf16[128,2048]{1,0:T(8,128)(2,1)S(1)}, u32[]{:S(2)}, u32[]{:S(2)}) %collective-permute-start.2) | collective-permute-done | bytes 524320 | tf_op jit(solution)/shard_map/ppermute | solution.py:194
  280.9 12.2 %collective-permute-done.3 = bf16[128,2048]{1,0:T(8,128)(2,1)S(1)} collective-permute-done((bf16[128,2048]{1,0:T(8,128)(2,1)S(1)}, bf16[128,2048]{1,0:T(8,128)(2,1)S(1)}, u32[]{:S(2)}, u32[]{:S(2)}) %collective-permute-start.3) | collective-permute-done | bytes 524320 | tf_op jit(solution)/shard_map/ppermute | solution.py:194
  298.2 7.6 collective-permute-done.4
  313.0 71.9 %all-gather.16.cloned.1.call-done = bf16[32,3,64,1024]{3,2,1,0:T(8,128)(2,1)} async-done(((bf16[8,3,64,1024]{3,2,1,0:T(8,128)(2,1)}), bf16[32,3,64,1024]{3,2,1,0:T(8,128)(2,1)}) %all-gather.16.cloned.1.call-update) | async-done | bytes 12582928 | tf_op jit(solution)/shard_map/all_gather | solution.py:143
  384.9 5.9 fusion.102
  416.0 10.2 collective-permute-done.11
  431.6 7.8 collective-permute-done.12
  439.8 12.1 %collective-permute-done.13 = bf16[128,2048]{1,0:T(8,128)(2,1)} collective-permute-done((bf16[128,2048]{1,0:T(8,128)(2,1)S(1)}, bf16[128,2048]{1,0:T(8,128)(2,1)}, u32[]{:S(2)}, u32[]{:S(2)}) %collective-permute-start.13) | collective-permute-done | bytes 524320 | tf_op jit(solution)/shard_map/ppermute | solution.py:203
  460.8 8.2 collective-permute-done.16
  477.8 9.9 collective-permute-done.17
  498.7 11.0 %collective-permute-done.18 = bf16[128,2048]{1,0:T(8,128)(2,1)S(1)} collective-permute-done((bf16[128,2048]{1,0:T(8,128)(2,1)S(1)}, bf16[128,2048]{1,0:T(8,128)(2,1)S(1)}, u32[]{:S(2)}, u32[]{:S(2)}) %collective-permute-start.18) | collective-permute-done | bytes 524320 | tf_op jit(solution)/shard_map/ppermute | solution.py:194
  517.4 9.5 collective-permute-done.25
  530.8 10.0 collective-permute-done.26
  545.8 8.0 collective-permute-done.27
  556.0 6.5 convolution_convert_fusion.5
  563.5 5.6 all-to-all-start.5
  574.6 5.3 all-to-all-done.5
  580.8 5.3 multiply_reduce_fusion
  608.1 7.1 all-to-all-start.10
  620.0 6.5 all-to-all-start.6
  626.5 7.3 convolution_convert_fusion.1
  641.2 7.3 convolution_convert_fusion.2
  651.0 37.1 %all-to-all-done.15 = bf16[4,8,64,1024]{3,2,1,0:T(8,128)(2,1)} async-done(((bf16[4,8,64,1024]{3,2,1,0:T(8,128)(2,1)}), bf16[4,8,64,1024]{3,2,1,0:T(8,128)(2,1)}, u32[]{:S(2)}, u32[]{:S(2)}) %all-to-all-start.15) | async-done | bytes 4194336 | tf_op jit(solution)/shard_map/all_to_all | solution.py:79
  693.5 7.3 convolution_convert_fusion.3
  703.3 42.1 %all-to-all-done.13 = bf16[4,8,64,1024]{3,2,1,0:T(8,128)(2,1)} async-done(((bf16[4,8,64,1024]{3,2,1,0:T(8,128)(2,1)}), bf16[4,8,64,1024]{3,2,1,0:T(8,128)(2,1)}, u32[]{:S(2)}, u32[]{:S(2)}) %all-to-all-start.13) | async-done | bytes 4194336 | tf_op jit(solution)/shard_map/all_to_all | solution.py:79
  750.2 6.8 convolution_convert_fusion.7
  766.9 47.3 %all-to-all-done.11 = bf16[4,8,64,1024]{3,2,1,0:T(8,128)(2,1)} async-done(((bf16[4,8,64,1024]{3,2,1,0:T(8,128)(2,1)}), bf16[4,8,64,1024]{3,2,1,0:T(8,128)(2,1)}, u32[]{:S(2)}, u32[]{:S(2)}) %all-to-all-start.11) | async-done | bytes 4194336 | tf_op jit(solution)/shard_map/all_to_all | solution.py:79
  814.2 5.3 all-to-all-start.7
  819.7 7.1 convolution_convert_fusion
  831.2 24.5 %all-to-all-done.7 = bf16[4,512,768]{1,2,0:T(8,128)(2,1)} async-done(((bf16[4,512,768]{1,2,0:T(8,128)(2,1)}), bf16[4,512,768]{1,2,0:T(8,128)(2,1)}, u32[]{:S(2)}, u32[]{:S(2)}) %all-to-all-start.7) | async-done | bytes 3145760 | tf_op jit(solution)/shard_map/all_to_all | solution.py:79
  855.7 5.6 all-to-all-start.16
  865.7 20.1 %all-to-all-done.16 = bf16[8,64,1024]{2,1,0:T(8,128)(2,1)S(1)} async-done(((bf16[8,64,1024]{2,1,0:T(8,128)(2,1)}), bf16[8,64,1024]{2,1,0:T(8,128)(2,1)S(1)}, u32[]{:S(2)}, u32[]{:S(2)}) %all-to-all-start.16) | async-done | bytes 1048608 | tf_op jit(solution)/shard_map/all_to_all | solution.py:79
  885.9 11.5 %all-to-all-start.14 = ((bf16[8,64,1024]{2,1,0:T(8,128)(2,1)}), bf16[8,64,1024]{2,1,0:T(8,128)(2,1)S(1)}, u32[]{:S(2)}, u32[]{:S(2)}) async-start(bf16[8,64,1024]{2,1,0:T(8,128)(2,1)} %reduce_sum.243), calls=%async_computation.15 | async-start | bytes 2097152 | tf_op jit(solution)/shard_map/all_to_all | solution.py:79
  901.9 21.9 %all-to-all-done.14 = bf16[8,64,1024]{2,1,0:T(8,128)(2,1)S(1)} async-done(((bf16[8,64,1024]{2,1,0:T(8,128)(2,1)}), bf16[8,64,1024]{2,1,0:T(8,128)(2,1)S(1)}, u32[]{:S(2)}, u32[]{:S(2)}) %all-to-all-start.14) | async-done | bytes 1048608 | tf_op jit(solution)/shard_map/all_to_all | solution.py:79
  923.8 15.7 %all-to-all-start.12 = ((bf16[8,64,1024]{2,1,0:T(8,128)(2,1)}), bf16[8,64,1024]{2,1,0:T(8,128)(2,1)S(1)}, u32[]{:S(2)}, u32[]{:S(2)}) async-start(bf16[8,64,1024]{2,1,0:T(8,128)(2,1)} %reduce_sum.242), calls=%async_computation.13 | async-start | bytes 2097152 | tf_op jit(solution)/shard_map/all_to_all | solution.py:79
  945.2 12.6 %all-to-all-done.12 = bf16[8,64,1024]{2,1,0:T(8,128)(2,1)S(1)} async-done(((bf16[8,64,1024]{2,1,0:T(8,128)(2,1)}), bf16[8,64,1024]{2,1,0:T(8,128)(2,1)S(1)}, u32[]{:S(2)}, u32[]{:S(2)}) %all-to-all-start.12) | async-done | bytes 1048608 | tf_op jit(solution)/shard_map/all_to_all | solution.py:79
  957.9 11.7 %all-to-all-start.8 = ((bf16[8,64,768]{2,1,0:T(8,128)(2,1)}), bf16[8,64,768]{2,1,0:T(8,128)(2,1)}, u32[]{:S(2)}, u32[]{:S(2)}) async-start(bf16[8,64,768]{2,1,0:T(8,128)(2,1)} %bitcast.298), calls=%async_computation.9 | async-start | bytes 1572864 | tf_op jit(solution)/shard_map/all_to_all | solution.py:79
  976.0 12.5 %all-to-all-done.8 = bf16[8,64,768]{2,1,0:T(8,128)(2,1)} async-done(((bf16[8,64,768]{2,1,0:T(8,128)(2,1)}), bf16[8,64,768]{2,1,0:T(8,128)(2,1)}, u32[]{:S(2)}, u32[]{:S(2)}) %all-to-all-start.8) | async-done | bytes 786464 | tf_op jit(solution)/shard_map/all_to_all | solution.py:79
  1000.9 6.0 all-to-all-done.9
  1018.4 7.9 collective-permute-done.28
  (394 shorter events, 270.9 us)
Async XLA Ops:
  7.2 160.1 %all-gather.8.cloned.1.call-start = ((), (), s32[]{:S(2)}) async-start(), calls=%async_computation.18 | async-start | bytes 3932160 | tf_op jit(solution)/shard_map/all_gather | solution.py:136
  37.2 134.2 %all-gather.14.cloned.1.call-start = ((), (), s32[]{:S(2)}) async-start(), calls=%async_computation.22 | async-start | bytes 4718592 | tf_op jit(solution)/shard_map/all_gather | solution.py:137
  38.0 221.9 %all-gather.10.cloned.1.call-start = ((), (), s32[]{:S(2)}) async-start(), calls=%async_computation.19 | async-start | bytes 8650752 | tf_op jit(solution)/shard_map/all_gather | solution.py:138
  38.7 346.2 %all-gather.16.cloned.1.call-start = ((), (), s32[]{:S(2)}) async-start(), calls=%async_computation.23 | async-start | bytes 15728640 | tf_op jit(solution)/shard_map/all_gather | solution.py:143
  152.6 14.5 %all-to-all-start.2 = ((bf16[32,2,128]{2,1,0:T(2,128)(2,1)}), bf16[32,2,128]{2,1,0:T(2,128)(2,1)S(1)}, u32[]{:S(2)}, u32[]{:S(2)}) async-start(bf16[32,2,128]{2,1,0:T(2,128)(2,1)} %reshape.430), calls=%async_computation.2 | async-start | bytes 32768 | tf_op jit(solution)/shard_map/all_to_all | solution.py:79
  180.2 8.5 all-to-all-start.1
  215.8 33.3 %all-to-all-start.3 = ((bf16[8,128,256]{1,2,0:T(8,128)(2,1)}), bf16[8,128,256]{1,2,0:T(8,128)(2,1)S(1)}, u32[]{:S(2)}, u32[]{:S(2)}) async-start(bf16[8,128,256]{1,2,0:T(8,128)(2,1)} %copy.293), calls=%async_computation.3 | async-start | bytes 1048576 | tf_op jit(solution)/shard_map/all_to_all | solution.py:79
  265.7 14.2 %collective-permute-start.2 = (bf16[128,2048]{1,0:T(8,128)(2,1)S(1)}, bf16[128,2048]{1,0:T(8,128)(2,1)S(1)}, u32[]{:S(2)}, u32[]{:S(2)}) collective-permute-start(bf16[128,2048]{1,0:T(8,128)(2,1)S(1)} %get-tuple-element.32), channel_id=1, source_target_pairs={{0,2},{2,6},{6,4},{4,0},{1,3},{3,7},{7,5},{5,1},{8,10},{10,14},{14... | collective-permute-start | bytes 1572872 | tf_op jit(solution)/shard_map/ppermute | solution.py:194
  279.9 13.3 %collective-permute-start.3 = (bf16[128,2048]{1,0:T(8,128)(2,1)S(1)}, bf16[128,2048]{1,0:T(8,128)(2,1)S(1)}, u32[]{:S(2)}, u32[]{:S(2)}) collective-permute-start(bf16[128,2048]{1,0:T(8,128)(2,1)S(1)} %collective-permute-done.2), channel_id=1, source_target_pairs={{0,2},{2,6},{6,4},{4,0},{1,3},{3,7},{7,5},{5,1},{8,10},{10,14},{14... | collective-permute-start | bytes 1572872 | tf_op jit(solution)/shard_map/ppermute | solution.py:194
  279.9 13.6 %collective-permute-start = (bf16[128,2048]{1,0:T(8,128)(2,1)S(1)}, bf16[128,2048]{1,0:T(8,128)(2,1)S(1)}, u32[]{:S(2)}, u32[]{:S(2)}) collective-permute-start(bf16[128,2048]{1,0:T(8,128)(2,1)S(1)} %get-tuple-element.32), channel_id=1, source_target_pairs={{0,8},{8,0},{1,9},{9,1},{2,10},{10,2},{3,11},{11,3},{4,12},{12,4},... | collective-permute-start | bytes 1572872 | tf_op jit(solution)/shard_map/ppermute | solution.py:93
  280.9 16.4 %collective-permute-start.9 = (bf16[128,2048]{1,0:T(8,128)(2,1)S(1)}, bf16[128,2048]{1,0:T(8,128)(2,1)S(1)}, u32[]{:S(2)}, u32[]{:S(2)}) collective-permute-start(bf16[128,2048]{1,0:T(8,128)(2,1)S(1)} %collective-permute-done.2), channel_id=1, source_target_pairs={{0,8},{8,0},{1,9},{9,1},{2,10},{10,2},{3,11},{11,3},{4,12},{12,4},... | collective-permute-start | bytes 1572872 | tf_op jit(solution)/shard_map/ppermute | solution.py:93
  293.1 12.7 %collective-permute-start.4 = (bf16[128,2048]{1,0:T(8,128)(2,1)S(1)}, bf16[128,2048]{1,0:T(8,128)(2,1)S(1)}, u32[]{:S(2)}, u32[]{:S(2)}) collective-permute-start(bf16[128,2048]{1,0:T(8,128)(2,1)S(1)} %collective-permute-done.3), channel_id=1, source_target_pairs={{0,2},{2,6},{6,4},{4,0},{1,3},{3,7},{7,5},{5,1},{8,10},{10,14},{14... | collective-permute-start | bytes 1572872 | tf_op jit(solution)/shard_map/ppermute | solution.py:194
  294.4 15.3 %collective-permute-start.7 = (bf16[128,2048]{1,0:T(8,128)(2,1)S(1)}, bf16[128,2048]{1,0:T(8,128)(2,1)S(1)}, u32[]{:S(2)}, u32[]{:S(2)}) collective-permute-start(bf16[128,2048]{1,0:T(8,128)(2,1)S(1)} %collective-permute-done.3), channel_id=1, source_target_pairs={{0,8},{8,0},{1,9},{9,1},{2,10},{10,2},{3,11},{11,3},{4,12},{12,4},... | collective-permute-start | bytes 1572872 | tf_op jit(solution)/shard_map/ppermute | solution.py:93
  305.8 6.0 collective-permute-start.5
  408.2 7.8 collective-permute-start.8
  412.0 14.1 %collective-permute-start.11 = (bf16[128,2048]{1,0:T(8,128)(2,1)S(1)}, bf16[128,2048]{1,0:T(8,128)(2,1)S(1)}, u32[]{:S(2)}, u32[]{:S(2)}) collective-permute-start(bf16[128,2048]{1,0:T(8,128)(2,1)S(1)} %fusion.49), channel_id=1, source_target_pairs={{0,2},{2,6},{6,4},{4,0},{1,3},{3,7},{7,5},{5,1},{8,10},{10,14},{14... | collective-permute-start | bytes 1572872 | tf_op jit(solution)/shard_map/ppermute | solution.py:203
  414.1 17.5 %collective-permute-start.6 = (bf16[128,2048]{1,0:T(8,128)(2,1)S(1)}, bf16[128,2048]{1,0:T(8,128)(2,1)S(1)}, u32[]{:S(2)}, u32[]{:S(2)}) collective-permute-start(bf16[128,2048]{1,0:T(8,128)(2,1)S(1)} %slice.321), channel_id=1, source_target_pairs={{0,8},{8,0},{1,9},{9,1},{2,10},{10,2},{3,11},{11,3},{4,12},{12,4},... | collective-permute-start | bytes 1572872 | tf_op jit(solution)/shard_map/ppermute | solution.py:93
  426.4 13.0 %collective-permute-start.12 = (bf16[128,2048]{1,0:T(8,128)(2,1)S(1)}, bf16[128,2048]{1,0:T(8,128)(2,1)S(1)}, u32[]{:S(2)}, u32[]{:S(2)}) collective-permute-start(bf16[128,2048]{1,0:T(8,128)(2,1)S(1)} %fusion.51), channel_id=1, source_target_pairs={{0,2},{2,6},{6,4},{4,0},{1,3},{3,7},{7,5},{5,1},{8,10},{10,14},{14... | collective-permute-start | bytes 1572872 | tf_op jit(solution)/shard_map/ppermute | solution.py:203
  430.2 9.6 collective-permute-start.1
  439.7 12.2 %collective-permute-start.13 = (bf16[128,2048]{1,0:T(8,128)(2,1)S(1)}, bf16[128,2048]{1,0:T(8,128)(2,1)}, u32[]{:S(2)}, u32[]{:S(2)}) collective-permute-start(bf16[128,2048]{1,0:T(8,128)(2,1)S(1)} %fusion.53), channel_id=1, source_target_pairs={{0,2},{2,6},{6,4},{4,0},{1,3},{3,7},{7,5},{5,1},{8,10},{10,14},{14... | collective-permute-start | bytes 1572872 | tf_op jit(solution)/shard_map/ppermute | solution.py:203
  457.5 11.5 %collective-permute-start.16 = (bf16[128,2048]{1,0:T(8,128)(2,1)}, bf16[128,2048]{1,0:T(8,128)(2,1)}, u32[]{:S(2)}, u32[]{:S(2)}) collective-permute-start(bf16[128,2048]{1,0:T(8,128)(2,1)} %get-tuple-element.30), channel_id=1, source_target_pairs={{0,2},{2,6},{6,4},{4,0},{1,3},{3,7},{7,5},{5,1},{8,10},{10,14},{14... | collective-permute-start | bytes 1572872 | tf_op jit(solution)/shard_map/ppermute | solution.py:194
  457.5 15.6 %collective-permute-start.14 = (bf16[128,2048]{1,0:T(8,128)(2,1)}, bf16[128,2048]{1,0:T(8,128)(2,1)}, u32[]{:S(2)}, u32[]{:S(2)}) collective-permute-start(bf16[128,2048]{1,0:T(8,128)(2,1)} %get-tuple-element.30), channel_id=1, source_target_pairs={{0,8},{8,0},{1,9},{9,1},{2,10},{10,2},{3,11},{11,3},{4,12},{12,4},... | collective-permute-start | bytes 1572872 | tf_op jit(solution)/shard_map/ppermute | solution.py:93
  469.0 19.5 %collective-permute-start.23 = (bf16[128,2048]{1,0:T(8,128)(2,1)}, bf16[128,2048]{1,0:T(8,128)(2,1)S(1)}, u32[]{:S(2)}, u32[]{:S(2)}) collective-permute-start(bf16[128,2048]{1,0:T(8,128)(2,1)} %collective-permute-done.16), channel_id=1, source_target_pairs={{0,8},{8,0},{1,9},{9,1},{2,10},{10,2},{3,11},{11,3},{4,12},{12,4},... | collective-permute-start | bytes 1572872 | tf_op jit(solution)/shard_map/ppermute | solution.py:93
  473.1 14.7 %collective-permute-start.17 = (bf16[128,2048]{1,0:T(8,128)(2,1)}, bf16[128,2048]{1,0:T(8,128)(2,1)S(1)}, u32[]{:S(2)}, u32[]{:S(2)}) collective-permute-start(bf16[128,2048]{1,0:T(8,128)(2,1)} %collective-permute-done.16), channel_id=1, source_target_pairs={{0,2},{2,6},{6,4},{4,0},{1,3},{3,7},{7,5},{5,1},{8,10},{10,14},{14... | collective-permute-start | bytes 1572872 | tf_op jit(solution)/shard_map/ppermute | solution.py:194
  487.7 8.0 collective-permute-start.21
  495.2 17.2 %collective-permute-start.24 = (bf16[128,2048]{1,0:T(8,128)(2,1)S(1)}, bf16[128,2048]{1,0:T(8,128)(2,1)S(1)}, u32[]{:S(2)}, u32[]{:S(2)}) collective-permute-start(bf16[128,2048]{1,0:T(8,128)(2,1)S(1)} %slice.315), channel_id=1, source_target_pairs={{0,8},{8,0},{1,9},{9,1},{2,10},{10,2},{3,11},{11,3},{4,12},{12,4},... | collective-permute-start | bytes 1572872 | tf_op jit(solution)/shard_map/ppermute | solution.py:93
  495.4 14.4 %collective-permute-start.18 = (bf16[128,2048]{1,0:T(8,128)(2,1)S(1)}, bf16[128,2048]{1,0:T(8,128)(2,1)S(1)}, u32[]{:S(2)}, u32[]{:S(2)}) collective-permute-start(bf16[128,2048]{1,0:T(8,128)(2,1)S(1)} %collective-permute-done.17), channel_id=1, source_target_pairs={{0,2},{2,6},{6,4},{4,0},{1,3},{3,7},{7,5},{5,1},{8,10},{10,14},{14... | collective-permute-start | bytes 1572872 | tf_op jit(solution)/shard_map/ppermute | solution.py:194
  512.5 14.5 %collective-permute-start.25 = (bf16[128,2048]{1,0:T(8,128)(2,1)S(1)}, bf16[128,2048]{1,0:T(8,128)(2,1)S(1)}, u32[]{:S(2)}, u32[]{:S(2)}) collective-permute-start(bf16[128,2048]{1,0:T(8,128)(2,1)S(1)} %fusion.43), channel_id=1, source_target_pairs={{0,2},{2,6},{6,4},{4,0},{1,3},{3,7},{7,5},{5,1},{8,10},{10,14},{14... | collective-permute-start | bytes 1572872 | tf_op jit(solution)/shard_map/ppermute | solution.py:203
  512.6 14.4 %collective-permute-start.22 = (bf16[128,2048]{1,0:T(8,128)(2,1)S(1)}, bf16[128,2048]{1,0:T(8,128)(2,1)S(1)}, u32[]{:S(2)}, u32[]{:S(2)}) collective-permute-start(bf16[128,2048]{1,0:T(8,128)(2,1)S(1)} %slice.316), channel_id=1, source_target_pairs={{0,8},{8,0},{1,9},{9,1},{2,10},{10,2},{3,11},{11,3},{4,12},{12,4},... | collective-permute-start | bytes 1572872 | tf_op jit(solution)/shard_map/ppermute | solution.py:93
  516.9 13.9 %collective-permute-start.20 = (bf16[128,2048]{1,0:T(8,128)(2,1)S(1)}, bf16[128,2048]{1,0:T(8,128)(2,1)S(1)}, u32[]{:S(2)}, u32[]{:S(2)}) collective-permute-start(bf16[128,2048]{1,0:T(8,128)(2,1)S(1)} %slice.317), channel_id=1, source_target_pairs={{0,8},{8,0},{1,9},{9,1},{2,10},{10,2},{3,11},{11,3},{4,12},{12,4},... | collective-permute-start | bytes 1572872 | tf_op jit(solution)/shard_map/ppermute | solution.py:93
  527.2 13.6 %collective-permute-start.26 = (bf16[128,2048]{1,0:T(8,128)(2,1)S(1)}, bf16[128,2048]{1,0:T(8,128)(2,1)S(1)}, u32[]{:S(2)}, u32[]{:S(2)}) collective-permute-start(bf16[128,2048]{1,0:T(8,128)(2,1)S(1)} %fusion.45), channel_id=1, source_target_pairs={{0,2},{2,6},{6,4},{4,0},{1,3},{3,7},{7,5},{5,1},{8,10},{10,14},{14... | collective-permute-start | bytes 1572872 | tf_op jit(solution)/shard_map/ppermute | solution.py:203
  529.9 15.9 %collective-permute-start.15 = (bf16[128,2048]{1,0:T(8,128)(2,1)S(1)}, bf16[128,2048]{1,0:T(8,128)(2,1)S(1)}, u32[]{:S(2)}, u32[]{:S(2)}) collective-permute-start(bf16[128,2048]{1,0:T(8,128)(2,1)S(1)} %slice.318), channel_id=1, source_target_pairs={{0,8},{8,0},{1,9},{9,1},{2,10},{10,2},{3,11},{11,3},{4,12},{12,4},... | collective-permute-start | bytes 1572872 | tf_op jit(solution)/shard_map/ppermute | solution.py:93
  541.0 12.8 %collective-permute-start.27 = (bf16[128,2048]{1,0:T(8,128)(2,1)S(1)}, bf16[128,2048]{1,0:T(8,128)(2,1)S(1)}, u32[]{:S(2)}, u32[]{:S(2)}) collective-permute-start(bf16[128,2048]{1,0:T(8,128)(2,1)S(1)} %fusion.47), channel_id=1, source_target_pairs={{0,2},{2,6},{6,4},{4,0},{1,3},{3,7},{7,5},{5,1},{8,10},{10,14},{14... | collective-permute-start | bytes 1572872 | tf_op jit(solution)/shard_map/ppermute | solution.py:203
  563.5 16.4 %all-to-all-start.5 = ((bf16[8,128,256]{1,2,0:T(8,128)(2,1)}), bf16[8,128,256]{1,2,0:T(8,128)(2,1)S(1)}, u32[]{:S(2)}, u32[]{:S(2)}) async-start(bf16[8,128,256]{1,2,0:T(8,128)(2,1)} %bitcast.39), calls=%async_computation.5 | async-start | bytes 1048576 | tf_op jit(solution)/shard_map/all_to_all | solution.py:79
  608.1 11.2 %all-to-all-start.10 = ((f32[32,1,256]{2,1,0:T(1,128)}), f32[32,1,256]{2,1,0:T(1,128)S(1)}, u32[]{:S(2)}, u32[]{:S(2)}) async-start(f32[32,1,256]{2,1,0:T(1,128)} %reshape.432), calls=%async_computation.11 | async-start | bytes 65536 | tf_op jit(solution)/shard_map/all_to_all | solution.py:79
  620.0 16.3 %all-to-all-start.6 = ((f32[8,2,1024]{2,1,0:T(2,128)}), f32[8,2,1024]{2,1,0:T(2,128)S(1)}, u32[]{:S(2)}, u32[]{:S(2)}) async-start(f32[8,2,1024]{2,1,0:T(2,128)} %broadcast_in_dim.23), calls=%async_computation.6 | async-start | bytes 131072 | tf_op jit(solution)/shard_map/all_to_all | solution.py:79
  636.3 51.7 %all-to-all-start.15 = ((bf16[4,8,64,1024]{3,2,1,0:T(8,128)(2,1)}), bf16[4,8,64,1024]{3,2,1,0:T(8,128)(2,1)}, u32[]{:S(2)}, u32[]{:S(2)}) async-start(bf16[4,8,64,1024]{3,2,1,0:T(8,128)(2,1)} %bitcast.268), calls=%async_computation.16 | async-start | bytes 8388608 | tf_op jit(solution)/shard_map/all_to_all | solution.py:79
  688.1 57.3 %all-to-all-start.13 = ((bf16[4,8,64,1024]{3,2,1,0:T(8,128)(2,1)}), bf16[4,8,64,1024]{3,2,1,0:T(8,128)(2,1)}, u32[]{:S(2)}, u32[]{:S(2)}) async-start(bf16[4,8,64,1024]{3,2,1,0:T(8,128)(2,1)} %bitcast.267), calls=%async_computation.14 | async-start | bytes 8388608 | tf_op jit(solution)/shard_map/all_to_all | solution.py:79
  692.9 278.6 %all-gather.12.cloned.1.call-start = ((), (), s32[]{:S(2)}) async-start(), calls=%async_computation.21 | async-start | bytes 4718592 | tf_op jit(solution)/shard_map/all_gather | solution.py:247
  745.4 68.8 %all-to-all-start.11 = ((bf16[4,8,64,1024]{3,2,1,0:T(8,128)(2,1)}), bf16[4,8,64,1024]{3,2,1,0:T(8,128)(2,1)}, u32[]{:S(2)}, u32[]{:S(2)}) async-start(bf16[4,8,64,1024]{3,2,1,0:T(8,128)(2,1)} %bitcast.266), calls=%async_computation.12 | async-start | bytes 8388608 | tf_op jit(solution)/shard_map/all_to_all | solution.py:79
  814.2 41.5 %all-to-all-start.7 = ((bf16[4,512,768]{1,2,0:T(8,128)(2,1)}), bf16[4,512,768]{1,2,0:T(8,128)(2,1)}, u32[]{:S(2)}, u32[]{:S(2)}) async-start(bf16[4,512,768]{1,2,0:T(8,128)(2,1)} %bitcast.270), calls=%async_computation.8 | async-start | bytes 6291456 | tf_op jit(solution)/shard_map/all_to_all | solution.py:79
  819.5 207.6 %reduce-scatter.2.cloned.1.call-start = ((), (), s32[]{:S(2)}) async-start(), calls=%async_computation.20 | async-start | bytes 4718592 | tf_op jit(solution)/shard_map/reduce_scatter | solution.py:285
  855.7 30.2 %all-to-all-start.16 = ((bf16[8,64,1024]{2,1,0:T(8,128)(2,1)}), bf16[8,64,1024]{2,1,0:T(8,128)(2,1)S(1)}, u32[]{:S(2)}, u32[]{:S(2)}) async-start(bf16[8,64,1024]{2,1,0:T(8,128)(2,1)} %reduce_sum.244), calls=%async_computation.17 | async-start | bytes 2097152 | tf_op jit(solution)/shard_map/all_to_all | solution.py:79
  885.9 37.9 %all-to-all-start.14 = ((bf16[8,64,1024]{2,1,0:T(8,128)(2,1)}), bf16[8,64,1024]{2,1,0:T(8,128)(2,1)S(1)}, u32[]{:S(2)}, u32[]{:S(2)}) async-start(bf16[8,64,1024]{2,1,0:T(8,128)(2,1)} %reduce_sum.243), calls=%async_computation.15 | async-start | bytes 2097152 | tf_op jit(solution)/shard_map/all_to_all | solution.py:79
  923.8 34.1 %all-to-all-start.12 = ((bf16[8,64,1024]{2,1,0:T(8,128)(2,1)}), bf16[8,64,1024]{2,1,0:T(8,128)(2,1)S(1)}, u32[]{:S(2)}, u32[]{:S(2)}) async-start(bf16[8,64,1024]{2,1,0:T(8,128)(2,1)} %reduce_sum.242), calls=%async_computation.13 | async-start | bytes 2097152 | tf_op jit(solution)/shard_map/all_to_all | solution.py:79
  957.9 30.7 %all-to-all-start.8 = ((bf16[8,64,768]{2,1,0:T(8,128)(2,1)}), bf16[8,64,768]{2,1,0:T(8,128)(2,1)}, u32[]{:S(2)}, u32[]{:S(2)}) async-start(bf16[8,64,768]{2,1,0:T(8,128)(2,1)} %bitcast.298), calls=%async_computation.9 | async-start | bytes 1572864 | tf_op jit(solution)/shard_map/all_to_all | solution.py:79
  988.6 18.4 %all-to-all-start.9 = ((bf16[4,64,2048]{2,1,0:T(8,128)(2,1)}), bf16[4,64,2048]{2,1,0:T(8,128)(2,1)}, u32[]{:S(2)}, u32[]{:S(2)}) async-start(bf16[4,64,2048]{2,1,0:T(8,128)(2,1)} %bitcast.314), calls=%async_computation.10 | async-start | bytes 2097152 | tf_op jit(solution)/shard_map/all_to_all | solution.py:79
  1008.3 18.0 %collective-permute-start.28 = (bf16[64,2048]{1,0:T(8,128)(2,1)S(1)}, bf16[64,2048]{1,0:T(8,128)(2,1)S(1)}, u32[]{:S(2)}, u32[]{:S(2)}) collective-permute-start(bf16[64,2048]{1,0:T(8,128)(2,1)S(1)} %reduce_sum.236), channel_id=1, source_target_pairs={{0,0},{1,4},{2,8},{3,12},{4,16},{5,20},{6,24},{7,28},{8,1},{9,5},{... | collective-permute-start | bytes 786440 | tf_op jit(solution)/shard_map/ppermute | solution.py:252
  (73 other events, 1213.2 us)
Sparse Core Ops, SparseCore 0:
  37.3 30.6 all-gather.7
  70.1 101.2 all-gather.13
  174.4 85.4 all-gather.9
  261.6 123.3 all-gather.15
  696.1 124.3 all-gather.11
  826.9 111.6 reduce-scatter.1

commit v2 on v1

--- a/solution.py
+++ b/solution.py
@@ -3,6 +3,8 @@
 import jax
 import jax.numpy as jnp
 from jax import lax
+from jax.experimental import pallas as pl
+from jax.experimental.pallas import tpu as pltpu
 from jax.sharding import Mesh
 from jax.sharding import PartitionSpec as P
 
@@ -16,7 +18,7 @@
 
 SEQ = ("z", "y")
 DP = ("x", "core")
-FEED = ("core", "z")
+FEED = ("z", "core")
 REST = ("x", "y")
 ALL = ("x", "core", "z", "y")
 SWAP = [(0, 1), (1, 0)]
@@ -54,25 +56,24 @@
     return (grad_out, gain_term)
 
 
-def rotation(first_pos, tok_count):
+def turn_tables(tok_count):
     half_dim = HEAD_DIM // 2
-    position = (first_pos + jnp.arange(tok_count)).astype(F32)
+    position = jnp.arange(tok_count).astype(F32)
     inverse = jnp.exp(-(jnp.arange(half_dim).astype(F32) / half_dim) * math.log(ROPE_BASE))
     angles = position[:, None] * inverse[None, :]
-    return (jnp.cos(angles)[:, None, :], jnp.sin(angles)[:, None, :])
-
-
-def rotate(array_in, cosine, sine_t, turn_sign):
-    half_dim = array_in.shape[-1] // 2
-    first_half = array_in[..., :half_dim]
-    second_half = array_in[..., half_dim:]
-    return jnp.concatenate(
-        [
-            first_half * cosine - turn_sign * second_half * sine_t,
-            second_half * cosine + turn_sign * first_half * sine_t,
-        ],
-        axis=-1,
-    )
+    cosine, sine_t = jnp.cos(angles), jnp.sin(angles)
+    return (
+        jnp.concatenate([cosine, cosine], axis=1),
+        jnp.concatenate([-sine_t, sine_t], axis=1),
+    )
+
+
+def rotate(array_in, cosine, sine_t):
+    return array_in * cosine + pltpu.roll(array_in, HEAD_DIM // 2, 1) * sine_t
+
+
+def rotate_back(array_in, cosine, sine_t):
+    return array_in * cosine - pltpu.roll(array_in, HEAD_DIM // 2, 1) * sine_t
 
 
 def exchange(array_in, axes):
@@ -84,13 +85,264 @@
     return exchange(jnp.broadcast_to(array_in[None], (count,) + array_in.shape), axes)
 
 
-def ring_pairs(count):
-    order = [0] + list(range(1, count, 2)) + [v for v in range(count - 1, 0, -1) if v % 2 == 0]
-    return [(order[i], order[(i + 1) % count]) for i in range(count)]
+def tie(value, *earlier):
+    return lax.optimization_barrier((value,) + earlier)[0]
+
+
+def ring_order(count):
+    return [0] + list(range(1, count, 2)) + [v for v in range(count - 1, 0, -1) if v % 2 == 0]
 
 
 def core_swap(array_in):
     return lax.ppermute(array_in, "core", SWAP)
+
+
+def pick(array_in, at, axis=0):
+    return lax.dynamic_index_in_dim(array_in, at, axis, keepdims=False)
+
+
+def visible(doc_col, doc_row, first, rows, width):
+    at = first + lax.broadcasted_iota(jnp.int32, (rows, width), 0)
+    of = lax.broadcasted_iota(jnp.int32, (rows, width), 1)
+    return (of <= at) & (doc_col == doc_row)
+
+
+def attend_kernel(
+    step,
+    q_lin,
+    k_lin,
+    v_lin,
+    factors,
+    gain_q,
+    gain_k,
+    cosine,
+    sine_t,
+    doc_col,
+    doc_row,
+    queries,
+    keys,
+    values,
+    totals,
+    attended,
+):
+    cos, sin = cosine[...], sine_t[...]
+    queries[...] = rotate(q_lin[...] * factors[:, 0:1] * gain_q[...], cos, sin).astype(BF16)
+    keys[...] = rotate(k_lin[...] * factors[:, 1:2] * gain_k[...], cos, sin).astype(BF16)
+    values[...] = v_lin[...].astype(BF16)
+    scale = 1.0 / math.sqrt(HEAD_DIM)
+    for first in range(0, queries.shape[0], step):
+        width = first + step
+        mine = pl.ds(first, step)
+        scores = dot_right_t(queries[mine, :], keys[0:width, :]) * scale
+        seen = visible(doc_col[mine, :], doc_row[:, 0:width], first, step, width)
+        scores = jnp.where(seen, scores, MASK_FILL)
+        row_max = jnp.max(scores, axis=1, keepdims=True)
+        row_sum = jnp.sum(jnp.exp(scores - row_max), axis=1, keepdims=True)
+        total = row_max + jnp.log(row_sum)
+        probs = jnp.exp(scores - total).astype(BF16)
+        totals[0, mine, :] = total
+        attended[mine, :] = matmul(probs, values[0:width, :]).astype(BF16)
+
+
+def attend_back_kernel(
+    step,
+    queries,
+    keys,
+    values,
+    totals,
+    g_att,
+    q_lin,
+    k_lin,
+    gain_q,
+    gain_k,
+    cosine,
+    sine_t,
+    doc_col,
+    doc_row,
+    grad_q,
+    grad_k,
+    grad_v,
+    dot_q,
+    dot_k,
+    k_sum,
+    v_sum,
+):
+    scale = 1.0 / math.sqrt(HEAD_DIM)
+    k_sum[...] = jnp.zeros_like(k_sum)
+    v_sum[...] = jnp.zeros_like(v_sum)
+    for first in range(0, queries.shape[0], step):
+        width = first + step
+        mine, upto = pl.ds(first, step), pl.ds(0, width)
+        scores = dot_right_t(queries[mine, :], keys[upto, :]) * scale
+        seen = visible(doc_col[mine, :], doc_row[:, 0:width], first, step, width)
+        scores = jnp.where(seen, scores, MASK_FILL)
+        prob_full = jnp.exp(scores - totals[0, mine, :])
+        grad_probs = dot_right_t(g_att[mine, :], values[upto, :])
+        offsets = jnp.sum(prob_full * grad_probs, axis=1, keepdims=True)
+        grad_scores = (prob_full * (grad_probs - offsets)).astype(BF16)
+        back = matmul(grad_scores, keys[upto, :]) * scale
+        back = rotate_back(back, cosine[mine, :], sine_t[mine, :])
+        grad_q[mine, :] = back
+        dot_q[0, mine, :] = jnp.sum(back * gain_q[...] * q_lin[mine, :], axis=1, keepdims=True)
+        k_sum[upto, :] += dot_left_t(grad_scores, queries[mine, :])
+        v_sum[upto, :] += dot_left_t(prob_full.astype(BF16), g_att[mine, :])
+    back = rotate_back(k_sum[...] * scale, cosine[...], sine_t[...])
+    grad_k[...] = back
+    dot_k[0] = jnp.sum(back * gain_k[...] * k_lin[...], axis=1, keepdims=True)
+    grad_v[...] = v_sum[...].astype(BF16)
+
+
+def head_specs(length, heads):
+    def part(offset):
+        return pl.BlockSpec((length, HEAD_DIM), lambda h: (0, h + offset))
+
+    def gain():
+        return pl.BlockSpec((1, HEAD_DIM), lambda h: (0, h))
+
+    def whole(shape):
+        return pl.BlockSpec(shape, lambda h: (0, 0))
+
+    each = pl.BlockSpec((1, length, 1), lambda h: (h, 0, 0))
+    table = whole((length, HEAD_DIM))
+    docs = [whole((length, 1)), whole((1, length))]
+    return part, gain, whole, each, table, docs
+
+
+def attend(qkv, factors, gain_q, gain_k, tables, docs, heads):
+    length = qkv.shape[0]
+    part, gain, whole, each, table, doc_specs = head_specs(length, heads)
+    low = jax.ShapeDtypeStruct((length, heads * HEAD_DIM), BF16)
+    step = min(256, length)
+    pairs = heads * length * length * HEAD_DIM
+    return pl.pallas_call(
+        lambda *refs: attend_kernel(step, *refs),
+        grid=(heads,),
+        in_specs=[part(0), part(heads), part(2 * heads), whole((length, 2)), gain(), gain()]
+        + [table, table]
+        + doc_specs,
+        out_specs=[part(0), part(0), part(0), each, part(0)],
+        out_shape=[low, low, low, jax.ShapeDtypeStruct((heads, length, 1), F32), low],
+        compiler_params=pltpu.CompilerParams(vmem_limit_bytes=24 * 1024 * 1024),
+        cost_estimate=pl.CostEstimate(
+            flops=3 * pairs, bytes_accessed=qkv.size * 6, transcendentals=heads * length * length
+        ),
+    )(qkv, qkv, qkv, factors, gain_q, gain_k, *tables, *docs)
+
+
+def attend_back(saved, g_att, qkv, gain_q, gain_k, tables, docs, heads):
+    queries, keys, values, totals = saved
+    length = qkv.shape[0]
+    part, gain, whole, each, table, doc_specs = head_specs(length, heads)
+    flat = jax.ShapeDtypeStruct((length, heads * HEAD_DIM), F32)
+    low = jax.ShapeDtypeStruct((length, heads * HEAD_DIM), BF16)
+    line = jax.ShapeDtypeStruct((heads, length, 1), F32)
+    step = min(256, length)
+    pairs = heads * length * length * HEAD_DIM
+    return pl.pallas_call(
+        lambda *refs: attend_back_kernel(step, *refs),
+        grid=(heads,),
+        in_specs=[part(0), part(0), part(0), each, part(0), part(0), part(heads), gain(), gain()]
+        + [table, table]
+        + doc_specs,
+        out_specs=[part(0), part(0), part(0), each, each],
+        out_shape=[flat, flat, low, line, line],
+        scratch_shapes=[pltpu.VMEM((length, HEAD_DIM), F32)] * 2,
+        compiler_params=pltpu.CompilerParams(vmem_limit_bytes=24 * 1024 * 1024),
+        cost_estimate=pl.CostEstimate(
+            flops=7 * pairs, bytes_accessed=qkv.size * 8, transcendentals=heads * length * length
+        ),
+    )(queries, keys, values, totals, g_att, qkv, qkv, gain_q, gain_k, *tables, *docs)
+
+
+def feed_kernel(part, other, w_g, w_u, w_d, *refs):
+    hid, gate, upward, active, mine, away, total = refs[-7:]
+    block, tokens = pl.program_id(0), part.shape[0]
+
+    @pl.when(block == 0)
+    def _():
+        hid[:tokens, :] = part[...]
+        hid[tokens:, :] = other[...]
+
+    g = matmul(hid[...], w_g[...])
+    u = matmul(hid[...], w_u[...])
+    a = (g * (1.0 / (1.0 + jnp.exp(-g))) * u).astype(BF16)
+    gate[...], upward[...], active[...] = g, u, a
+    term = dot_right_t(a, w_d[...])
+
+    @pl.when(block == 0)
+    def _():
+        total[...] = term
+
+    @pl.when(block > 0)
+    def _():
+        total[...] += term
+
+    @pl.when(block == pl.num_programs(0) - 1)
+    def _():
+        mine[...] = total[:tokens, :]
+        away[...] = total[tokens:, :].astype(BF16)
+
+
+def feed_back_kernel(part, other, w_g, w_u, w_d, gate, upward, *refs):
+    g_res, g_gate, g_up, mine, away, total = refs[-6:]
+    block, tokens = pl.program_id(0), part.shape[0]
+
+    @pl.when(block == 0)
+    def _():
+        g_res[:tokens, :] = part[...]
+        g_res[tokens:, :] = other[...]
+
+    a = matmul(g_res[...], w_d[...])
+    g, u = gate[...], upward[...]
+    s = 1.0 / (1.0 + jnp.exp(-g))
+    gg = (a * u * s * (1.0 + g * (1.0 - s))).astype(BF16)
+    gu = (a * g * s).astype(BF16)
+    g_gate[...], g_up[...] = gg, gu
+    term = dot_right_t(gg, w_g[...]) + dot_right_t(gu, w_u[...])
+
+    @pl.when(block == 0)
+    def _():
+        total[...] = term
+
+    @pl.when(block > 0)
+    def _():
+        total[...] += term
+
+    @pl.when(block == pl.num_programs(0) - 1)
+    def _():
+        mine[...] = total[:tokens, :]
+        away[...] = total[tokens:, :].astype(BF16)
+
+
+def feed_step(at, count, pair, weights, saved, held, kernel, dtypes):
+    tokens, width = pair[0].shape
+    feed = weights[0].shape[1]
+    step = min(256, feed)
+    rows = 2 * tokens
+    block = pl.BlockSpec((rows, step), lambda f: (at, f))
+    part = pl.BlockSpec((tokens, width), lambda f: (0, 0))
+    full = pl.BlockSpec((rows, width), lambda f: (at, 0))
+    n_in = 5 + len(saved)
+    shapes = [jax.ShapeDtypeStruct((count * rows, width), BF16)]
+    shapes += [jax.ShapeDtypeStruct((count * rows, feed), d) for d in dtypes]
+    tail = [jax.ShapeDtypeStruct((tokens, width), d) for d in (F32, BF16)]
+    flops = 6 * rows * width * feed
+    return pl.pallas_call(
+        kernel,
+        grid=(feed // step,),
+        in_specs=[part, part]
+        + [pl.BlockSpec((width, step), lambda f: (0, f))] * 3
+        + [block] * len(saved)
+        + [pl.BlockSpec(memory_space=pl.ANY)] * len(held),
+        out_specs=[full] + [block] * len(dtypes) + [part, part],
+        out_shape=shapes + tail,
+        scratch_shapes=[pltpu.VMEM((rows, width), F32)],
+        input_output_aliases={n_in + k: k for k in range(len(held))},
+        compiler_params=pltpu.CompilerParams(vmem_limit_bytes=32 * 1024 * 1024),
+        cost_estimate=pl.CostEstimate(
+            flops=flops, bytes_accessed=6 * width * feed, transcendentals=rows * feed
+        ),
+    )(*pair, *weights, *saved, *held)
 
 
 def body(
@@ -121,156 +373,233 @@
     feed_width = w_gate.shape[1]
     n_feed = n_core * n_z
     own_feed = feed_width // n_feed
-    ring = ring_pairs(n_z)
+    x_at, core_at, z_at, y_at = (lax.axis_index(a) for a in ALL)
+    order = ring_order(n_z)
+    ring = [(order[i], order[(i + 1) % n_z]) for i in range(n_z)]
+    behind = jnp.array(
+        [[order[(order.index(z) - s) % n_z] for z in range(n_z)] for s in range(n_z)], jnp.int32
+    )
     tokens = inputs[0]
 
-    gains = spread(jnp.stack([gain_query, gain_key, gain_attn, gain_ffn]), ALL)
-    gains = gains.transpose(1, 0, 2).reshape(4, model_width).astype(F32)
-    my_gq = lax.dynamic_slice_in_dim(gains[0], seq_at * own_width, own_width)
-    my_gk = lax.dynamic_slice_in_dim(gains[1], seq_at * own_width, own_width)
-    gain_a, gain_f = gains[2], gains[3]
+    def ring_send(part):
+        return lax.ppermute(part, "z", ring)
+
+    def seq_gather(own):
+        chunks, held = [], own
+        for step in range(n_z):
+            chunks += [held, lax.ppermute(held, "y", SWAP)]
+            if step < n_z - 1:
+                held = ring_send(held)
+        return jnp.concatenate(chunks, axis=0)
+
+    def row_gather(own, gates):
+        chunks, held = [], own
+        for step in range(n_z):
+            chunks.append((held, lax.ppermute(held, "y", SWAP)))
+            if step < n_z - 1:
+                held = ring_send(tie(held, *gates(step, held)))
+        whole = jnp.zeros((n_seq * tok_count, own.shape[1]), own.dtype)
+        for step, (mine, other) in enumerate(chunks):
+            first = behind[step, z_at] * n_y * tok_count
+            whole = lax.dynamic_update_slice(whole, mine, (first + y_at * tok_count, 0))
+            whole = lax.dynamic_update_slice(whole, other, (first + (1 - y_at) * tok_count, 0))
+        return whole, held
+
+    def seq_order(array_in):
+        chunks = []
+        for step in range(n_z):
+            for at_y in (y_at, 1 - y_at):
+                first = (behind[step, z_at] * n_y + at_y) * tok_count
+                chunks.append(lax.dynamic_slice_in_dim(array_in, first, tok_count))
+        return jnp.concatenate(chunks, axis=0)
+
+    def seq_sum(part_of):
+        total = None
+        for step in list(range(1, n_z)) + [0]:
+            part = part_of(behind[step, z_at]).reshape(n_y, tok_count, model_width)
+            away = lax.ppermute(pick(part, 1 - y_at).astype(BF16), "y", SWAP)
+            mine = pick(part, y_at) + away.astype(F32)
+            if total is not None:
+                mine = mine + ring_send(total.astype(BF16)).astype(F32)
+            total = mine
+        return total
+
+    def feed_weights(mats, earlier):
+        blocks = jnp.stack(mats).reshape(len(mats), own_rows, n_feed, own_feed)
+        mine = exchange(tie(blocks.transpose(2, 0, 1, 3), *earlier), FEED)
+        return [mine[:, at].reshape(n_feed * own_rows, own_feed) for at in range(len(mats))]
+
+    def rest_gather(mine, late, later):
+        over_x, over_y = lax.ppermute(mine, "x", SWAP), lax.ppermute(mine, "y", SWAP)
+        half = mine.shape[0] // 2
+        corner_x = lax.ppermute(tie(over_x[:half], late), "y", SWAP)
+        corner_y = lax.ppermute(tie(over_y[half:], late), "x", SWAP)
+        mine = tie(mine, later)
+        whole = jnp.zeros((n_x, n_y) + mine.shape, BF16)
+        for at_x, at_y, first, part in (
+            (x_at, y_at, 0, mine),
+            (1 - x_at, y_at, 0, over_x),
+            (x_at, 1 - y_at, 0, over_y),
+            (1 - x_at, 1 - y_at, 0, corner_x),
+            (1 - x_at, 1 - y_at, half, corner_y),
+        ):
+            whole = lax.dynamic_update_slice(whole, part[None, None], (at_x, at_y, first, 0))
+        return whole.reshape(model_width, own_feed)
+
+    def seq_total(term):
+        term = term + lax.ppermute(term, "y", SWAP)
+        hop = 1
+        while hop < n_z:
+            term = term + lax.ppermute(term, "z", [(z, z ^ hop) for z in range(n_z)])
+            hop *= 2
+        return term
+
+    def to_feed_order(array_in):
+        lead = array_in.shape[:-1]
+        parts = array_in.reshape((-1, n_x, n_core, n_z, n_y, own_rows))
+        return parts.transpose(0, 1, 4, 3, 2, 5).reshape(lead + (model_width,))
+
+    def from_feed_order(array_in):
+        lead = array_in.shape[:-1]
+        parts = array_in.reshape((-1, n_x, n_y, n_z, n_core, own_rows))
+        return parts.transpose(0, 1, 4, 3, 2, 5).reshape(lead + (model_width,))
 
     w_heads = jnp.stack([w_query, w_key, w_value])
     w_heads = w_heads.reshape(3, own_rows, n_seq, own_width).transpose(2, 1, 0, 3)
     w_heads = exchange(w_heads.reshape(n_seq, own_rows, 3 * own_width), SEQ)
-    w_heads = lax.all_gather(w_heads, DP, axis=0, tiled=True).reshape(model_width, 3 * own_width)
-    x_row = lax.all_gather(tokens, SEQ, axis=0, tiled=True)
-    full_o = lax.all_gather(w_out, ALL, axis=0, tiled=True)
-
-    w_feed = jnp.stack([w_gate, w_up, w_down.T])
-    w_feed = w_feed.reshape(3, own_rows, n_feed, own_feed).transpose(2, 0, 1, 3)
-    w_feed = exchange(w_feed, FEED)
-    w_feed = lax.all_gather(w_feed, REST, axis=0, tiled=False)
-    w_feed = w_feed.reshape(n_x, n_y, n_core, n_z, 3, own_rows, own_feed)
-    w_feed = w_feed.transpose(4, 0, 2, 3, 1, 5, 6).reshape(3, model_width, own_feed)
-    w_g, w_u, w_d = w_feed[0], w_feed[1], w_feed[2]
+    w_mine = w_heads.reshape(n_seq * own_rows, 3 * own_width)
+
+    w_over = lax.ppermute(w_mine, "x", SWAP)
+    w_heads = jnp.zeros((n_x, n_core) + w_mine.shape, BF16)
+    for at_x, part in ((x_at, w_mine), (1 - x_at, w_over)):
+        w_heads = lax.dynamic_update_slice(w_heads, part[None, None], (at_x, core_at, 0, 0))
+        w_heads = lax.dynamic_update_slice(
+            w_heads, core_swap(part)[None, None], (at_x, 1 - core_at, 0, 0)
+        )
+    w_heads = w_heads.reshape(model_width, 3 * own_width)
+    def gates(step, held):
+        return (w_mine,) if step == 1 else ()
+
+    x_row, x_last = row_gather(tokens, gates)
+    full_o = lax.all_gather(to_feed_order(w_out), ALL, axis=0, tiled=True)
+    moved = feed_weights([w_gate, w_up, w_down.T], (x_last,))
+
+    gains = spread(tie(jnp.stack([gain_query, gain_key, gain_attn, gain_ffn]), *moved), ALL)
+    gains = gains.transpose(1, 0, 2).reshape(4, model_width).astype(F32)
+    my_gq = lax.dynamic_slice_in_dim(gains[0:1], seq_at * own_width, own_width, 1)
+    my_gk = lax.dynamic_slice_in_dim(gains[1:2], seq_at * own_width, own_width, 1)
+    gain_a, gain_f = to_feed_order(gains[2]), to_feed_order(gains[3])
 
     qkv = matmul(x_row, w_heads)
-    q_lin, k_lin, v_lin = (
-        qkv[:, :own_width],
-        qkv[:, own_width : 2 * own_width],
-        qkv[:, 2 * own_width :],
-    )
+    q_lin, k_lin = qkv[:, :own_width], qkv[:, own_width : 2 * own_width]
     squares = jnp.stack([jnp.sum(q_lin * q_lin, axis=1), jnp.sum(k_lin * k_lin, axis=1)])
-    squares = jnp.sum(spread(squares, SEQ), axis=0) / model_width
-    factors = lax.rsqrt(squares + NORM_EPS)
-    q_factor, k_factor = factors[0][:, None], factors[1][:, None]
-    cosine, sine_t = rotation(0, length)
-
-    def to_heads(array_in, turn_sign):
-        heads = rotate(array_in.reshape(length, own_heads, HEAD_DIM), cosine, sine_t, turn_sign)
-        return heads.astype(BF16).transpose(1, 0, 2)
-
-    def from_heads(array_in):
-        return array_in.transpose(1, 0, 2).reshape(length, own_width)
-
-    queries = to_heads(q_lin * q_factor * my_gq, 1.0)
-    keys = to_heads(k_lin * k_factor * my_gk, 1.0)
-    values = v_lin.astype(BF16).reshape(length, own_heads, HEAD_DIM).transpose(1, 0, 2)
-
+    squares = seq_total(squares) / model_width
+    factors = lax.rsqrt(squares + NORM_EPS).T
+    q_factor, k_factor = factors[:, 0:1], factors[:, 1:2]
+    tables = turn_tables(length)
+    doc_ends = jnp.cumsum(doc_lengths[0])
     position = jnp.arange(length)
-    doc_ends = jnp.cumsum(doc_lengths[0])
     doc_ids = jnp.sum((position[:, None] >= doc_ends[None, :]).astype(jnp.int32), axis=1)
-    allowed = (position[None, :] <= position[:, None]) & (doc_ids[None, :] == doc_ids[:, None])
-    scores = jnp.einsum("htd,hkd->htk", queries, keys, preferred_element_type=F32) * score_scale
-    scores = jnp.where(allowed[None], scores, MASK_FILL)
-    row_max = jnp.max(scores, axis=-1, keepdims=True)
-    totals = row_max + jnp.log(jnp.sum(jnp.exp(scores - row_max), axis=-1, keepdims=True))
-    prob_full = jnp.exp(scores - totals)
-    probs = prob_full.astype(BF16)
-    mixed = jnp.einsum("htk,hkd->htd", probs, values, preferred_element_type=F32)
-    attended = from_heads(mixed).astype(BF16)
+    docs = (doc_ids[:, None], doc_ids[None, :])
+    *saved, attended = attend(qkv, factors, my_gq, my_gk, tables, docs, own_heads)
 
     att_tok = exchange(attended.reshape(n_seq, tok_count, own_width), SEQ)
     att_tok = att_tok.transpose(1, 0, 2).reshape(tok_count, model_width)
     branch = matmul(att_tok, full_o)
+    w_g = rest_gather(moved[0], attended, branch)
+    w_u = lax.all_gather(moved[1], REST, axis=0, tiled=True)
+    w_d = rest_gather(tie(moved[2], qkv), attended, branch)
     branch_norm, branch_factor = norm_apply(branch, gain_a)
-    hidden = tokens.astype(F32) + branch_norm
+    hidden = to_feed_order(tokens).astype(F32) + branch_norm
     hidden_low = hidden.astype(BF16)
 
-    def ring_gather(own):
-        held = [own]
-        for _ in range(n_z - 1):
-            held.append(lax.ppermute(held[-1], "z", ring))
-        return [jnp.concatenate([part, core_swap(part)], axis=0) for part in held]
-
-    def ring_sum(parts):
-        total = None
-        for step in list(range(1, n_z)) + [0]:
-            part = parts[step]
-            mine = part[:tok_count] + core_swap(part[tok_count:].astype(BF16)).astype(F32)
-            if total is not None:
-                mine = mine + lax.ppermute(total.astype(BF16), "z", ring).astype(F32)
-            total = mine
-        return total
-
-    hid = ring_gather(hidden_low)
-    gate = [matmul(part, w_g) for part in hid]
-    upward = [matmul(part, w_u) for part in hid]
-    sig = [jax.nn.sigmoid(part) for part in gate]
-    active = [(g * s * u).astype(BF16) for g, s, u in zip(gate, sig, upward)]
-    result = ring_sum([dot_right_t(part, w_d) for part in active])
+    def feed_pass(own, saved, kernel, dtypes):
+        held, total, rows = [], None, own
+        for at in range(n_z):
+            pair = (rows, core_swap(rows))
+            if at < n_z - 1:
+                rows = ring_send(rows)
+            if at > 1:
+                pair = tie(pair, total)
+            *held, mine, away = feed_step(
+                at, n_z, pair, (w_g, w_u, w_d), saved, held, kernel, dtypes
+            )
+            if at == 0:
+                first = (mine, away)
+            else:
+                total = add_up(mine, away, total)
+        return held, add_up(*first, total)
+
+    def add_up(mine, away, total):
+        mine = mine + core_swap(away).astype(F32)
+        if total is not None:
+            mine = mine + ring_send(total.astype(BF16)).astype(F32)
+        return mine
+
+    (hid, gate, upward, active), result = feed_pass(
+        hidden_low, (), feed_kernel, (F32, F32, BF16)
+    )
     result_norm, result_factor = norm_apply(result, gain_f)
-    output = (hidden + result_norm).astype(BF16)
-
-    grad_top = cotangent[0].astype(F32)
+    output = from_feed_order((hidden + result_norm).astype(BF16))
+
+    grad_top = to_feed_order(cotangent[0]).astype(F32)
     grad_result, ffn_gain_term = norm_back(result, result_factor, gain_f, grad_top)
-    g_res = ring_gather(grad_result.astype(BF16))
-    g_act = [matmul(part, w_d) for part in g_res]
-    g_gate = [
-        (a * u * s * (1.0 + g * (1.0 - s))).astype(BF16)
-        for a, u, s, g in zip(g_act, upward, sig, gate)
-    ]
-    g_up = [(a * g * s).astype(BF16) for a, g, s in zip(g_act, gate, sig)]
-    grad_hidden = grad_top + ring_sum(
-        [dot_right_t(a, w_g) + dot_right_t(b, w_u) for a, b in zip(g_gate, g_up)]
-    )
-
-    def feed_grad(left, right):
-        term = dot_left_t(jnp.concatenate(left, axis=0), jnp.concatenate(right, axis=0))
-        term = term.astype(BF16).reshape(n_x, n_core, n_z, n_y, own_rows, own_feed)
-        term = term.transpose(0, 3, 1, 2, 4, 5).reshape(n_x * n_y, n_feed, own_rows, own_feed)
-        term = jnp.sum(exchange(term, REST).astype(F32), axis=0)
-        term = exchange(term.astype(BF16), FEED)
+    def token_sum(left, right):
+        return dot_left_t(left, right).astype(BF16)
+
+    def rest_sum(term):
+        return lax.psum_scatter(term, REST, scatter_dimension=0, tiled=True)
+
+    def feed_home(term):
+        return exchange(term.reshape(n_feed, own_rows, own_feed), FEED)
+
+    def feed_rows(term):
         return term.transpose(1, 0, 2).reshape(own_rows, feed_width).astype(F32)
 
-    grad_w_down = feed_grad(g_res, active).T
-    grad_w_gate = feed_grad(hid, g_gate)
-    grad_w_up = feed_grad(hid, g_up)
+    def dp_sum(term):
+        rows = term.shape[0] // n_dp
+
+        def of(array_in, at):
+            return lax.dynamic_slice_in_dim(array_in, at * rows, rows)
+
+        def cores(at):
+            return jnp.concatenate([of(term, x * n_core + at) for x in range(n_x)])
+
+        away = core_swap(cores(1 - core_at))
+        term = (cores(core_at).astype(F32) + away.astype(F32)).astype(BF16)
+        away = lax.ppermute(of(term, 1 - x_at), "x", SWAP)
+        return (of(term, x_at).astype(F32) + away.astype(F32)).astype(BF16)
+
+    (g_res, g_gate, g_up), grad_ffn = feed_pass(
+        grad_result.astype(BF16), (gate, upward), feed_back_kernel, (BF16, BF16)
+    )
+    grad_hidden = grad_top + grad_ffn
+    term_d = token_sum(g_res, active)
+    sum_d = rest_sum(term_d)
+    term_g, term_u = token_sum(hid, g_gate), token_sum(hid, g_up)
 
     grad_branch, attn_gain_term = norm_back(branch, branch_factor, gain_a, grad_hidden)
     grad_branch = grad_branch.astype(BF16)
     grad_attended = dot_right_t(grad_branch, full_o).astype(BF16)
     g_att = grad_attended.reshape(tok_count, n_seq, own_width).transpose(1, 0, 2)
-    g_att = exchange(g_att, SEQ).reshape(length, own_heads, HEAD_DIM).transpose(1, 0, 2)
-
-    branch_row = lax.all_gather(grad_branch, SEQ, axis=0, tiled=True)
-    grad_w_out = dot_left_t(attended, branch_row).astype(BF16)
-    grad_w_out = grad_w_out.reshape(n_dp, own_rows, model_width)
-    grad_w_out = jnp.sum(exchange(grad_w_out, DP).astype(F32), axis=0)
+    g_att = exchange(g_att, SEQ).reshape(length, own_width)
+    g_att = tie(g_att, term_g, term_u)
+    sum_g, sum_u = rest_sum(term_g), rest_sum(term_u)
+
+    grad_q, grad_k, grad_v, dot_q, dot_k = attend_back(
+        saved, g_att, qkv, my_gq, my_gk, tables, docs, own_heads
+    )
+    dots = jnp.stack([jnp.sum(dot_q, axis=(0, 2)), jnp.sum(dot_k, axis=(0, 2))])
+    dots = seq_total(dots) / model_width
+    home_d = feed_home(tie(sum_d, dots))
+
+    branch_row = seq_gather(tie(grad_branch, dots))
+    grad_w_out = dot_left_t(seq_order(attended), branch_row).astype(BF16)
+    grad_w_out = dp_sum(grad_w_out)
     home = [(d * n_seq + s, s * n_dp + d) for d in range(n_dp) for s in range(n_seq)]
-    grad_w_out = lax.ppermute(grad_w_out.astype(BF16), ALL, home).astype(F32)
-
-    grad_probs = jnp.einsum("htd,hkd->htk", g_att, values, preferred_element_type=F32)
-    offsets = jnp.sum(prob_full * grad_probs, axis=-1, keepdims=True)
-    grad_scores = (prob_full * (grad_probs - offsets)).astype(BF16)
-    grad_q = (
-        jnp.einsum("htk,hkd->htd", grad_scores, keys, preferred_element_type=F32) * score_scale
-    )
-    grad_k = (
-        jnp.einsum("htk,htd->hkd", grad_scores, queries, preferred_element_type=F32) * score_scale
-    )
-    grad_v = jnp.einsum("htk,htd->hkd", probs, g_att, preferred_element_type=F32)
-
-    def turn_back(array_in):
-        heads = rotate(array_in.transpose(1, 0, 2), cosine, sine_t, -1.0)
-        return heads.reshape(length, own_width)
-
-    grad_q, grad_k = turn_back(grad_q), turn_back(grad_k)
-    dots = jnp.stack(
-        [jnp.sum(grad_q * my_gq * q_lin, axis=1), jnp.sum(grad_k * my_gk * k_lin, axis=1)]
-    )
-    dots = jnp.sum(spread(dots, SEQ), axis=0) / model_width
+    grad_w_out = lax.ppermute(grad_w_out, ALL, home)
+    grad_w_out = from_feed_order(grad_w_out).astype(F32)
+
 
     def lin_back(grad_in, lin, factor, gain_vec, mean_dot):
         gain_term = jnp.sum(grad_in * lin * factor, axis=0)
@@ -279,16 +608,20 @@
 
     grad_q_lin, query_gain_term = lin_back(grad_q, q_lin, q_factor, my_gq, dots[0][:, None])
     grad_k_lin, key_gain_term = lin_back(grad_k, k_lin, k_factor, my_gk, dots[1][:, None])
-    grad_lin = jnp.concatenate([grad_q_lin, grad_k_lin, from_heads(grad_v).astype(BF16)], axis=1)
-
-    grad_row = dot_right_t(grad_lin, w_heads).astype(BF16)
-    grad_input = grad_hidden + lax.psum_scatter(
-        grad_row, SEQ, scatter_dimension=0, tiled=True
-    ).astype(F32)
+    grad_lin = jnp.concatenate([grad_q_lin, grad_k_lin, grad_v], axis=1)
+
+    def row_part(z_of):
+        rows = lax.dynamic_slice_in_dim(grad_lin, z_of * n_y * tok_count, n_y * tok_count)
+        return dot_right_t(rows, w_heads)
+
+    grad_input = from_feed_order(grad_hidden) + seq_sum(row_part)
 
     grad_heads = dot_left_t(x_row, grad_lin).astype(BF16)
-    grad_heads = grad_heads.reshape(n_dp, n_seq * own_rows, 3 * own_width)
-    grad_heads = jnp.sum(exchange(grad_heads, DP).astype(F32), axis=0).astype(BF16)
+    grad_heads = dp_sum(grad_heads)
+    home_g = feed_home(tie(sum_g, home_d))
+    home_u = feed_home(tie(sum_u, home_g))
+    grad_w_gate, grad_w_up = feed_rows(home_g), feed_rows(home_u)
+    grad_w_down = feed_rows(home_d).T
     grad_heads = exchange(grad_heads.reshape(n_seq, own_rows, 3 * own_width), SEQ)
     grad_heads = grad_heads.reshape(n_seq, own_rows, 3, own_width).transpose(2, 1, 0, 3)
     grad_heads = grad_heads.reshape(3, own_rows, model_width).astype(F32)
@@ -299,7 +632,12 @@
         )
 
     gain_terms = jnp.stack(
-        [place(query_gain_term), place(key_gain_term), attn_gain_term, ffn_gain_term]
+        [
+            place(query_gain_term),
+            place(key_gain_term),
+            from_feed_order(attn_gain_term),
+            from_feed_order(ffn_gain_term),
+        ]
     )
     gain_terms = gain_terms.reshape(4, n_all, own_rows).transpose(1, 0, 2)
     gain_grads = jnp.sum(exchange(gain_terms, ALL), axis=0)
@@ -327,6 +665,19 @@
     inverse = jnp.exp(-(jnp.arange(half_dim).astype(jnp.float32) / half_dim) * math.log(ROPE_BASE))
     angles = position[:, None] * inverse[None, :]
     return (jnp.cos(angles)[None, :, None, :], jnp.sin(angles)[None, :, None, :])
+
+
+def plain_rotate(array_in, cosine, sine_t, turn_sign):
+    half_dim = array_in.shape[-1] // 2
+    first_half = array_in[..., :half_dim]
+    second_half = array_in[..., half_dim:]
+    return jnp.concatenate(
+        [
+            first_half * cosine - turn_sign * second_half * sine_t,
+            second_half * cosine + turn_sign * first_half * sine_t,
+        ],
+        axis=-1,
+    )
 
 
 def plain_body(
@@ -373,12 +724,12 @@
     q_norm, q_factor = norm_apply(q_lin, full_gq.astype(jnp.float32))
     k_norm, k_factor = norm_apply(k_lin, full_gk.astype(jnp.float32))
     queries = (
-        rotate(q_norm.reshape(row_count, tok_count, HEADS, HEAD_DIM), cosine, sine_t, 1.0)
+        plain_rotate(q_norm.reshape(row_count, tok_count, HEADS, HEAD_DIM), cosine, sine_t, 1.0)
         .astype(jnp.bfloat16)
         .transpose(2, 0, 1, 3)
     )
     keys_mine = (
-        rotate(k_norm.reshape(row_count, tok_count, HEADS, HEAD_DIM), cosine, sine_t, 1.0)
+        plain_rotate(k_norm.reshape(row_count, tok_count, HEADS, HEAD_DIM), cosine, sine_t, 1.0)
         .astype(jnp.bfloat16)
         .transpose(2, 0, 1, 3)
     )
@@ -506,10 +857,10 @@
             value_terms.astype(jnp.bfloat16), "seq", scatter_dimension=2, tiled=True
         ).astype(jnp.float32),
     )
-    grad_q_norm = rotate(grad_queries.transpose(1, 2, 0, 3), cosine, sine_t, -1.0).reshape(
+    grad_q_norm = plain_rotate(grad_queries.transpose(1, 2, 0, 3), cosine, sine_t, -1.0).reshape(
         row_count * tok_count, model_width
     )
-    grad_k_norm = rotate(grad_keys.transpose(1, 2, 0, 3), cosine, sine_t, -1.0).reshape(
+    grad_k_norm = plain_rotate(grad_keys.transpose(1, 2, 0, 3), cosine, sine_t, -1.0).reshape(
         row_count * tok_count, model_width
     )
     grad_q_lin, query_gain_term = norm_back(
@@ -564,7 +915,7 @@
 
 def solution(mesh):
     n_dp, n_seq = mesh.shape["dp"], mesh.shape["seq"]
-    if HEADS % n_seq == 0 and n_dp % 2 == 0 and n_seq % 2 == 0:
+    if n_dp == 4 and n_seq % 2 == 0 and HEADS % n_seq == 0:
         grid = Mesh(mesh.devices.reshape(n_dp // 2, 2, n_seq // 2, 2), ALL)
         layer, dp, seq = body, DP, SEQ
     else:

time: 1050 us -> 938 us (0.89)
  blocking collectives: 131 us -> 0 us
  Pallas kernels: 0 us -> 89.4 us
  local copies, waits for them, and re-layouts: 91.3 us -> 167 us
  waiting for transfers between devices: 478 us -> 413 us
  matrix products: 120 us -> 57.5 us
  starting transfers between devices: 137 us -> 122 us
    ppermute x13 -> x51, waiting for transfers between devices: 129 us -> 391 us  [the longest x21 217 us: ring_send(): return lax.ppermute(part, 'z', ring)]
    all_to_all x15 -> x10, waiting for transfers between devices: 261 us -> 18.1 us  [exchange(): lax.all_to_all(array_in, axes, split_axis=0, concat_axis=0, tiled=True)]
    all_to_all x2 -> x0, blocking collectives: 131 us -> none  [exchange(): lax.all_to_all(array_in, axes, split_axis=0, concat_axis=0, tiled=True)]
    pallas_call x0 -> x10, Pallas kernels: none -> 89.4 us  [the longest x8 71.7 us: feed_step(): pl.pallas_call(kernel, grid=(feed // step,), in_specs=[part, part] + [pl....]
    all_gather x5 -> x2, waiting for transfers between devices: 86.9 us -> 0.01 us  [the longest x1 0.01 us: body(): full_o = lax.all_gather(to_feed_order(w_out), ALL, axis=0, tiled=True)]
    all_to_all x15 -> x10, starting transfers between devices: 110 us -> 68.6 us  [exchange(): lax.all_to_all(array_in, axes, split_axis=0, concat_axis=0, tiled=True)]
    unnamed x172 -> x214, local copies, waits for them, and re-layouts: 40.3 us -> 71 us
    ppermute x13 -> x51, starting transfers between devices: 6.53 us -> 34 us  [the longest x21 5.17 us: ring_send(): return lax.ppermute(part, 'z', ring)]
  transfers between devices with their start and end apart: 50 -> 86, of which waited for: 30 -> 43; matrix products, arithmetic and copies ran while one was open for 19% -> 24% of each run, Pallas kernels for 0% -> 8%
where the time goes in v2:
time: 938 us; the launch traced here: 927 us
  waiting for transfers between devices  413 us (44%)
  local copies, waits for them, and re-layouts  167 us (18%)
  starting transfers between devices  122 us (13%)
  Pallas kernels  89.4 us (10%)
  matrix products  57.5 us (6%)
  other arithmetic  56.3 us (6%)
  between operations  21.1 us (2%)
    ppermute x21, waiting for transfers between devices, ring_send(): return lax.ppermute(part, 'z', ring)  217 us
    pallas_call x8, Pallas kernels, feed_step(): pl.pallas_call(kernel, grid=(feed // step,), in_specs=[part, part] + [pl....  71.7 us
    unnamed x214, local copies, waits for them, and re-layouts  71 us
    all_to_all x10, starting transfers between devices, exchange(): lax.all_to_all(array_in, axes, split_axis=0, concat_axis=0, tiled=True)  68.6 us
    ppermute x4, waiting for transfers between devices, seq_total(): term = term + lax.ppermute(term, 'z', [(z, z ^ hop) for z in range(n_z)])  51.5 us
    dot_general x5, matrix products, dot_left_t(): lax.dot_general(left_mat, right_mat, (((0,), (0,)), ((), ())), preferred_...  34.6 us
    ppermute x1, waiting for transfers between devices, body(): grad_w_out = lax.ppermute(grad_w_out, ALL, home)  30.2 us
    ppermute x2, waiting for transfers between devices, seq_total(): term = term + lax.ppermute(term, 'y', SWAP)  20.9 us
  transfers between devices with their start and end apart: 86, of which 43 were waited for; matrix products, arithmetic and copies ran while one was open for 24% of the time, Pallas kernels for 8%

profile of v2, /device:TPU:25, one launch (start us, length us, event | category | flops | bytes accessed | tf_op | source)
XLA Modules:
  0.0 926.8 jit_solution(15009062865437525419)
XLA Ops:
  22.2 45.2 %collective-permute-done.1 = bf16[128,2048]{1,0:T(8,128)(2,1)} collective-permute-done((bf16[128,2048]{1,0:T(8,128)(2,1)S(1)}, bf16[128,2048]{1,0:T(8,128)(2,1)}, u32[]{:S(2)}, u32[]{:S(2)}) %collective-permute-start.1) | collective-permute-done | bytes 524320 | tf_op jit(solution)/shard_map/ppermute | solution.py:385
  67.4 28.2 %collective-permute-done.3 = bf16[128,2048]{1,0:T(8,128)(2,1)S(1)} collective-permute-done((bf16[128,2048]{1,0:T(8,128)(2,1)}, bf16[128,2048]{1,0:T(8,128)(2,1)S(1)}, u32[]{:S(2)}, u32[]{:S(2)}) %collective-permute-start.3) | collective-permute-done | bytes 524320 | tf_op jit(solution)/shard_map/ppermute | solution.py:385
  97.9 16.3 %collective-permute-done.5 = bf16[128,2048]{1,0:T(8,128)(2,1)S(1)} collective-permute-done((bf16[128,2048]{1,0:T(8,128)(2,1)S(1)}, bf16[128,2048]{1,0:T(8,128)(2,1)S(1)}, u32[]{:S(2)}, u32[]{:S(2)}) %collective-permute-start.5) | collective-permute-done | bytes 524320 | tf_op jit(solution)/shard_map/ppermute | solution.py:385
  118.3 9.2 all-to-all-start.1
  157.2 6.3 collective-permute-done.8
  169.0 9.5 %collective-permute-done.6 = bf16[128,2048]{1,0:T(8,128)(2,1)S(1)} collective-permute-done((bf16[128,2048]{1,0:T(8,128)(2,1)S(1)}, bf16[128,2048]{1,0:T(8,128)(2,1)S(1)}, u32[]{:S(2)}, u32[]{:S(2)}) %collective-permute-start.6) | collective-permute-done | bytes 524320 | tf_op jit(solution)/shard_map/ppermute | solution.py:398
  179.4 7.3 fusion.20
  204.3 13.3 %collective-permute-done.11 = f32[2,1024]{0,1:T(8,128)S(1)} collective-permute-done((f32[2,1024]{0,1:T(8,128)}, f32[2,1024]{0,1:T(8,128)S(1)}, u32[]{:S(2)}, u32[]{:S(2)}) %collective-permute-start.11) | collective-permute-done | bytes 8224 | tf_op jit(solution)/shard_map/ppermute | solution.py:453
  221.8 7.6 all-to-all-start.2
  229.3 16.6 %collective-permute-done.12 = f32[2,1024]{0,1:T(8,128)} collective-permute-done((f32[2,1024]{0,1:T(8,128)}, f32[2,1024]{0,1:T(8,128)}, u32[]{:S(2)}, u32[]{:S(2)}) %collective-permute-start.12) | collective-permute-done | bytes 8224 | tf_op jit(solution)/shard_map/ppermute | solution.py:453
  255.4 7.2 shard_map.246
  287.7 10.9 %collective-permute-done.14 = bf16[512,1024]{1,0:T(8,128)(2,1)} collective-permute-done((bf16[512,1024]{1,0:T(8,128)(2,1)}, bf16[512,1024]{1,0:T(8,128)(2,1)}, u32[]{:S(2)}, u32[]{:S(2)}) %collective-permute-start.14) | collective-permute-done | bytes 1048608 | tf_op jit(solution)/shard_map/ppermute | solution.py:433
  327.8 7.6 collective-permute-done.23.part
  341.7 8.9 shard_map.247
  350.6 8.2 shard_map.248
  361.8 7.9 shard_map.249
  375.4 9.9 %collective-permute-done.31 = bf16[128,2048]{1,0:T(8,128)(2,1)S(1)} collective-permute-done((bf16[128,2048]{1,0:T(8,128)(2,1)S(1)}, bf16[128,2048]{1,0:T(8,128)(2,1)S(1)}, u32[]{:S(2)}, u32[]{:S(2)}) %collective-permute-start.31) | collective-permute-done | bytes 524320 | tf_op jit(solution)/shard_map/ppermute | solution.py:385
  385.5 7.7 shard_map.250
  403.0 13.1 %collective-permute-done.33 = bf16[128,2048]{1,0:T(8,128)(2,1)S(1)} collective-permute-done((bf16[128,2048]{1,0:T(8,128)(2,1)S(1)}, bf16[128,2048]{1,0:T(8,128)(2,1)S(1)}, u32[]{:S(2)}, u32[]{:S(2)}) %collective-permute-start.33) | collective-permute-done | bytes 524320 | tf_op jit(solution)/shard_map/ppermute | solution.py:385
  424.0 7.0 collective-permute-done.34
  435.9 10.9 %collective-permute-done.37.part = bf16[128,2048]{1,0:T(8,128)(2,1)S(1)} collective-permute-done((bf16[128,2048]{1,0:T(8,128)(2,1)S(1)}, bf16[128,2048]{1,0:T(8,128)(2,1)S(1)}, u32[]{:S(2)}, u32[]{:S(2)}) %collective-permute-start.37) | collective-permute-done | bytes 524320 | tf_op jit(solution)/shard_map/ppermute | solution.py:385
  451.6 9.7 %shard_map.251 = (bf16[1024,2048]{1,0:T(8,128)(2,1)S(1)}, bf16[1024,1024]{1,0:T(8,128)(2,1)S(1)}, bf16[1024,1024]{1,0:T(8,128)(2,1)S(1)}, f32[128,2048]{1,0:T(8,128)S(1)}, bf16[128,2048]{1,0:T(8,128)(2,1)S(1)}) custom-call(bf16[128,2048]{1,0:T(8,128)(2,1)S(1)} %subtract_convert_fusion.3.part, bf16[128,2048]{1,0:T(8,128)(2,1)S(1)} %collective-permute-done.35.other, ...), custom_call_target="tpu_custom_call" | custom-call | flops 3221225472 | bytes 12582912 | tf_op jit(solution)/shard_map/pallas_call | solution.py:330
  462.3 9.7 %shard_map.252 = (bf16[1024,2048]{1,0:T(8,128)(2,1)S(1)}, bf16[1024,1024]{1,0:T(8,128)(2,1)S(1)}, bf16[1024,1024]{1,0:T(8,128)(2,1)S(1)}, f32[128,2048]{1,0:T(8,128)S(1)}, bf16[128,2048]{1,0:T(8,128)(2,1)S(1)}) custom-call(bf16[128,2048]{1,0:T(8,128)(2,1)S(1)} %collective-permute-done.37.part, ...), custom_call_target="tpu_custom_call", output_to_operand_aliasing={{0}: (7, {}), {1}: (8, {}), {2}: (9, {})} | custom-call | flops 3221225472 | bytes 12582912 | tf_op jit(solution)/shard_map/pallas_call | solution.py:330
  474.7 9.7 %shard_map.253 = (bf16[1024,2048]{1,0:T(8,128)(2,1)S(1)}, bf16[1024,1024]{1,0:T(8,128)(2,1)S(1)}, bf16[1024,1024]{1,0:T(8,128)(2,1)S(1)}, f32[128,2048]{1,0:T(8,128)S(1)}, bf16[128,2048]{1,0:T(8,128)(2,1)S(1)}) custom-call(bf16[128,2048]{1,0:T(8,128)(2,1)S(1)} %collective-permute-done.38.part, ...), custom_call_target="tpu_custom_call", output_to_operand_aliasing={{0}: (7, {}), {1}: (8, {}), {2}: (9, {})} | custom-call | flops 3221225472 | bytes 12582912 | tf_op jit(solution)/shard_map/pallas_call | solution.py:330
  487.8 11.6 %collective-permute-done.45 = bf16[128,2048]{1,0:T(8,128)(2,1)S(1)} collective-permute-done((bf16[128,2048]{1,0:T(8,128)(2,1)S(1)}, bf16[128,2048]{1,0:T(8,128)(2,1)S(1)}, u32[]{:S(2)}, u32[]{:S(2)}) %collective-permute-start.45) | collective-permute-done | bytes 524320 | tf_op jit(solution)/shard_map/ppermute | solution.py:385
  500.4 9.8 %shard_map.254 = (bf16[1024,2048]{1,0:T(8,128)(2,1)S(1)}, bf16[1024,1024]{1,0:T(8,128)(2,1)S(1)}, bf16[1024,1024]{1,0:T(8,128)(2,1)S(1)}, f32[128,2048]{1,0:T(8,128)S(1)}, bf16[128,2048]{1,0:T(8,128)(2,1)S(1)}) custom-call(bf16[128,2048]{1,0:T(8,128)(2,1)S(1)} %collective-permute-done.39.part, ...), custom_call_target="tpu_custom_call", output_to_operand_aliasing={{0}: (7, {}), {1}: (8, {}), {2}: (9, {})} | custom-call | flops 3221225472 | bytes 12582912 | tf_op jit(solution)/shard_map/pallas_call | solution.py:330
  514.6 6.1 convolution_convert_fusion
  520.8 9.5 %convolution_convert_fusion.2 = bf16[2048,1024]{1,0:T(8,128)(2,1)} fusion(bf16[1024,2048]{1,0:T(8,128)(2,1)} %copy-done.7, bf16[1024,1024]{1,0:T(8,128)(2,1)} %copy-done.10), kind=kOutput, calls=%fused_computation.2 | convolution fusion | flops 4297064448 | bytes 10485760 | tf_op jit(solution)/shard_map/dot_general | solution.py:40
  536.9 9.3 %collective-permute-done.47 = bf16[128,2048]{1,0:T(8,128)(2,1)} collective-permute-done((bf16[128,2048]{1,0:T(8,128)(2,1)}, bf16[128,2048]{1,0:T(8,128)(2,1)}, u32[]{:S(2)}, u32[]{:S(2)}) %collective-permute-start.47) | collective-permute-done | bytes 524320 | tf_op jit(solution)/shard_map/ppermute | solution.py:385
  548.2 13.3 %collective-permute-done.48 = bf16[128,2048]{1,0:T(8,128)(2,1)S(1)} collective-permute-done((bf16[128,2048]{1,0:T(8,128)(2,1)S(1)}, bf16[128,2048]{1,0:T(8,128)(2,1)S(1)}, u32[]{:S(2)}, u32[]{:S(2)}) %collective-permute-start.48) | collective-permute-done | bytes 524320 | tf_op jit(solution)/shard_map/ppermute | solution.py:385
  563.5 6.6 convolution_convert_fusion.5
  570.9 5.8 all-to-all-start.4
  576.9 9.5 %convolution_convert_fusion.1 = bf16[2048,1024]{1,0:T(8,128)(2,1)} fusion(bf16[1024,2048]{1,0:T(8,128)(2,1)} %copy-done.7, bf16[1024,1024]{1,0:T(8,128)(2,1)} %copy-done.11), kind=kOutput, calls=%fused_computation.1 | convolution fusion | flops 4297064448 | bytes 10485760 | tf_op jit(solution)/shard_map/dot_general | solution.py:40
  596.0 10.5 %shard_map.255 = (f32[1024,256]{1,0:T(8,128)S(1)}, f32[1024,256]{1,0:T(8,128)S(1)}, bf16[1024,256]{1,0:T(8,128)(2,1)S(1)}, f32[2,1024,1]{2,1,0:T(8,128)S(1)}, f32[2,1024,1]{2,1,0:T(8,128)S(1)}) custom-call(bf16[1024,256]{1,0:T(8,128)(2,1)S(1)} %copy-done.34, bf16[1024,256]{1,0:T(8,128)(2,1)S(1)} %copy-done.36, bf16[1024,256]{1,0:T(8,128)(2,1)S(1)} %copy-done.38, ...), custom_call_target="tpu_custom_call" | custom-call | flops 1879048192 | bytes 6291456 | tf_op jit(solution)/shard_map/pallas_call | solution.py:241
  618.3 20.9 %collective-permute-done.49 = f32[2,1024]{0,1:T(8,128)S(1)} collective-permute-done((f32[2,1024]{0,1:T(8,128)}, f32[2,1024]{0,1:T(8,128)S(1)}, u32[]{:S(2)}, u32[]{:S(2)}) %collective-permute-start.49) | collective-permute-done | bytes 8224 | tf_op jit(solution)/shard_map/ppermute | solution.py:450
  642.0 10.7 %collective-permute-done.50 = f32[2,1024]{0,1:T(8,128)S(1)} collective-permute-done((f32[2,1024]{0,1:T(8,128)S(1)}, f32[2,1024]{0,1:T(8,128)S(1)}, u32[]{:S(2)}, u32[]{:S(2)}) %collective-permute-start.50) | collective-permute-done | bytes 8224 | tf_op jit(solution)/shard_map/ppermute | solution.py:453
  668.6 10.9 %collective-permute-done.51 = f32[2,1024]{0,1:T(8,128)} collective-permute-done((f32[2,1024]{0,1:T(8,128)}, f32[2,1024]{0,1:T(8,128)}, u32[]{:S(2)}, u32[]{:S(2)}) %collective-permute-start.51) | collective-permute-done | bytes 8224 | tf_op jit(solution)/shard_map/ppermute | solution.py:453
  683.2 5.8 convolution_convert_fusion.3
  693.1 6.6 all-to-all-start.6
  717.9 20.0 %collective-permute-done.55 = bf16[128,2048]{1,0:T(8,128)(2,1)} collective-permute-done((bf16[128,2048]{1,0:T(8,128)(2,1)}, bf16[128,2048]{1,0:T(8,128)(2,1)}, u32[]{:S(2)}, u32[]{:S(2)}) %collective-permute-start.55) | collective-permute-done | bytes 524320 | tf_op jit(solution)/shard_map/ppermute | solution.py:420
  740.5 5.9 all-to-all-start.7
  756.4 28.9 %collective-permute-done.66 = bf16[128,2048]{1,0:T(8,128)(2,1)} collective-permute-done((bf16[128,2048]{1,0:T(8,128)(2,1)S(1)}, bf16[128,2048]{1,0:T(8,128)(2,1)}, u32[]{:S(2)}, u32[]{:S(2)}) %collective-permute-start.66) | collective-permute-done | bytes 524320 | tf_op jit(solution)/shard_map/ppermute | solution.py:385
  792.5 8.0 all-to-all-start.8
  800.5 8.0 collective-permute-done.67
  833.6 6.2 collective-permute-done.57
  842.9 10.3 %all-to-all-done.5 = bf16[8,64,768]{2,1,0:T(8,128)(2,1)} async-done(((bf16[8,64,768]{2,1,0:T(8,128)(2,1)}), bf16[8,64,768]{2,1,0:T(8,128)(2,1)}, u32[]{:S(2)}, u32[]{:S(2)}) %all-to-all-start.5) | async-done | bytes 786464 | tf_op jit(solution)/shard_map/all_to_all | solution.py:80
  853.2 9.3 %all-to-all-start.9 = ((bf16[8,64,1024]{2,1,0:T(8,128)(2,1)}), bf16[8,64,1024]{2,1,0:T(8,128)(2,1)}, u32[]{:S(2)}, u32[]{:S(2)}) async-start(bf16[8,64,1024]{2,1,0:T(8,128)(2,1)} %bitcast.302), calls=%async_computation.12 | async-start | bytes 2097152 | tf_op jit(solution)/shard_map/all_to_all | solution.py:80
  870.8 30.2 %collective-permute-done.70 = bf16[64,2048]{1,0:T(8,128)(2,1)S(1)} collective-permute-done((bf16[64,2048]{1,0:T(8,128)(2,1)S(1)}, bf16[64,2048]{1,0:T(8,128)(2,1)S(1)}, u32[]{:S(2)}, u32[]{:S(2)}) %collective-permute-start.70) | collective-permute-done | bytes 262176 | tf_op jit(solution)/shard_map/ppermute | solution.py:600
  (526 shorter events, 343.9 us)
Async XLA Ops:
  7.2 298.7 %all-gather.3.cloned.1.call-start = ((), (), s32[]{:S(2)}) async-start(), calls=%async_computation.13 | async-start | bytes 8650752 | tf_op jit(solution)/shard_map/all_gather | solution.py:484
  16.3 51.1 %all-to-all-start = ((bf16[8,64,768]{2,1,0:T(8,128)(2,1)}), bf16[8,64,768]{2,1,0:T(8,128)(2,1)}, u32[]{:S(2)}, u32[]{:S(2)}) async-start(bf16[8,64,768]{2,1,0:T(8,128)(2,1)} %reshape.260), calls=%async_computation | async-start | bytes 1572864 | tf_op jit(solution)/shard_map/all_to_all | solution.py:80
  21.9 45.5 %collective-permute-start.1 = (bf16[128,2048]{1,0:T(8,128)(2,1)S(1)}, bf16[128,2048]{1,0:T(8,128)(2,1)}, u32[]{:S(2)}, u32[]{:S(2)}) collective-permute-start(bf16[128,2048]{1,0:T(8,128)(2,1)S(1)} %bitcast.281), channel_id=1, source_target_pairs={{0,2},{2,6},{6,4},{4,0},{1,3},{3,7},{7,5},{5,1},{8,10},{10,14},{14... | collective-permute-start | bytes 1572872 | tf_op jit(solution)/shard_map/ppermute | solution.py:385
  67.4 28.2 %collective-permute-start.3 = (bf16[128,2048]{1,0:T(8,128)(2,1)}, bf16[128,2048]{1,0:T(8,128)(2,1)S(1)}, u32[]{:S(2)}, u32[]{:S(2)}) collective-permute-start(bf16[128,2048]{1,0:T(8,128)(2,1)} %collective-permute-done.1), channel_id=1, source_target_pairs={{0,2},{2,6},{6,4},{4,0},{1,3},{3,7},{7,5},{5,1},{8,10},{10,14},{14... | collective-permute-start | bytes 1572872 | tf_op jit(solution)/shard_map/ppermute | solution.py:385
  118.3 78.1 %all-to-all-start.1 = ((bf16[8,3,64,1024]{3,2,1,0:T(8,128)(2,1)}), bf16[8,3,64,1024]{3,2,1,0:T(8,128)(2,1)}, u32[]{:S(2)}, u32[]{:S(2)}) async-start(bf16[8,3,64,1024]{3,2,1,0:T(8,128)(2,1)} %copy.305), calls=%async_computation.1 | async-start | bytes 6291456 | tf_op jit(solution)/shard_map/all_to_all | solution.py:80
  127.5 212.0 %all-gather.5.cloned.1.call-start = ((), (), s32[]{:S(2)}) async-start(), calls=%async_computation.14 | async-start | bytes 5242880 | tf_op jit(solution)/shard_map/all_gather | solution.py:510
  142.1 22.0 %collective-permute-start.7 = (bf16[512,768]{1,0:T(8,128)(2,1)}, bf16[512,768]{1,0:T(8,128)(2,1)S(1)}, u32[]{:S(2)}, u32[]{:S(2)}) collective-permute-start(bf16[512,768]{1,0:T(8,128)(2,1)} %bitcast.7), channel_id=1, source_target_pairs={{0,8},{8,0},{1,9},{9,1},{2,10},{10,2},{3,11},{11,3},{4,12},{12,4},... | collective-permute-start | bytes 2359304 | tf_op jit(solution)/shard_map/ppermute | solution.py:97
  144.0 19.5 %collective-permute-start.8 = (bf16[512,768]{1,0:T(8,128)(2,1)}, bf16[512,768]{1,0:T(8,128)(2,1)S(1)}, u32[]{:S(2)}, u32[]{:S(2)}) collective-permute-start(bf16[512,768]{1,0:T(8,128)(2,1)} %bitcast.7), channel_id=1, source_target_pairs={{0,16},{16,0},{1,17},{17,1},{2,18},{18,2},{3,19},{19,3},{4,20},{20... | collective-permute-start | bytes 2359304 | tf_op jit(solution)/shard_map/ppermute | solution.py:472
  219.5 26.4 %collective-permute-start.12 = (f32[2,1024]{0,1:T(8,128)}, f32[2,1024]{0,1:T(8,128)}, u32[]{:S(2)}, u32[]{:S(2)}) collective-permute-start(f32[2,1024]{0,1:T(8,128)} %add.388), channel_id=1, source_target_pairs={{0,4},{2,6},{4,0},{6,2},{1,5},{3,7},{5,1},{7,3},{8,12},{10,14},{12... | collective-permute-start | bytes 24584 | tf_op jit(solution)/shard_map/ppermute | solution.py:453
  221.8 29.1 %all-to-all-start.2 = ((bf16[32,2,128]{2,1,0:T(2,128)(2,1)}), bf16[32,2,128]{2,1,0:T(2,128)(2,1)S(1)}, u32[]{:S(2)}, u32[]{:S(2)}) async-start(bf16[32,2,128]{2,1,0:T(2,128)(2,1)} %reshape.315), calls=%async_computation.2 | async-start | bytes 32768 | tf_op jit(solution)/shard_map/all_to_all | solution.py:80
  248.0 33.6 %collective-permute-start.19 = (bf16[512,1024]{1,0:T(8,128)(2,1)}, bf16[512,1024]{1,0:T(8,128)(2,1)}, u32[]{:S(2)}, u32[]{:S(2)}) collective-permute-start(bf16[512,1024]{1,0:T(8,128)(2,1)} %bitcast.272), channel_id=1, source_target_pairs={{0,1},{1,0},{2,3},{3,2},{4,5},{5,4},{6,7},{7,6},{8,9},{9,8},{10,11... | collective-permute-start | bytes 3145736 | tf_op jit(solution)/shard_map/ppermute | solution.py:433
  249.4 35.2 %collective-permute-start.18 = (bf16[512,1024]{1,0:T(8,128)(2,1)}, bf16[512,1024]{1,0:T(8,128)(2,1)}, u32[]{:S(2)}, u32[]{:S(2)}) collective-permute-start(bf16[512,1024]{1,0:T(8,128)(2,1)} %bitcast.273), channel_id=1, source_target_pairs={{0,16},{16,0},{1,17},{17,1},{2,18},{18,2},{3,19},{19,3},{4,20},{20... | collective-permute-start | bytes 3145736 | tf_op jit(solution)/shard_map/ppermute | solution.py:433
  250.6 48.0 %collective-permute-start.14 = (bf16[512,1024]{1,0:T(8,128)(2,1)}, bf16[512,1024]{1,0:T(8,128)(2,1)}, u32[]{:S(2)}, u32[]{:S(2)}) collective-permute-start(bf16[512,1024]{1,0:T(8,128)(2,1)} %bitcast.269), channel_id=1, source_target_pairs={{0,16},{16,0},{1,17},{17,1},{2,18},{18,2},{3,19},{19,3},{4,20},{20... | collective-permute-start | bytes 3145736 | tf_op jit(solution)/shard_map/ppermute | solution.py:433
  250.9 52.0 %collective-permute-start.15 = (bf16[512,1024]{1,0:T(8,128)(2,1)}, bf16[512,1024]{1,0:T(8,128)(2,1)}, u32[]{:S(2)}, u32[]{:S(2)}) collective-permute-start(bf16[512,1024]{1,0:T(8,128)(2,1)} %bitcast.270), channel_id=1, source_target_pairs={{0,1},{1,0},{2,3},{3,2},{4,5},{5,4},{6,7},{7,6},{8,9},{9,8},{10,11... | collective-permute-start | bytes 3145736 | tf_op jit(solution)/shard_map/ppermute | solution.py:433
  268.8 37.1 %all-to-all-start.3 = ((bf16[8,128,256]{1,2,0:T(8,128)(2,1)}), bf16[8,128,256]{1,2,0:T(8,128)(2,1)}, u32[]{:S(2)}, u32[]{:S(2)}) async-start(bf16[8,128,256]{1,2,0:T(8,128)(2,1)} %copy.311), calls=%async_computation.3 | async-start | bytes 1048576 | tf_op jit(solution)/shard_map/all_to_all | solution.py:80
  274.5 465.9 %reduce-scatter.6.cloned.1.call-start = ((), (), s32[]{:S(2)}) async-start(), calls=%async_computation.16 | async-start | bytes 5242880 | tf_op jit(solution)/shard_map/reduce_scatter | solution.py:551
  283.5 38.7 %collective-permute-start.21 = (bf16[256,1024]{1,0:T(8,128)(2,1)}, bf16[256,1024]{1,0:T(8,128)(2,1)}, u32[]{:S(2)}, u32[]{:S(2)}) collective-permute-start(bf16[256,1024]{1,0:T(8,128)(2,1)} %slice.120), channel_id=1, source_target_pairs={{0,16},{16,0},{1,17},{17,1},{2,18},{18,2},{3,19},{19,3},{4,20},{20... | collective-permute-start | bytes 1572872 | tf_op jit(solution)/shard_map/ppermute | solution.py:436
  286.5 34.2 %collective-permute-start.20 = (bf16[256,1024]{1,0:T(8,128)(2,1)}, bf16[256,1024]{1,0:T(8,128)(2,1)}, u32[]{:S(2)}, u32[]{:S(2)}) collective-permute-start(bf16[256,1024]{1,0:T(8,128)(2,1)} %slice.119), channel_id=1, source_target_pairs={{0,1},{1,0},{2,3},{3,2},{4,5},{5,4},{6,7},{7,6},{8,9},{9,8},{10,11... | collective-permute-start | bytes 1572872 | tf_op jit(solution)/shard_map/ppermute | solution.py:435
  300.4 26.3 %collective-permute-start.16 = (bf16[256,1024]{1,0:T(8,128)(2,1)}, bf16[256,1024]{1,0:T(8,128)(2,1)}, u32[]{:S(2)}, u32[]{:S(2)}) collective-permute-start(bf16[256,1024]{1,0:T(8,128)(2,1)} %slice.117), channel_id=1, source_target_pairs={{0,1},{1,0},{2,3},{3,2},{4,5},{5,4},{6,7},{7,6},{8,9},{9,8},{10,11... | collective-permute-start | bytes 1572872 | tf_op jit(solution)/shard_map/ppermute | solution.py:435
  304.7 31.6 %collective-permute-start.17 = (bf16[256,1024]{1,0:T(8,128)(2,1)}, bf16[256,1024]{1,0:T(8,128)(2,1)}, u32[]{:S(2)}, u32[]{:S(2)}) collective-permute-start(bf16[256,1024]{1,0:T(8,128)(2,1)} %slice.118), channel_id=1, source_target_pairs={{0,16},{16,0},{1,17},{17,1},{2,18},{18,2},{3,19},{19,3},{4,20},{20... | collective-permute-start | bytes 1572872 | tf_op jit(solution)/shard_map/ppermute | solution.py:436
  312.1 27.4 %collective-permute-start.13 = (bf16[128,2048]{1,0:T(8,128)(2,1)}, bf16[128,2048]{1,0:T(8,128)(2,1)}, u32[]{:S(2)}, u32[]{:S(2)}) collective-permute-start(bf16[128,2048]{1,0:T(8,128)(2,1)} %fusion.15.part), channel_id=1, source_target_pairs={{0,8},{8,0},{1,9},{9,1},{2,10},{10,2},{3,11},{11,3},{4,12},{12,4},... | collective-permute-start | bytes 1572872 | tf_op jit(solution)/shard_map/ppermute | solution.py:97
  339.5 19.5 %collective-permute-start.24 = (bf16[128,2048]{1,0:T(8,128)(2,1)}, bf16[128,2048]{1,0:T(8,128)(2,1)}, u32[]{:S(2)}, u32[]{:S(2)}) collective-permute-start(bf16[128,2048]{1,0:T(8,128)(2,1)} %collective-permute-done.23.part), channel_id=1, source_target_pairs={{0,2},{2,6},{6,4},{4,0},{1,3},{3,7},{7,5},{5,1},{8,10},{10,14},{14... | collective-permute-start | bytes 1572872 | tf_op jit(solution)/shard_map/ppermute | solution.py:385
  401.7 22.3 %collective-permute-start.22 = (bf16[128,2048]{1,0:T(8,128)(2,1)}, bf16[128,2048]{1,0:T(8,128)(2,1)}, u32[]{:S(2)}, u32[]{:S(2)}) collective-permute-start(bf16[128,2048]{1,0:T(8,128)(2,1)} %get-tuple-element.102), channel_id=1, source_target_pairs={{0,8},{8,0},{1,9},{9,1},{2,10},{10,2},{3,11},{11,3},{4,12},{12,4},... | collective-permute-start | bytes 1572872 | tf_op jit(solution)/shard_map/ppermute | solution.py:97
  449.4 22.7 %collective-permute-start.38 = (bf16[128,2048]{1,0:T(8,128)(2,1)S(1)}, bf16[128,2048]{1,0:T(8,128)(2,1)S(1)}, u32[]{:S(2)}, u32[]{:S(2)}) collective-permute-start(bf16[128,2048]{1,0:T(8,128)(2,1)S(1)} %collective-permute-done.37.part), channel_id=1, source_target_pairs={{0,2},{2,6},{6,4},{4,0},{1,3},{3,7},{7,5},{5,1},{8,10},{10,14},{14... | collective-permute-start | bytes 1572872 | tf_op jit(solution)/shard_map/ppermute | solution.py:385
  520.8 271.7 %reduce-scatter.4.cloned.1.call-start = ((), (), s32[]{:S(2)}) async-start(), calls=%async_computation.15 | async-start | bytes 5242880 | tf_op jit(solution)/shard_map/reduce_scatter | solution.py:551
  576.8 266.1 %reduce-scatter.8.cloned.1.call-start = ((), (), s32[]{:S(2)}) async-start(), calls=%async_computation.17 | async-start | bytes 5242880 | tf_op jit(solution)/shard_map/reduce_scatter | solution.py:551
  615.1 24.1 %collective-permute-start.49 = (f32[2,1024]{0,1:T(8,128)}, f32[2,1024]{0,1:T(8,128)S(1)}, u32[]{:S(2)}, u32[]{:S(2)}) collective-permute-start(f32[2,1024]{0,1:T(8,128)} %copy.329), channel_id=1, source_target_pairs={{0,1},{1,0},{2,3},{3,2},{4,5},{5,4},{6,7},{7,6},{8,9},{9,8},{10,11... | collective-permute-start | bytes 24584 | tf_op jit(solution)/shard_map/ppermute | solution.py:450
  653.5 26.0 %collective-permute-start.51 = (f32[2,1024]{0,1:T(8,128)}, f32[2,1024]{0,1:T(8,128)}, u32[]{:S(2)}, u32[]{:S(2)}) collective-permute-start(f32[2,1024]{0,1:T(8,128)} %add.416), channel_id=1, source_target_pairs={{0,4},{2,6},{4,0},{6,2},{1,5},{3,7},{5,1},{7,3},{8,12},{10,14},{12... | collective-permute-start | bytes 24584 | tf_op jit(solution)/shard_map/ppermute | solution.py:453
  681.3 65.1 %collective-permute-start.61 = (bf16[128,2048]{1,0:T(8,128)(2,1)}, bf16[128,2048]{1,0:T(8,128)(2,1)}, u32[]{:S(2)}, u32[]{:S(2)}) collective-permute-start(bf16[128,2048]{1,0:T(8,128)(2,1)} %copy-done.64), channel_id=1, source_target_pairs={{0,1},{1,0},{2,3},{3,2},{4,5},{5,4},{6,7},{7,6},{8,9},{9,8},{10,11... | collective-permute-start | bytes 1572872 | tf_op jit(solution)/shard_map/ppermute | solution.py:390
  681.6 35.0 %collective-permute-start.62 = (bf16[128,2048]{1,0:T(8,128)(2,1)}, bf16[128,2048]{1,0:T(8,128)(2,1)}, u32[]{:S(2)}, u32[]{:S(2)}) collective-permute-start(bf16[128,2048]{1,0:T(8,128)(2,1)} %copy-done.64), channel_id=1, source_target_pairs={{0,2},{2,6},{6,4},{4,0},{1,3},{3,7},{7,5},{5,1},{8,10},{10,14},{14... | collective-permute-start | bytes 1572872 | tf_op jit(solution)/shard_map/ppermute | solution.py:385
  693.1 22.2 %all-to-all-start.6 = ((f32[32,1,256]{2,1,0:T(1,128)}), f32[32,1,256]{2,1,0:T(1,128)S(1)}, u32[]{:S(2)}, u32[]{:S(2)}) async-start(f32[32,1,256]{2,1,0:T(1,128)} %reshape.317), calls=%async_computation.6 | async-start | bytes 65536 | tf_op jit(solution)/shard_map/all_to_all | solution.py:80
  702.3 83.3 %collective-permute-start.59 = (bf16[1024,768]{1,0:T(8,128)(2,1)}, bf16[1024,768]{1,0:T(8,128)(2,1)}, u32[]{:S(2)}, u32[]{:S(2)}) collective-permute-start(bf16[1024,768]{1,0:T(8,128)(2,1)} %pad_maximum_fusion.1), channel_id=1, source_target_pairs={{0,8},{8,0},{1,9},{9,1},{2,10},{10,2},{3,11},{11,3},{4,12},{12,4},... | collective-permute-start | bytes 4718600 | tf_op jit(solution)/shard_map/ppermute | solution.py:97
  706.6 160.7 %collective-permute-start.52 = (bf16[128,2048]{1,0:T(8,128)(2,1)}, bf16[128,2048]{1,0:T(8,128)(2,1)}, u32[]{:S(2)}, u32[]{:S(2)}) collective-permute-start(bf16[128,2048]{1,0:T(8,128)(2,1)} %fusion.10), channel_id=1, source_target_pairs={{0,1},{1,0},{2,3},{3,2},{4,5},{5,4},{6,7},{7,6},{8,9},{9,8},{10,11... | collective-permute-start | bytes 1572872 | tf_op jit(solution)/shard_map/ppermute | solution.py:420
  709.8 28.1 %collective-permute-start.55 = (bf16[128,2048]{1,0:T(8,128)(2,1)}, bf16[128,2048]{1,0:T(8,128)(2,1)}, u32[]{:S(2)}, u32[]{:S(2)}) collective-permute-start(bf16[128,2048]{1,0:T(8,128)(2,1)} %fusion.13), channel_id=1, source_target_pairs={{0,1},{1,0},{2,3},{3,2},{4,5},{5,4},{6,7},{7,6},{8,9},{9,8},{10,11... | collective-permute-start | bytes 1572872 | tf_op jit(solution)/shard_map/ppermute | solution.py:420
  716.6 37.7 %collective-permute-start.63 = (bf16[128,2048]{1,0:T(8,128)(2,1)}, bf16[128,2048]{1,0:T(8,128)(2,1)S(1)}, u32[]{:S(2)}, u32[]{:S(2)}) collective-permute-start(bf16[128,2048]{1,0:T(8,128)(2,1)} %collective-permute-done.62), channel_id=1, source_target_pairs={{0,1},{1,0},{2,3},{3,2},{4,5},{5,4},{6,7},{7,6},{8,9},{9,8},{10,11... | collective-permute-start | bytes 1572872 | tf_op jit(solution)/shard_map/ppermute | solution.py:390
  740.5 52.0 %all-to-all-start.7 = ((bf16[8,64,1024]{2,1,0:T(8,128)(2,1)}), bf16[8,64,1024]{2,1,0:T(8,128)(2,1)S(1)}, u32[]{:S(2)}, u32[]{:S(2)}) async-start(bf16[8,64,1024]{2,1,0:T(8,128)(2,1)} %bitcast.301), calls=%async_computation.9 | async-start | bytes 2097152 | tf_op jit(solution)/shard_map/all_to_all | solution.py:80
  746.4 87.2 %collective-permute-start.53 = (bf16[128,2048]{1,0:T(8,128)(2,1)}, bf16[128,2048]{1,0:T(8,128)(2,1)}, u32[]{:S(2)}, u32[]{:S(2)}) collective-permute-start(bf16[128,2048]{1,0:T(8,128)(2,1)} %fusion.11), channel_id=1, source_target_pairs={{0,1},{1,0},{2,3},{3,2},{4,5},{5,4},{6,7},{7,6},{8,9},{9,8},{10,11... | collective-permute-start | bytes 1572872 | tf_op jit(solution)/shard_map/ppermute | solution.py:420
  752.4 32.9 %collective-permute-start.66 = (bf16[128,2048]{1,0:T(8,128)(2,1)S(1)}, bf16[128,2048]{1,0:T(8,128)(2,1)}, u32[]{:S(2)}, u32[]{:S(2)}) collective-permute-start(bf16[128,2048]{1,0:T(8,128)(2,1)S(1)} %collective-permute-done.64), channel_id=1, source_target_pairs={{0,2},{2,6},{6,4},{4,0},{1,3},{3,7},{7,5},{5,1},{8,10},{10,14},{14... | collective-permute-start | bytes 1572872 | tf_op jit(solution)/shard_map/ppermute | solution.py:385
  754.3 35.4 %collective-permute-start.65 = (bf16[128,2048]{1,0:T(8,128)(2,1)S(1)}, bf16[128,2048]{1,0:T(8,128)(2,1)S(1)}, u32[]{:S(2)}, u32[]{:S(2)}) collective-permute-start(bf16[128,2048]{1,0:T(8,128)(2,1)S(1)} %collective-permute-done.64), channel_id=1, source_target_pairs={{0,1},{1,0},{2,3},{3,2},{4,5},{5,4},{6,7},{7,6},{8,9},{9,8},{10,11... | collective-permute-start | bytes 1572872 | tf_op jit(solution)/shard_map/ppermute | solution.py:390
  785.4 30.8 %collective-permute-start.54 = (bf16[128,2048]{1,0:T(8,128)(2,1)}, bf16[128,2048]{1,0:T(8,128)(2,1)}, u32[]{:S(2)}, u32[]{:S(2)}) collective-permute-start(bf16[128,2048]{1,0:T(8,128)(2,1)} %fusion.12), channel_id=1, source_target_pairs={{0,1},{1,0},{2,3},{3,2},{4,5},{5,4},{6,7},{7,6},{8,9},{9,8},{10,11... | collective-permute-start | bytes 1572872 | tf_op jit(solution)/shard_map/ppermute | solution.py:420
  785.6 22.8 %collective-permute-start.67 = (bf16[128,2048]{1,0:T(8,128)(2,1)}, bf16[128,2048]{1,0:T(8,128)(2,1)}, u32[]{:S(2)}, u32[]{:S(2)}) collective-permute-start(bf16[128,2048]{1,0:T(8,128)(2,1)} %collective-permute-done.66), channel_id=1, source_target_pairs={{0,1},{1,0},{2,3},{3,2},{4,5},{5,4},{6,7},{7,6},{8,9},{9,8},{10,11... | collective-permute-start | bytes 1572872 | tf_op jit(solution)/shard_map/ppermute | solution.py:390
  789.7 29.5 %collective-permute-start.56 = (bf16[128,2048]{1,0:T(8,128)(2,1)}, bf16[128,2048]{1,0:T(8,128)(2,1)}, u32[]{:S(2)}, u32[]{:S(2)}) collective-permute-start(bf16[128,2048]{1,0:T(8,128)(2,1)} %fusion), channel_id=1, source_target_pairs={{0,2},{2,6},{6,4},{4,0},{1,3},{3,7},{7,5},{5,1},{8,10},{10,14},{14... | collective-permute-start | bytes 1572872 | tf_op jit(solution)/shard_map/ppermute | solution.py:385
  792.5 33.7 %all-to-all-start.8 = ((bf16[8,64,1024]{2,1,0:T(8,128)(2,1)}), bf16[8,64,1024]{2,1,0:T(8,128)(2,1)}, u32[]{:S(2)}, u32[]{:S(2)}) async-start(bf16[8,64,1024]{2,1,0:T(8,128)(2,1)} %bitcast.300), calls=%async_computation.10 | async-start | bytes 2097152 | tf_op jit(solution)/shard_map/all_to_all | solution.py:80
  826.2 27.0 %all-to-all-start.5 = ((bf16[8,64,768]{2,1,0:T(8,128)(2,1)}), bf16[8,64,768]{2,1,0:T(8,128)(2,1)}, u32[]{:S(2)}, u32[]{:S(2)}) async-start(bf16[8,64,768]{2,1,0:T(8,128)(2,1)} %bitcast.82), calls=%async_computation.5 | async-start | bytes 1572864 | tf_op jit(solution)/shard_map/all_to_all | solution.py:80
  832.0 30.6 %collective-permute-start.69 = (bf16[64,2048]{1,0:T(8,128)(2,1)S(1)}, bf16[64,2048]{1,0:T(8,128)(2,1)}, u32[]{:S(2)}, u32[]{:S(2)}) collective-permute-start(bf16[64,2048]{1,0:T(8,128)(2,1)S(1)} %constant_dynamic-slice_fusion), channel_id=1, source_target_pairs={{0,16},{16,0},{1,17},{17,1},{2,18},{18,2},{3,19},{19,3},{4,20},{20... | collective-permute-start | bytes 786440 | tf_op jit(solution)/shard_map/ppermute | solution.py:570
  842.4 26.0 %collective-permute-start.58 = (bf16[128,2048]{1,0:T(8,128)(2,1)}, bf16[128,2048]{1,0:T(8,128)(2,1)}, u32[]{:S(2)}, u32[]{:S(2)}) collective-permute-start(bf16[128,2048]{1,0:T(8,128)(2,1)} %fusion.4), channel_id=1, source_target_pairs={{0,2},{2,6},{6,4},{4,0},{1,3},{3,7},{7,5},{5,1},{8,10},{10,14},{14... | collective-permute-start | bytes 1572872 | tf_op jit(solution)/shard_map/ppermute | solution.py:385
  853.2 63.6 %all-to-all-start.9 = ((bf16[8,64,1024]{2,1,0:T(8,128)(2,1)}), bf16[8,64,1024]{2,1,0:T(8,128)(2,1)}, u32[]{:S(2)}, u32[]{:S(2)}) async-start(bf16[8,64,1024]{2,1,0:T(8,128)(2,1)} %bitcast.302), calls=%async_computation.12 | async-start | bytes 2097152 | tf_op jit(solution)/shard_map/all_to_all | solution.py:80
  863.7 37.3 %collective-permute-start.70 = (bf16[64,2048]{1,0:T(8,128)(2,1)S(1)}, bf16[64,2048]{1,0:T(8,128)(2,1)S(1)}, u32[]{:S(2)}, u32[]{:S(2)}) collective-permute-start(bf16[64,2048]{1,0:T(8,128)(2,1)S(1)} %add_convert_fusion.6), channel_id=1, source_target_pairs={{0,0},{1,4},{2,8},{3,12},{4,16},{5,20},{6,24},{7,28},{8,1},{9,5},{... | collective-permute-start | bytes 786440 | tf_op jit(solution)/shard_map/ppermute | solution.py:600
  (130 other events, 1338.9 us)
Sparse Core Ops, SparseCore 0:
  11.0 107.6 all-gather.2
  200.2 56.2 all-gather.4
  520.9 52.1 reduce-scatter.5
  576.2 63.4 reduce-scatter.3
  655.2 67.0 reduce-scatter.7

commit v3 on v2

--- a/solution.py
+++ b/solution.py
@@ -398,12 +398,25 @@
             chunks.append((held, lax.ppermute(held, "y", SWAP)))
             if step < n_z - 1:
                 held = ring_send(tie(held, *gates(step, held)))
-        whole = jnp.zeros((n_seq * tok_count, own.shape[1]), own.dtype)
-        for step, (mine, other) in enumerate(chunks):
-            first = behind[step, z_at] * n_y * tok_count
-            whole = lax.dynamic_update_slice(whole, mine, (first + y_at * tok_count, 0))
-            whole = lax.dynamic_update_slice(whole, other, (first + (1 - y_at) * tok_count, 0))
-        return whole, held
+
+        def whole(first, count):
+            out = jnp.zeros((n_seq * count, own.shape[1]), own.dtype)
+            for step, pair in enumerate(chunks):
+                for at_y, part in zip((y_at, 1 - y_at), pair):
+                    at = (behind[step, z_at] * n_y + at_y) * count
+                    part = part[first : first + count]
+                    out = lax.dynamic_update_slice(out, part, (at, 0))
+            return out
+
+        return whole(0, tok_count), whole(tok_count, own.shape[0] - tok_count), held
+
+    def dp_gather(mine):
+        out = jnp.zeros((n_x, n_core) + mine.shape, mine.dtype)
+        for at_x, part in ((x_at, mine), (1 - x_at, lax.ppermute(mine, "x", SWAP))):
+            for at_core, block in ((core_at, part), (1 - core_at, core_swap(part))):
+                block = block[None, None]
+                out = lax.dynamic_update_slice(out, block, (at_x, at_core, 0, 0))
+        return out.reshape((n_dp * mine.shape[0], mine.shape[1]))
 
     def seq_order(array_in):
         chunks = []
@@ -429,30 +442,24 @@
         mine = exchange(tie(blocks.transpose(2, 0, 1, 3), *earlier), FEED)
         return [mine[:, at].reshape(n_feed * own_rows, own_feed) for at in range(len(mats))]
 
-    def rest_gather(mine, late, later):
-        over_x, over_y = lax.ppermute(mine, "x", SWAP), lax.ppermute(mine, "y", SWAP)
-        half = mine.shape[0] // 2
-        corner_x = lax.ppermute(tie(over_x[:half], late), "y", SWAP)
-        corner_y = lax.ppermute(tie(over_y[half:], late), "x", SWAP)
+    def rest_send(mine):
+        return mine, lax.ppermute(mine, "y", SWAP), lax.ppermute(mine, "x", SWAP)
+
+    def rest_gather(sent, corner, later):
+        mine, over_y, over_x = sent
         mine = tie(mine, later)
         whole = jnp.zeros((n_x, n_y) + mine.shape, BF16)
-        for at_x, at_y, first, part in (
-            (x_at, y_at, 0, mine),
-            (1 - x_at, y_at, 0, over_x),
-            (x_at, 1 - y_at, 0, over_y),
-            (1 - x_at, 1 - y_at, 0, corner_x),
-            (1 - x_at, 1 - y_at, half, corner_y),
+        for at_x, at_y, part in (
+            (x_at, y_at, mine),
+            (1 - x_at, y_at, over_x),
+            (x_at, 1 - y_at, over_y),
+            (1 - x_at, 1 - y_at, corner),
         ):
-            whole = lax.dynamic_update_slice(whole, part[None, None], (at_x, at_y, first, 0))
+            whole = lax.dynamic_update_slice(whole, part[None, None], (at_x, at_y, 0, 0))
         return whole.reshape(model_width, own_feed)
 
     def seq_total(term):
-        term = term + lax.ppermute(term, "y", SWAP)
-        hop = 1
-        while hop < n_z:
-            term = term + lax.ppermute(term, "z", [(z, z ^ hop) for z in range(n_z)])
-            hop *= 2
-        return term
+        return jnp.sum(spread(term, SEQ), axis=0)
 
     def to_feed_order(array_in):
         lead = array_in.shape[:-1]
@@ -464,31 +471,25 @@
         parts = array_in.reshape((-1, n_x, n_y, n_z, n_core, own_rows))
         return parts.transpose(0, 1, 4, 3, 2, 5).reshape(lead + (model_width,))
 
-    w_heads = jnp.stack([w_query, w_key, w_value])
-    w_heads = w_heads.reshape(3, own_rows, n_seq, own_width).transpose(2, 1, 0, 3)
-    w_heads = exchange(w_heads.reshape(n_seq, own_rows, 3 * own_width), SEQ)
-    w_mine = w_heads.reshape(n_seq * own_rows, 3 * own_width)
-
-    w_over = lax.ppermute(w_mine, "x", SWAP)
-    w_heads = jnp.zeros((n_x, n_core) + w_mine.shape, BF16)
-    for at_x, part in ((x_at, w_mine), (1 - x_at, w_over)):
-        w_heads = lax.dynamic_update_slice(w_heads, part[None, None], (at_x, core_at, 0, 0))
-        w_heads = lax.dynamic_update_slice(
-            w_heads, core_swap(part)[None, None], (at_x, 1 - core_at, 0, 0)
-        )
-    w_heads = w_heads.reshape(model_width, 3 * own_width)
-    def gates(step, held):
-        return (w_mine,) if step == 1 else ()
-
-    x_row, x_last = row_gather(tokens, gates)
-    full_o = lax.all_gather(to_feed_order(w_out), ALL, axis=0, tiled=True)
-    moved = feed_weights([w_gate, w_up, w_down.T], (x_last,))
-
-    gains = spread(tie(jnp.stack([gain_query, gain_key, gain_attn, gain_ffn]), *moved), ALL)
+    gains = spread(jnp.stack([gain_query, gain_key, gain_attn, gain_ffn]), ALL)
     gains = gains.transpose(1, 0, 2).reshape(4, model_width).astype(F32)
     my_gq = lax.dynamic_slice_in_dim(gains[0:1], seq_at * own_width, own_width, 1)
     my_gk = lax.dynamic_slice_in_dim(gains[1:2], seq_at * own_width, own_width, 1)
     gain_a, gain_f = to_feed_order(gains[2]), to_feed_order(gains[3])
+
+    w_heads = jnp.stack([w_query, w_key, w_value])
+    w_heads = w_heads.reshape(3, own_rows, n_seq, own_width).transpose(2, 1, 0, 3)
+    w_heads = w_heads.reshape(n_seq, own_rows, 3 * own_width)
+    w_heads = exchange(tie(w_heads, gains), SEQ)
+    w_mine = w_heads.reshape(n_seq * own_rows, 3 * own_width)
+
+    w_heads = dp_gather(w_mine)
+    def gates(step, held):
+        return (w_mine,) if step == 1 else ()
+
+    own = jnp.concatenate([tokens, to_feed_order(w_out)])
+    x_row, w_out_mine, x_last = row_gather(own, gates)
+    moved = feed_weights([w_gate, w_up], (x_last,))
 
     qkv = matmul(x_row, w_heads)
     q_lin, k_lin = qkv[:, :own_width], qkv[:, own_width : 2 * own_width]
@@ -501,14 +502,21 @@
     position = jnp.arange(length)
     doc_ids = jnp.sum((position[:, None] >= doc_ends[None, :]).astype(jnp.int32), axis=1)
     docs = (doc_ids[:, None], doc_ids[None, :])
+    w_u = lax.all_gather(moved[1], REST, axis=0, tiled=True)
+    sent_g = rest_send(tie(moved[0], squares))
+    moved += feed_weights([w_down.T], (squares,))
+    sent_d = rest_send(moved[2])
     *saved, attended = attend(qkv, factors, my_gq, my_gk, tables, docs, own_heads)
 
-    att_tok = exchange(attended.reshape(n_seq, tok_count, own_width), SEQ)
+    corner_g = lax.ppermute(sent_g[1], "x", SWAP)
+    att_tok = tie(attended.reshape(n_seq, tok_count, own_width), *sent_g)
+    att_tok = exchange(att_tok, SEQ)
+    corner_d = lax.ppermute(sent_d[1], "x", SWAP)
     att_tok = att_tok.transpose(1, 0, 2).reshape(tok_count, model_width)
-    branch = matmul(att_tok, full_o)
-    w_g = rest_gather(moved[0], attended, branch)
-    w_u = lax.all_gather(moved[1], REST, axis=0, tiled=True)
-    w_d = rest_gather(tie(moved[2], qkv), attended, branch)
+    full_o = dp_gather(w_out_mine)
+    branch = tie(matmul(att_tok, full_o), *sent_d)
+    w_g = rest_gather(sent_g, corner_g, branch)
+    w_d = rest_gather(sent_d, corner_d, branch)
     branch_norm, branch_factor = norm_apply(branch, gain_a)
     hidden = to_feed_order(tokens).astype(F32) + branch_norm
     hidden_low = hidden.astype(BF16)
@@ -590,10 +598,10 @@
         saved, g_att, qkv, my_gq, my_gk, tables, docs, own_heads
     )
     dots = jnp.stack([jnp.sum(dot_q, axis=(0, 2)), jnp.sum(dot_k, axis=(0, 2))])
-    dots = seq_total(dots) / model_width
+    branch_row = seq_gather(grad_branch)
+    dots = seq_total(tie(dots, branch_row)) / model_width
     home_d = feed_home(tie(sum_d, dots))
 
-    branch_row = seq_gather(tie(grad_branch, dots))
     grad_w_out = dot_left_t(seq_order(attended), branch_row).astype(BF16)
     grad_w_out = dp_sum(grad_w_out)
     home = [(d * n_seq + s, s * n_dp + d) for d in range(n_dp) for s in range(n_seq)]

time: 938 us -> 902 us (0.962)
  waiting for transfers between devices: 413 us -> 319 us
  local copies, waits for them, and re-layouts: 167 us -> 200 us
  starting transfers between devices: 122 us -> 133 us
    ppermute x21, waiting for transfers between devices: 217 us -> 147 us  [ring_send(): return lax.ppermute(part, 'z', ring)]
    ppermute x15 -> x8, waiting for transfers between devices: 94.3 us -> 60.3 us  [the longest x4 45.3 us: rest_send(): return (mine, lax.ppermute(mine, 'y', SWAP), lax.ppermute(mine, 'x', SWAP))]
    dynamic_update_slice x22 -> x32, local copies, waits for them, and re-layouts: 19.1 us -> 42.8 us  [the longest x16 21.5 us: whole(): out = lax.dynamic_update_slice(out, part, (at, 0))]
    ppermute x4, waiting for transfers between devices: 20 us -> 0.01 us  [seq_sum(): away = lax.ppermute(pick(part, 1 - y_at).astype(BF16), 'y', SWAP)]
    ppermute x4, waiting for transfers between devices: 8.01 us -> 26.4 us  [seq_gather(): chunks += [held, lax.ppermute(held, 'y', SWAP)]]
    all_to_all x10 -> x13, starting transfers between devices: 68.6 us -> 78 us  [exchange(): lax.all_to_all(array_in, axes, split_axis=0, concat_axis=0, tiled=True)]
    ppermute x20 -> x22, starting transfers between devices: 18.8 us -> 27.3 us  [core_swap(): return lax.ppermute(array_in, 'core', SWAP)]
    all_to_all x10 -> x13, waiting for transfers between devices: 18.1 us -> 26.6 us  [exchange(): lax.all_to_all(array_in, axes, split_axis=0, concat_axis=0, tiled=True)]
  transfers between devices with their start and end apart: 86 -> 83, of which waited for: 43 -> 32; matrix products, arithmetic and copies ran while one was open for 24% -> 30% of each run, Pallas kernels for 8% -> 8%
where the time goes in v3:
time: 902 us; the launch traced here: 887 us
  waiting for transfers between devices  319 us (35%)
  local copies, waits for them, and re-layouts  200 us (22%)
  starting transfers between devices  133 us (15%)
  Pallas kernels  89.2 us (10%)
  other arithmetic  64.2 us (7%)
  matrix products  60.3 us (7%)
  between operations  20.9 us (2%)
    ppermute x21, waiting for transfers between devices, ring_send(): return lax.ppermute(part, 'z', ring)  147 us
    all_to_all x13, starting transfers between devices, exchange(): lax.all_to_all(array_in, axes, split_axis=0, concat_axis=0, tiled=True)  78 us
    unnamed x201, local copies, waits for them, and re-layouts  75.5 us
    pallas_call x8, Pallas kernels, feed_step(): pl.pallas_call(kernel, grid=(feed // step,), in_specs=[part, part] + [pl....  71.4 us
    ppermute x4, waiting for transfers between devices, rest_send(): return (mine, lax.ppermute(mine, 'y', SWAP), lax.ppermute(mine, 'x', SWAP))  45.3 us
    dot_general x5, matrix products, dot_left_t(): lax.dot_general(left_mat, right_mat, (((0,), (0,)), ((), ())), preferred_...  34.5 us
    ppermute x1, waiting for transfers between devices, body(): grad_w_out = lax.ppermute(grad_w_out, ALL, home)  28.2 us
    ppermute x22, starting transfers between devices, core_swap(): return lax.ppermute(array_in, 'core', SWAP)  27.3 us
  transfers between devices with their start and end apart: 83, of which 32 were waited for; matrix products, arithmetic and copies ran while one was open for 30% of the time, Pallas kernels for 8%

profile of v3, /device:TPU:25, one launch (start us, length us, event | category | flops | bytes accessed | tf_op | source)
XLA Modules:
  0.0 887.4 jit_solution(7007001496658987981)
XLA Ops:
  40.0 8.6 all-to-all-done
  48.6 6.7 all-to-all-start.2
  60.6 15.5 %collective-permute-done.3 = bf16[192,2048]{1,0:T(8,128)(2,1)S(1)} collective-permute-done((bf16[192,2048]{1,0:T(8,128)(2,1)}, bf16[192,2048]{1,0:T(8,128)(2,1)S(1)}, u32[]{:S(2)}, u32[]{:S(2)}) %collective-permute-start.3) | collective-permute-done | bytes 786464 | tf_op jit(solution)/shard_map/ppermute | solution.py:385
  80.2 14.4 %collective-permute-done.5 = bf16[192,2048]{1,0:T(8,128)(2,1)S(1)} collective-permute-done((bf16[192,2048]{1,0:T(8,128)(2,1)S(1)}, bf16[192,2048]{1,0:T(8,128)(2,1)S(1)}, u32[]{:S(2)}, u32[]{:S(2)}) %collective-permute-start.5) | collective-permute-done | bytes 786464 | tf_op jit(solution)/shard_map/ppermute | solution.py:385
  97.8 13.4 %collective-permute-done.6 = bf16[192,2048]{1,0:T(8,128)(2,1)S(1)} collective-permute-done((bf16[192,2048]{1,0:T(8,128)(2,1)S(1)}, bf16[192,2048]{1,0:T(8,128)(2,1)S(1)}, u32[]{:S(2)}, u32[]{:S(2)}) %collective-permute-start.6) | collective-permute-done | bytes 786464 | tf_op jit(solution)/shard_map/ppermute | solution.py:398
  112.3 5.3 fusion.19.refs_0_.refs_1_.refs_2_.refs_5_.refs_6_
  118.7 6.2 all-to-all-start.1
  130.6 8.7 all-to-all-start.3
  168.7 17.0 %all-to-all-done.3 = bf16[8,2,64,1024]{3,2,1,0:T(8,128)(2,1)} async-done(((bf16[8,2,64,1024]{3,2,1,0:T(8,128)(2,1)}), bf16[8,2,64,1024]{3,2,1,0:T(8,128)(2,1)}, u32[]{:S(2)}, u32[]{:S(2)}) %all-to-all-start.3) | async-done | bytes 2097184 | tf_op jit(solution)/shard_map/all_to_all | solution.py:80
  185.8 6.8 all-to-all-start.5
  207.3 7.3 shard_map.246
  224.3 11.3 %collective-permute-done.10 = bf16[512,1024]{1,0:T(8,128)(2,1)} collective-permute-done((bf16[512,1024]{1,0:T(8,128)(2,1)}, bf16[512,1024]{1,0:T(8,128)(2,1)}, u32[]{:S(2)}, u32[]{:S(2)}) %collective-permute-start.10) | collective-permute-done | bytes 1048608 | tf_op jit(solution)/shard_map/ppermute | solution.py:446
  246.4 33.3 %collective-permute-done.15 = bf16[512,1024]{1,0:T(8,128)(2,1)} collective-permute-done((bf16[512,1024]{1,0:T(8,128)(2,1)}, bf16[512,1024]{1,0:T(8,128)(2,1)}, u32[]{:S(2)}, u32[]{:S(2)}) %collective-permute-start.15) | collective-permute-done | bytes 1048608 | tf_op jit(solution)/shard_map/ppermute | solution.py:446
  310.2 14.3 %collective-permute-done.18 = bf16[512,1024]{1,0:T(8,128)(2,1)} collective-permute-done((bf16[512,1024]{1,0:T(8,128)(2,1)}, bf16[512,1024]{1,0:T(8,128)(2,1)}, u32[]{:S(2)}, u32[]{:S(2)}) %collective-permute-start.18) | collective-permute-done | bytes 1048608 | tf_op jit(solution)/shard_map/ppermute | solution.py:511
  333.2 8.6 shard_map.247
  341.8 8.2 shard_map.248
  356.5 7.9 shard_map.249
  370.2 9.5 %collective-permute-done.29 = bf16[128,2048]{1,0:T(8,128)(2,1)S(1)} collective-permute-done((bf16[128,2048]{1,0:T(8,128)(2,1)S(1)}, bf16[128,2048]{1,0:T(8,128)(2,1)S(1)}, u32[]{:S(2)}, u32[]{:S(2)}) %collective-permute-start.29) | collective-permute-done | bytes 524320 | tf_op jit(solution)/shard_map/ppermute | solution.py:385
  379.9 7.7 shard_map.250
  398.3 12.2 %collective-permute-done.31 = bf16[128,2048]{1,0:T(8,128)(2,1)S(1)} collective-permute-done((bf16[128,2048]{1,0:T(8,128)(2,1)S(1)}, bf16[128,2048]{1,0:T(8,128)(2,1)S(1)}, u32[]{:S(2)}, u32[]{:S(2)}) %collective-permute-start.31) | collective-permute-done | bytes 524320 | tf_op jit(solution)/shard_map/ppermute | solution.py:385
  418.6 7.0 collective-permute-done.32
  430.5 10.9 %collective-permute-done.35.part = bf16[128,2048]{1,0:T(8,128)(2,1)S(1)} collective-permute-done((bf16[128,2048]{1,0:T(8,128)(2,1)S(1)}, bf16[128,2048]{1,0:T(8,128)(2,1)S(1)}, u32[]{:S(2)}, u32[]{:S(2)}) %collective-permute-start.35) | collective-permute-done | bytes 524320 | tf_op jit(solution)/shard_map/ppermute | solution.py:385
  446.1 9.7 %shard_map.251 = (bf16[1024,2048]{1,0:T(8,128)(2,1)S(1)}, bf16[1024,1024]{1,0:T(8,128)(2,1)S(1)}, bf16[1024,1024]{1,0:T(8,128)(2,1)S(1)}, f32[128,2048]{1,0:T(8,128)S(1)}, bf16[128,2048]{1,0:T(8,128)(2,1)S(1)}) custom-call(bf16[128,2048]{1,0:T(8,128)(2,1)S(1)} %subtract_convert_fusion.3.part, bf16[128,2048]{1,0:T(8,128)(2,1)S(1)} %collective-permute-done.33.other, ...), custom_call_target="tpu_custom_call" | custom-call | flops 3221225472 | bytes 12582912 | tf_op jit(solution)/shard_map/pallas_call | solution.py:330
  456.9 9.7 %shard_map.252 = (bf16[1024,2048]{1,0:T(8,128)(2,1)S(1)}, bf16[1024,1024]{1,0:T(8,128)(2,1)S(1)}, bf16[1024,1024]{1,0:T(8,128)(2,1)S(1)}, f32[128,2048]{1,0:T(8,128)S(1)}, bf16[128,2048]{1,0:T(8,128)(2,1)S(1)}) custom-call(bf16[128,2048]{1,0:T(8,128)(2,1)S(1)} %collective-permute-done.35.part, ...), custom_call_target="tpu_custom_call", output_to_operand_aliasing={{0}: (7, {}), {1}: (8, {}), {2}: (9, {})} | custom-call | flops 3221225472 | bytes 12582912 | tf_op jit(solution)/shard_map/pallas_call | solution.py:330
  469.3 9.7 %shard_map.253 = (bf16[1024,2048]{1,0:T(8,128)(2,1)S(1)}, bf16[1024,1024]{1,0:T(8,128)(2,1)S(1)}, bf16[1024,1024]{1,0:T(8,128)(2,1)S(1)}, f32[128,2048]{1,0:T(8,128)S(1)}, bf16[128,2048]{1,0:T(8,128)(2,1)S(1)}) custom-call(bf16[128,2048]{1,0:T(8,128)(2,1)S(1)} %collective-permute-done.36.part, ...), custom_call_target="tpu_custom_call", output_to_operand_aliasing={{0}: (7, {}), {1}: (8, {}), {2}: (9, {})} | custom-call | flops 3221225472 | bytes 12582912 | tf_op jit(solution)/shard_map/pallas_call | solution.py:330
  482.4 11.5 %collective-permute-done.43 = bf16[128,2048]{1,0:T(8,128)(2,1)S(1)} collective-permute-done((bf16[128,2048]{1,0:T(8,128)(2,1)S(1)}, bf16[128,2048]{1,0:T(8,128)(2,1)S(1)}, u32[]{:S(2)}, u32[]{:S(2)}) %collective-permute-start.43) | collective-permute-done | bytes 524320 | tf_op jit(solution)/shard_map/ppermute | solution.py:385
  494.9 9.8 %shard_map.254 = (bf16[1024,2048]{1,0:T(8,128)(2,1)S(1)}, bf16[1024,1024]{1,0:T(8,128)(2,1)S(1)}, bf16[1024,1024]{1,0:T(8,128)(2,1)S(1)}, f32[128,2048]{1,0:T(8,128)S(1)}, bf16[128,2048]{1,0:T(8,128)(2,1)S(1)}) custom-call(bf16[128,2048]{1,0:T(8,128)(2,1)S(1)} %collective-permute-done.37.part, ...), custom_call_target="tpu_custom_call", output_to_operand_aliasing={{0}: (7, {}), {1}: (8, {}), {2}: (9, {})} | custom-call | flops 3221225472 | bytes 12582912 | tf_op jit(solution)/shard_map/pallas_call | solution.py:330
  509.2 6.1 convolution_convert_fusion
  515.4 9.5 %convolution_convert_fusion.2 = bf16[2048,1024]{1,0:T(8,128)(2,1)} fusion(bf16[1024,2048]{1,0:T(8,128)(2,1)} %copy-done.7, bf16[1024,1024]{1,0:T(8,128)(2,1)} %copy-done.10), kind=kOutput, calls=%fused_computation.2 | convolution fusion | flops 4297064448 | bytes 10485760 | tf_op jit(solution)/shard_map/dot_general | solution.py:40
  533.1 7.7 collective-permute-done.45
  544.3 12.8 %collective-permute-done.46 = bf16[128,2048]{1,0:T(8,128)(2,1)} collective-permute-done((bf16[128,2048]{1,0:T(8,128)(2,1)}, bf16[128,2048]{1,0:T(8,128)(2,1)}, u32[]{:S(2)}, u32[]{:S(2)}) %collective-permute-start.46) | collective-permute-done | bytes 524320 | tf_op jit(solution)/shard_map/ppermute | solution.py:385
  564.8 6.5 convolution_convert_fusion.5
  572.2 6.0 all-to-all-start.6
  578.5 9.5 %convolution_convert_fusion.1 = bf16[2048,1024]{1,0:T(8,128)(2,1)} fusion(bf16[1024,2048]{1,0:T(8,128)(2,1)} %copy-done.7, bf16[1024,1024]{1,0:T(8,128)(2,1)} %copy-done.11), kind=kOutput, calls=%fused_computation.1 | convolution fusion | flops 4297064448 | bytes 10485760 | tf_op jit(solution)/shard_map/dot_general | solution.py:40
  593.6 7.7 collective-permute-done.50
  608.9 10.5 %shard_map.255 = (f32[1024,256]{1,0:T(8,128)S(1)}, f32[1024,256]{1,0:T(8,128)S(1)}, bf16[1024,256]{1,0:T(8,128)(2,1)S(1)}, f32[2,1024,1]{2,1,0:T(8,128)S(1)}, f32[2,1024,1]{2,1,0:T(8,128)S(1)}) custom-call(bf16[1024,256]{1,0:T(8,128)(2,1)S(1)} %copy-done.34, bf16[1024,256]{1,0:T(8,128)(2,1)S(1)} %copy-done.36, bf16[1024,256]{1,0:T(8,128)(2,1)S(1)} %copy-done.38, ...), custom_call_target="tpu_custom_call" | custom-call | flops 1879048192 | bytes 6291456 | tf_op jit(solution)/shard_map/pallas_call | solution.py:241
  632.5 17.9 %collective-permute-done.51 = bf16[128,2048]{1,0:T(8,128)(2,1)S(1)} collective-permute-done((bf16[128,2048]{1,0:T(8,128)(2,1)}, bf16[128,2048]{1,0:T(8,128)(2,1)S(1)}, u32[]{:S(2)}, u32[]{:S(2)}) %collective-permute-start.51) | collective-permute-done | bytes 524320 | tf_op jit(solution)/shard_map/ppermute | solution.py:390
  653.2 8.5 collective-permute-done.53
  663.1 4.9 all-to-all-start.7
  682.2 5.7 convolution_convert_fusion.3
  689.7 5.1 all-to-all-start.10
  724.0 5.3 all-to-all-start.9
  733.5 7.4 all-to-all-start.11
  751.7 12.8 %collective-permute-done.62 = bf16[512,768]{1,0:T(8,128)(2,1)S(1)} collective-permute-done((bf16[512,768]{1,0:T(8,128)(2,1)S(1)}, bf16[512,768]{1,0:T(8,128)(2,1)S(1)}, u32[]{:S(2)}, u32[]{:S(2)}) %collective-permute-start.62) | collective-permute-done | bytes 786464 | tf_op jit(solution)/shard_map/ppermute | solution.py:578
  771.2 10.3 %collective-permute-done.58 = bf16[128,2048]{1,0:T(8,128)(2,1)} collective-permute-done((bf16[128,2048]{1,0:T(8,128)(2,1)}, bf16[128,2048]{1,0:T(8,128)(2,1)}, u32[]{:S(2)}, u32[]{:S(2)}) %collective-permute-start.58) | collective-permute-done | bytes 524320 | tf_op jit(solution)/shard_map/ppermute | solution.py:385
  784.7 19.5 %collective-permute-done.59 = bf16[128,2048]{1,0:T(8,128)(2,1)S(1)} collective-permute-done((bf16[128,2048]{1,0:T(8,128)(2,1)S(1)}, bf16[128,2048]{1,0:T(8,128)(2,1)S(1)}, u32[]{:S(2)}, u32[]{:S(2)}) %collective-permute-start.59) | collective-permute-done | bytes 524320 | tf_op jit(solution)/shard_map/ppermute | solution.py:385
  807.1 6.9 all-to-all-start.12
  826.6 28.2 %collective-permute-done.65 = bf16[64,2048]{1,0:T(8,128)(2,1)S(1)} collective-permute-done((bf16[64,2048]{1,0:T(8,128)(2,1)}, bf16[64,2048]{1,0:T(8,128)(2,1)S(1)}, u32[]{:S(2)}, u32[]{:S(2)}) %collective-permute-start.65) | collective-permute-done | bytes 262176 | tf_op jit(solution)/shard_map/ppermute | solution.py:608
  (517 shorter events, 366.3 us)
Async XLA Ops:
  11.6 24.6 %collective-permute-start = (bf16[192,2048]{1,0:T(8,128)(2,1)}, bf16[192,2048]{1,0:T(8,128)(2,1)}, u32[]{:S(2)}, u32[]{:S(2)}) collective-permute-start(bf16[192,2048]{1,0:T(8,128)(2,1)} %pad_maximum_fusion.2), channel_id=1, source_target_pairs={{0,1},{1,0},{2,3},{3,2},{4,5},{5,4},{6,7},{7,6},{8,9},{9,8},{10,11... | collective-permute-start | bytes 2359304 | tf_op jit(solution)/shard_map/ppermute | solution.py:398
  12.8 22.2 %collective-permute-start.1 = (bf16[192,2048]{1,0:T(8,128)(2,1)}, bf16[192,2048]{1,0:T(8,128)(2,1)}, u32[]{:S(2)}, u32[]{:S(2)}) collective-permute-start(bf16[192,2048]{1,0:T(8,128)(2,1)} %pad_maximum_fusion.2), channel_id=1, source_target_pairs={{0,2},{2,6},{6,4},{4,0},{1,3},{3,7},{7,5},{5,1},{8,10},{10,14},{14... | collective-permute-start | bytes 2359304 | tf_op jit(solution)/shard_map/ppermute | solution.py:385
  18.0 30.7 %all-to-all-start = ((bf16[8,64,768]{2,1,0:T(8,128)(2,1)}), bf16[8,64,768]{2,1,0:T(8,128)(2,1)S(1)}, u32[]{:S(2)}, u32[]{:S(2)}) async-start(bf16[8,64,768]{2,1,0:T(8,128)(2,1)} %reshape.265), calls=%async_computation | async-start | bytes 1572864 | tf_op jit(solution)/shard_map/all_to_all | solution.py:80
  35.1 24.7 %collective-permute-start.2 = (bf16[192,2048]{1,0:T(8,128)(2,1)}, bf16[192,2048]{1,0:T(8,128)(2,1)S(1)}, u32[]{:S(2)}, u32[]{:S(2)}) collective-permute-start(bf16[192,2048]{1,0:T(8,128)(2,1)} %collective-permute-done.1), channel_id=1, source_target_pairs={{0,1},{1,0},{2,3},{3,2},{4,5},{5,4},{6,7},{7,6},{8,9},{9,8},{10,11... | collective-permute-start | bytes 2359304 | tf_op jit(solution)/shard_map/ppermute | solution.py:398
  48.6 69.4 %all-to-all-start.2 = ((bf16[32,2,128]{2,1,0:T(2,128)(2,1)}), bf16[32,2,128]{2,1,0:T(2,128)(2,1)S(1)}, u32[]{:S(2)}, u32[]{:S(2)}) async-start(bf16[32,2,128]{2,1,0:T(2,128)(2,1)} %reshape.319), calls=%async_computation.2 | async-start | bytes 32768 | tf_op jit(solution)/shard_map/all_to_all | solution.py:80
  55.4 22.0 %collective-permute-start.8 = (bf16[512,768]{1,0:T(8,128)(2,1)S(1)}, bf16[512,768]{1,0:T(8,128)(2,1)S(1)}, u32[]{:S(2)}, u32[]{:S(2)}) collective-permute-start(bf16[512,768]{1,0:T(8,128)(2,1)S(1)} %bitcast.282), channel_id=1, source_target_pairs={{0,16},{16,0},{1,17},{17,1},{2,18},{18,2},{3,19},{19,3},{4,20},{20... | collective-permute-start | bytes 2359304 | tf_op jit(solution)/shard_map/ppermute | solution.py:415
  58.5 21.5 %collective-permute-start.7 = (bf16[512,768]{1,0:T(8,128)(2,1)S(1)}, bf16[512,768]{1,0:T(8,128)(2,1)S(1)}, u32[]{:S(2)}, u32[]{:S(2)}) collective-permute-start(bf16[512,768]{1,0:T(8,128)(2,1)S(1)} %bitcast.283), channel_id=1, source_target_pairs={{0,8},{8,0},{1,9},{9,1},{2,10},{10,2},{3,11},{11,3},{4,12},{12,4},... | collective-permute-start | bytes 2359304 | tf_op jit(solution)/shard_map/ppermute | solution.py:97
  130.6 55.2 %all-to-all-start.3 = ((bf16[8,2,64,1024]{3,2,1,0:T(8,128)(2,1)}), bf16[8,2,64,1024]{3,2,1,0:T(8,128)(2,1)}, u32[]{:S(2)}, u32[]{:S(2)}) async-start(bf16[8,2,64,1024]{3,2,1,0:T(8,128)(2,1)} %copy.296), calls=%async_computation.3 | async-start | bytes 4194304 | tf_op jit(solution)/shard_map/all_to_all | solution.py:80
  147.6 48.2 %collective-permute-start.13 = (bf16[512,2048]{1,0:T(8,128)(2,1)}, bf16[512,2048]{1,0:T(8,128)(2,1)}, u32[]{:S(2)}, u32[]{:S(2)}) collective-permute-start(bf16[512,2048]{1,0:T(8,128)(2,1)} %slice_dynamic-update-slice_fusion.7), channel_id=1, source_target_pairs={{0,16},{16,0},{1,17},{17,1},{2,18},{18,2},{3,19},{19,3},{4,20},{20... | collective-permute-start | bytes 6291464 | tf_op jit(solution)/shard_map/ppermute | solution.py:415
  164.3 55.7 %collective-permute-start.12 = (bf16[512,2048]{1,0:T(8,128)(2,1)}, bf16[512,2048]{1,0:T(8,128)(2,1)}, u32[]{:S(2)}, u32[]{:S(2)}) collective-permute-start(bf16[512,2048]{1,0:T(8,128)(2,1)} %slice_dynamic-update-slice_fusion.7), channel_id=1, source_target_pairs={{0,8},{8,0},{1,9},{9,1},{2,10},{10,2},{3,11},{11,3},{4,12},{12,4},... | collective-permute-start | bytes 6291464 | tf_op jit(solution)/shard_map/ppermute | solution.py:97
  185.8 33.8 %all-to-all-start.5 = ((bf16[8,1,64,1024]{3,2,1,0:T(8,128)(2,1)}), bf16[8,1,64,1024]{3,2,1,0:T(8,128)(2,1)}, u32[]{:S(2)}, u32[]{:S(2)}) async-start(bf16[8,1,64,1024]{3,2,1,0:T(8,128)(2,1)} %copy.298), calls=%async_computation.5 | async-start | bytes 2097152 | tf_op jit(solution)/shard_map/all_to_all | solution.py:80
  192.6 136.3 %all-gather.2.cloned.1.call-start = ((), (), s32[]{:S(2)}) async-start(), calls=%async_computation.16 | async-start | bytes 5242880 | tf_op jit(solution)/shard_map/all_gather | solution.py:505
  195.8 85.3 %collective-permute-start.14 = (bf16[512,2048]{1,0:T(8,128)(2,1)}, bf16[512,2048]{1,0:T(8,128)(2,1)}, u32[]{:S(2)}, u32[]{:S(2)}) collective-permute-start(bf16[512,2048]{1,0:T(8,128)(2,1)} %collective-permute-done.13), channel_id=1, source_target_pairs={{0,8},{8,0},{1,9},{9,1},{2,10},{10,2},{3,11},{11,3},{4,12},{12,4},... | collective-permute-start | bytes 6291464 | tf_op jit(solution)/shard_map/ppermute | solution.py:97
  199.3 36.2 %collective-permute-start.10 = (bf16[512,1024]{1,0:T(8,128)(2,1)}, bf16[512,1024]{1,0:T(8,128)(2,1)}, u32[]{:S(2)}, u32[]{:S(2)}) collective-permute-start(bf16[512,1024]{1,0:T(8,128)(2,1)} %bitcast.279), channel_id=1, source_target_pairs={{0,1},{1,0},{2,3},{3,2},{4,5},{5,4},{6,7},{7,6},{8,9},{9,8},{10,11... | collective-permute-start | bytes 3145736 | tf_op jit(solution)/shard_map/ppermute | solution.py:446
  200.5 35.8 %collective-permute-start.11 = (bf16[512,1024]{1,0:T(8,128)(2,1)}, bf16[512,1024]{1,0:T(8,128)(2,1)}, u32[]{:S(2)}, u32[]{:S(2)}) collective-permute-start(bf16[512,1024]{1,0:T(8,128)(2,1)} %bitcast.280), channel_id=1, source_target_pairs={{0,16},{16,0},{1,17},{17,1},{2,18},{18,2},{3,19},{19,3},{4,20},{20... | collective-permute-start | bytes 3145736 | tf_op jit(solution)/shard_map/ppermute | solution.py:446
  219.6 60.1 %collective-permute-start.15 = (bf16[512,1024]{1,0:T(8,128)(2,1)}, bf16[512,1024]{1,0:T(8,128)(2,1)}, u32[]{:S(2)}, u32[]{:S(2)}) collective-permute-start(bf16[512,1024]{1,0:T(8,128)(2,1)} %bitcast.40), channel_id=1, source_target_pairs={{0,1},{1,0},{2,3},{3,2},{4,5},{5,4},{6,7},{7,6},{8,9},{9,8},{10,11... | collective-permute-start | bytes 3145736 | tf_op jit(solution)/shard_map/ppermute | solution.py:446
  219.9 69.3 %collective-permute-start.16 = (bf16[512,1024]{1,0:T(8,128)(2,1)}, bf16[512,1024]{1,0:T(8,128)(2,1)}, u32[]{:S(2)}, u32[]{:S(2)}) collective-permute-start(bf16[512,1024]{1,0:T(8,128)(2,1)} %bitcast.40), channel_id=1, source_target_pairs={{0,16},{16,0},{1,17},{17,1},{2,18},{18,2},{3,19},{19,3},{4,20},{20... | collective-permute-start | bytes 3145736 | tf_op jit(solution)/shard_map/ppermute | solution.py:446
  238.3 46.0 %all-to-all-start.4 = ((bf16[8,128,256]{1,2,0:T(8,128)(2,1)}), bf16[8,128,256]{1,2,0:T(8,128)(2,1)}, u32[]{:S(2)}, u32[]{:S(2)}) async-start(bf16[8,128,256]{1,2,0:T(8,128)(2,1)} %copy.297), calls=%async_computation.4 | async-start | bytes 1048576 | tf_op jit(solution)/shard_map/all_to_all | solution.py:80
  243.0 446.7 %reduce-scatter.6.cloned.1.call-start = ((), (), s32[]{:S(2)}) async-start(), calls=%async_computation.18 | async-start | bytes 5242880 | tf_op jit(solution)/shard_map/reduce_scatter | solution.py:559
  279.7 22.3 %collective-permute-start.19 = (bf16[512,1024]{1,0:T(8,128)(2,1)}, bf16[512,1024]{1,0:T(8,128)(2,1)}, u32[]{:S(2)}, u32[]{:S(2)}) collective-permute-start(bf16[512,1024]{1,0:T(8,128)(2,1)} %collective-permute-done.15), channel_id=1, source_target_pairs={{0,16},{16,0},{1,17},{17,1},{2,18},{18,2},{3,19},{19,3},{4,20},{20... | collective-permute-start | bytes 3145736 | tf_op jit(solution)/shard_map/ppermute | solution.py:514
  279.7 44.8 %collective-permute-start.18 = (bf16[512,1024]{1,0:T(8,128)(2,1)}, bf16[512,1024]{1,0:T(8,128)(2,1)}, u32[]{:S(2)}, u32[]{:S(2)}) collective-permute-start(bf16[512,1024]{1,0:T(8,128)(2,1)} %collective-permute-done.10), channel_id=1, source_target_pairs={{0,16},{16,0},{1,17},{17,1},{2,18},{18,2},{3,19},{19,3},{4,20},{20... | collective-permute-start | bytes 3145736 | tf_op jit(solution)/shard_map/ppermute | solution.py:511
  289.7 38.4 %collective-permute-start.17 = (bf16[128,2048]{1,0:T(8,128)(2,1)S(1)}, bf16[128,2048]{1,0:T(8,128)(2,1)S(1)}, u32[]{:S(2)}, u32[]{:S(2)}) collective-permute-start(bf16[128,2048]{1,0:T(8,128)(2,1)S(1)} %fusion.15.part), channel_id=1, source_target_pairs={{0,8},{8,0},{1,9},{9,1},{2,10},{10,2},{3,11},{11,3},{4,12},{12,4},... | collective-permute-start | bytes 1572872 | tf_op jit(solution)/shard_map/ppermute | solution.py:97
  307.0 34.8 %collective-permute-start.26 = (bf16[128,2048]{1,0:T(8,128)(2,1)}, bf16[128,2048]{1,0:T(8,128)(2,1)}, u32[]{:S(2)}, u32[]{:S(2)}) collective-permute-start(bf16[128,2048]{1,0:T(8,128)(2,1)} %collective-permute-done.21.part), channel_id=1, source_target_pairs={{0,8},{8,0},{1,9},{9,1},{2,10},{10,2},{3,11},{11,3},{4,12},{12,4},... | collective-permute-start | bytes 1572872 | tf_op jit(solution)/shard_map/ppermute | solution.py:97
  327.8 26.2 %collective-permute-start.22 = (bf16[128,2048]{1,0:T(8,128)(2,1)}, bf16[128,2048]{1,0:T(8,128)(2,1)}, u32[]{:S(2)}, u32[]{:S(2)}) collective-permute-start(bf16[128,2048]{1,0:T(8,128)(2,1)} %collective-permute-done.21.part), channel_id=1, source_target_pairs={{0,2},{2,6},{6,4},{4,0},{1,3},{3,7},{7,5},{5,1},{8,10},{10,14},{14... | collective-permute-start | bytes 1572872 | tf_op jit(solution)/shard_map/ppermute | solution.py:385
  396.1 22.5 %collective-permute-start.20 = (bf16[128,2048]{1,0:T(8,128)(2,1)}, bf16[128,2048]{1,0:T(8,128)(2,1)}, u32[]{:S(2)}, u32[]{:S(2)}) collective-permute-start(bf16[128,2048]{1,0:T(8,128)(2,1)} %get-tuple-element.98), channel_id=1, source_target_pairs={{0,8},{8,0},{1,9},{9,1},{2,10},{10,2},{3,11},{11,3},{4,12},{12,4},... | collective-permute-start | bytes 1572872 | tf_op jit(solution)/shard_map/ppermute | solution.py:97
  443.9 22.7 %collective-permute-start.36 = (bf16[128,2048]{1,0:T(8,128)(2,1)S(1)}, bf16[128,2048]{1,0:T(8,128)(2,1)S(1)}, u32[]{:S(2)}, u32[]{:S(2)}) collective-permute-start(bf16[128,2048]{1,0:T(8,128)(2,1)S(1)} %collective-permute-done.35.part), channel_id=1, source_target_pairs={{0,2},{2,6},{6,4},{4,0},{1,3},{3,7},{7,5},{5,1},{8,10},{10,14},{14... | collective-permute-start | bytes 1572872 | tf_op jit(solution)/shard_map/ppermute | solution.py:385
  515.4 217.2 %reduce-scatter.4.cloned.1.call-start = ((), (), s32[]{:S(2)}) async-start(), calls=%async_computation.17 | async-start | bytes 5242880 | tf_op jit(solution)/shard_map/reduce_scatter | solution.py:559
  562.8 27.1 %collective-permute-start.47 = (bf16[128,2048]{1,0:T(8,128)(2,1)}, bf16[128,2048]{1,0:T(8,128)(2,1)}, u32[]{:S(2)}, u32[]{:S(2)}) collective-permute-start(bf16[128,2048]{1,0:T(8,128)(2,1)} %get-tuple-element.256), channel_id=1, source_target_pairs={{0,1},{1,0},{2,3},{3,2},{4,5},{5,4},{6,7},{7,6},{8,9},{9,8},{10,11... | collective-permute-start | bytes 1572872 | tf_op jit(solution)/shard_map/ppermute | solution.py:390
  572.2 21.5 %all-to-all-start.6 = ((bf16[8,128,256]{2,1,0:T(8,128)(2,1)}), bf16[8,128,256]{2,1,0:T(8,128)(2,1)}, u32[]{:S(2)}, u32[]{:S(2)}) async-start(bf16[8,128,256]{2,1,0:T(8,128)(2,1)} %bitcast.291), calls=%async_computation.6 | async-start | bytes 1048576 | tf_op jit(solution)/shard_map/all_to_all | solution.py:80
  578.2 228.1 %reduce-scatter.8.cloned.1.call-start = ((), (), s32[]{:S(2)}) async-start(), calls=%async_computation.19 | async-start | bytes 5242880 | tf_op jit(solution)/shard_map/reduce_scatter | solution.py:559
  578.2 23.1 %collective-permute-start.50 = (bf16[128,2048]{1,0:T(8,128)(2,1)}, bf16[128,2048]{1,0:T(8,128)(2,1)}, u32[]{:S(2)}, u32[]{:S(2)}) collective-permute-start(bf16[128,2048]{1,0:T(8,128)(2,1)} %collective-permute-done.48), channel_id=1, source_target_pairs={{0,2},{2,6},{6,4},{4,0},{1,3},{3,7},{7,5},{5,1},{8,10},{10,14},{14... | collective-permute-start | bytes 1572872 | tf_op jit(solution)/shard_map/ppermute | solution.py:385
  588.7 39.9 %collective-permute-start.49 = (bf16[128,2048]{1,0:T(8,128)(2,1)}, bf16[128,2048]{1,0:T(8,128)(2,1)}, u32[]{:S(2)}, u32[]{:S(2)}) collective-permute-start(bf16[128,2048]{1,0:T(8,128)(2,1)} %collective-permute-done.48), channel_id=1, source_target_pairs={{0,1},{1,0},{2,3},{3,2},{4,5},{5,4},{6,7},{7,6},{8,9},{9,8},{10,11... | collective-permute-start | bytes 1572872 | tf_op jit(solution)/shard_map/ppermute | solution.py:390
  601.3 29.3 %collective-permute-start.52 = (bf16[128,2048]{1,0:T(8,128)(2,1)}, bf16[128,2048]{1,0:T(8,128)(2,1)}, u32[]{:S(2)}, u32[]{:S(2)}) collective-permute-start(bf16[128,2048]{1,0:T(8,128)(2,1)} %collective-permute-done.50), channel_id=1, source_target_pairs={{0,2},{2,6},{6,4},{4,0},{1,3},{3,7},{7,5},{5,1},{8,10},{10,14},{14... | collective-permute-start | bytes 1572872 | tf_op jit(solution)/shard_map/ppermute | solution.py:385
  627.0 23.4 %collective-permute-start.51 = (bf16[128,2048]{1,0:T(8,128)(2,1)}, bf16[128,2048]{1,0:T(8,128)(2,1)S(1)}, u32[]{:S(2)}, u32[]{:S(2)}) collective-permute-start(bf16[128,2048]{1,0:T(8,128)(2,1)} %collective-permute-done.50), channel_id=1, source_target_pairs={{0,1},{1,0},{2,3},{3,2},{4,5},{5,4},{6,7},{7,6},{8,9},{9,8},{10,11... | collective-permute-start | bytes 1572872 | tf_op jit(solution)/shard_map/ppermute | solution.py:390
  630.6 31.1 %collective-permute-start.53 = (bf16[128,2048]{1,0:T(8,128)(2,1)}, bf16[128,2048]{1,0:T(8,128)(2,1)S(1)}, u32[]{:S(2)}, u32[]{:S(2)}) collective-permute-start(bf16[128,2048]{1,0:T(8,128)(2,1)} %collective-permute-done.52), channel_id=1, source_target_pairs={{0,1},{1,0},{2,3},{3,2},{4,5},{5,4},{6,7},{7,6},{8,9},{9,8},{10,11... | collective-permute-start | bytes 1572872 | tf_op jit(solution)/shard_map/ppermute | solution.py:390
  673.4 109.6 %collective-permute-start.63 = (bf16[128,2048]{1,0:T(8,128)(2,1)}, bf16[128,2048]{1,0:T(8,128)(2,1)}, u32[]{:S(2)}, u32[]{:S(2)}) collective-permute-start(bf16[128,2048]{1,0:T(8,128)(2,1)} %pad_maximum_fusion.5), channel_id=1, source_target_pairs={{0,8},{8,0},{1,9},{9,1},{2,10},{10,2},{3,11},{11,3},{4,12},{12,4},... | collective-permute-start | bytes 1572872 | tf_op jit(solution)/shard_map/ppermute | solution.py:97
  689.7 34.3 %all-to-all-start.10 = ((bf16[8,64,1024]{2,1,0:T(8,128)(2,1)}), bf16[8,64,1024]{2,1,0:T(8,128)(2,1)}, u32[]{:S(2)}, u32[]{:S(2)}) async-start(bf16[8,64,1024]{2,1,0:T(8,128)(2,1)} %bitcast.309), calls=%async_computation.12 | async-start | bytes 2097152 | tf_op jit(solution)/shard_map/all_to_all | solution.py:80
  697.7 45.7 %collective-permute-start.61 = (bf16[1024,768]{1,0:T(8,128)(2,1)}, bf16[1024,768]{1,0:T(8,128)(2,1)}, u32[]{:S(2)}, u32[]{:S(2)}) collective-permute-start(bf16[1024,768]{1,0:T(8,128)(2,1)} %pad_maximum_fusion.1), channel_id=1, source_target_pairs={{0,8},{8,0},{1,9},{9,1},{2,10},{10,2},{3,11},{11,3},{4,12},{12,4},... | collective-permute-start | bytes 4718600 | tf_op jit(solution)/shard_map/ppermute | solution.py:97
  717.4 144.9 %collective-permute-start.54 = (bf16[128,2048]{1,0:T(8,128)(2,1)}, bf16[128,2048]{1,0:T(8,128)(2,1)}, u32[]{:S(2)}, u32[]{:S(2)}) collective-permute-start(bf16[128,2048]{1,0:T(8,128)(2,1)} %fusion.10), channel_id=1, source_target_pairs={{0,1},{1,0},{2,3},{3,2},{4,5},{5,4},{6,7},{7,6},{8,9},{9,8},{10,11... | collective-permute-start | bytes 1572872 | tf_op jit(solution)/shard_map/ppermute | solution.py:433
  733.5 33.1 %all-to-all-start.11 = ((bf16[8,64,1024]{2,1,0:T(8,128)(2,1)}), bf16[8,64,1024]{2,1,0:T(8,128)(2,1)}, u32[]{:S(2)}, u32[]{:S(2)}) async-start(bf16[8,64,1024]{2,1,0:T(8,128)(2,1)} %bitcast.308), calls=%async_computation.13 | async-start | bytes 2097152 | tf_op jit(solution)/shard_map/all_to_all | solution.py:80
  743.0 28.3 %collective-permute-start.56 = (bf16[128,2048]{1,0:T(8,128)(2,1)}, bf16[128,2048]{1,0:T(8,128)(2,1)}, u32[]{:S(2)}, u32[]{:S(2)}) collective-permute-start(bf16[128,2048]{1,0:T(8,128)(2,1)} %fusion.12), channel_id=1, source_target_pairs={{0,1},{1,0},{2,3},{3,2},{4,5},{5,4},{6,7},{7,6},{8,9},{9,8},{10,11... | collective-permute-start | bytes 1572872 | tf_op jit(solution)/shard_map/ppermute | solution.py:433
  748.2 33.3 %collective-permute-start.58 = (bf16[128,2048]{1,0:T(8,128)(2,1)}, bf16[128,2048]{1,0:T(8,128)(2,1)}, u32[]{:S(2)}, u32[]{:S(2)}) collective-permute-start(bf16[128,2048]{1,0:T(8,128)(2,1)} %fusion), channel_id=1, source_target_pairs={{0,2},{2,6},{6,4},{4,0},{1,3},{3,7},{7,5},{5,1},{8,10},{10,14},{14... | collective-permute-start | bytes 1572872 | tf_op jit(solution)/shard_map/ppermute | solution.py:385
  766.6 39.7 %all-to-all-start.8 = ((bf16[8,64,768]{2,1,0:T(8,128)(2,1)}), bf16[8,64,768]{2,1,0:T(8,128)(2,1)S(1)}, u32[]{:S(2)}, u32[]{:S(2)}) async-start(bf16[8,64,768]{2,1,0:T(8,128)(2,1)} %bitcast.90), calls=%async_computation.8 | async-start | bytes 1572864 | tf_op jit(solution)/shard_map/all_to_all | solution.py:80
  782.9 21.3 %collective-permute-start.59 = (bf16[128,2048]{1,0:T(8,128)(2,1)S(1)}, bf16[128,2048]{1,0:T(8,128)(2,1)S(1)}, u32[]{:S(2)}, u32[]{:S(2)}) collective-permute-start(bf16[128,2048]{1,0:T(8,128)(2,1)S(1)} %fusion.2), channel_id=1, source_target_pairs={{0,2},{2,6},{6,4},{4,0},{1,3},{3,7},{7,5},{5,1},{8,10},{10,14},{14... | collective-permute-start | bytes 1572872 | tf_op jit(solution)/shard_map/ppermute | solution.py:385
  784.2 29.8 %collective-permute-start.64 = (bf16[64,2048]{1,0:T(8,128)(2,1)S(1)}, bf16[64,2048]{1,0:T(8,128)(2,1)}, u32[]{:S(2)}, u32[]{:S(2)}) collective-permute-start(bf16[64,2048]{1,0:T(8,128)(2,1)S(1)} %constant_dynamic-slice_fusion), channel_id=1, source_target_pairs={{0,16},{16,0},{1,17},{17,1},{2,18},{18,2},{3,19},{19,3},{4,20},{20... | collective-permute-start | bytes 786440 | tf_op jit(solution)/shard_map/ppermute | solution.py:578
  806.3 56.1 %collective-permute-start.60 = (bf16[128,2048]{1,0:T(8,128)(2,1)}, bf16[128,2048]{1,0:T(8,128)(2,1)}, u32[]{:S(2)}, u32[]{:S(2)}) collective-permute-start(bf16[128,2048]{1,0:T(8,128)(2,1)} %fusion.4), channel_id=1, source_target_pairs={{0,2},{2,6},{6,4},{4,0},{1,3},{3,7},{7,5},{5,1},{8,10},{10,14},{14... | collective-permute-start | bytes 1572872 | tf_op jit(solution)/shard_map/ppermute | solution.py:385
  807.1 71.6 %all-to-all-start.12 = ((bf16[8,64,1024]{2,1,0:T(8,128)(2,1)}), bf16[8,64,1024]{2,1,0:T(8,128)(2,1)S(1)}, u32[]{:S(2)}, u32[]{:S(2)}) async-start(bf16[8,64,1024]{2,1,0:T(8,128)(2,1)} %bitcast.310), calls=%async_computation.15 | async-start | bytes 2097152 | tf_op jit(solution)/shard_map/all_to_all | solution.py:80
  815.7 39.1 %collective-permute-start.65 = (bf16[64,2048]{1,0:T(8,128)(2,1)}, bf16[64,2048]{1,0:T(8,128)(2,1)S(1)}, u32[]{:S(2)}, u32[]{:S(2)}) collective-permute-start(bf16[64,2048]{1,0:T(8,128)(2,1)} %add_convert_fusion.6), channel_id=1, source_target_pairs={{0,0},{1,4},{2,8},{3,12},{4,16},{5,20},{6,24},{7,28},{8,1},{9,5},{... | collective-permute-start | bytes 786440 | tf_op jit(solution)/shard_map/ppermute | solution.py:608
  (121 other events, 1057.5 us)
Sparse Core Ops, SparseCore 0:
  199.4 87.3 all-gather.1
  515.5 54.6 reduce-scatter.5
  573.5 76.6 reduce-scatter.3
  653.0 54.8 reduce-scatter.7

commit v4 on v3

--- a/solution.py
+++ b/solution.py
@@ -317,7 +317,7 @@
 def feed_step(at, count, pair, weights, saved, held, kernel, dtypes):
     tokens, width = pair[0].shape
     feed = weights[0].shape[1]
-    step = min(256, feed)
+    step = min(512, feed)
     rows = 2 * tokens
     block = pl.BlockSpec((rows, step), lambda f: (at, f))
     part = pl.BlockSpec((tokens, width), lambda f: (0, 0))
@@ -426,10 +426,11 @@
                 chunks.append(lax.dynamic_slice_in_dim(array_in, first, tok_count))
         return jnp.concatenate(chunks, axis=0)
 
-    def seq_sum(part_of):
+    def seq_sum(part_of, *last):
         total = None
         for step in list(range(1, n_z)) + [0]:
-            part = part_of(behind[step, z_at]).reshape(n_y, tok_count, model_width)
+            part = part_of(behind[step, z_at], *(() if step else last))
+            part = part.reshape(n_y, tok_count, model_width)
             away = lax.ppermute(pick(part, 1 - y_at).astype(BF16), "y", SWAP)
             mine = pick(part, y_at) + away.astype(F32)
             if total is not None:
@@ -511,22 +512,22 @@
     corner_g = lax.ppermute(sent_g[1], "x", SWAP)
     att_tok = tie(attended.reshape(n_seq, tok_count, own_width), *sent_g)
     att_tok = exchange(att_tok, SEQ)
-    corner_d = lax.ppermute(sent_d[1], "x", SWAP)
+    corner_d = lax.ppermute(sent_d[2], "y", SWAP)
     att_tok = att_tok.transpose(1, 0, 2).reshape(tok_count, model_width)
     full_o = dp_gather(w_out_mine)
-    branch = tie(matmul(att_tok, full_o), *sent_d)
+    branch = matmul(att_tok, full_o)
     w_g = rest_gather(sent_g, corner_g, branch)
     w_d = rest_gather(sent_d, corner_d, branch)
     branch_norm, branch_factor = norm_apply(branch, gain_a)
     hidden = to_feed_order(tokens).astype(F32) + branch_norm
     hidden_low = hidden.astype(BF16)
 
-    def feed_pass(own, saved, kernel, dtypes):
+    def feed_pass(own, saved, kernel, dtypes, gate=()):
         held, total, rows = [], None, own
         for at in range(n_z):
             pair = (rows, core_swap(rows))
             if at < n_z - 1:
-                rows = ring_send(rows)
+                rows = ring_send(tie(rows, *gate) if gate and at == 1 else rows)
             if at > 1:
                 pair = tie(pair, total)
             *held, mine, away = feed_step(
@@ -545,7 +546,7 @@
         return mine
 
     (hid, gate, upward, active), result = feed_pass(
-        hidden_low, (), feed_kernel, (F32, F32, BF16)
+        hidden_low, (), feed_kernel, (F32, F32, BF16), sent_d
     )
     result_norm, result_factor = norm_apply(result, gain_f)
     output = from_feed_order((hidden + result_norm).astype(BF16))
@@ -598,15 +599,21 @@
         saved, g_att, qkv, my_gq, my_gk, tables, docs, own_heads
     )
     dots = jnp.stack([jnp.sum(dot_q, axis=(0, 2)), jnp.sum(dot_k, axis=(0, 2))])
-    branch_row = seq_gather(grad_branch)
-    dots = seq_total(tie(dots, branch_row)) / model_width
+    branch_row = seq_gather(from_feed_order(tie(grad_branch, grad_attended)))
+    hidden_back, ffn_gain_term, attn_gain_term = [
+        from_feed_order(tie(a, grad_attended))
+        for a in (grad_hidden, ffn_gain_term, attn_gain_term)
+    ]
+    early = (branch_row, hidden_back, ffn_gain_term, attn_gain_term)
+    dots = seq_total(tie(dots, *early)) / model_width
     home_d = feed_home(tie(sum_d, dots))
+    grad_w_down = feed_rows(home_d).T
 
     grad_w_out = dot_left_t(seq_order(attended), branch_row).astype(BF16)
     grad_w_out = dp_sum(grad_w_out)
     home = [(d * n_seq + s, s * n_dp + d) for d in range(n_dp) for s in range(n_seq)]
     grad_w_out = lax.ppermute(grad_w_out, ALL, home)
-    grad_w_out = from_feed_order(grad_w_out).astype(F32)
+    grad_w_out = grad_w_out.astype(F32)
 
 
     def lin_back(grad_in, lin, factor, gain_vec, mean_dot):
@@ -618,37 +625,37 @@
     grad_k_lin, key_gain_term = lin_back(grad_k, k_lin, k_factor, my_gk, dots[1][:, None])
     grad_lin = jnp.concatenate([grad_q_lin, grad_k_lin, grad_v], axis=1)
 
-    def row_part(z_of):
-        rows = lax.dynamic_slice_in_dim(grad_lin, z_of * n_y * tok_count, n_y * tok_count)
-        return dot_right_t(rows, w_heads)
-
-    grad_input = from_feed_order(grad_hidden) + seq_sum(row_part)
-
-    grad_heads = dot_left_t(x_row, grad_lin).astype(BF16)
-    grad_heads = dp_sum(grad_heads)
-    home_g = feed_home(tie(sum_g, home_d))
-    home_u = feed_home(tie(sum_u, home_g))
-    grad_w_gate, grad_w_up = feed_rows(home_g), feed_rows(home_u)
-    grad_w_down = feed_rows(home_d).T
-    grad_heads = exchange(grad_heads.reshape(n_seq, own_rows, 3 * own_width), SEQ)
-    grad_heads = grad_heads.reshape(n_seq, own_rows, 3, own_width).transpose(2, 1, 0, 3)
-    grad_heads = grad_heads.reshape(3, own_rows, model_width).astype(F32)
-
     def place(term):
-        return lax.dynamic_update_slice(
-            jnp.zeros((model_width,), F32), term, (seq_at * own_width,)
-        )
+        mine = jnp.arange(n_seq)[:, None] == seq_at
+        return jnp.where(mine, term[None, :], 0.0).reshape(model_width)
 
     gain_terms = jnp.stack(
         [
             place(query_gain_term),
             place(key_gain_term),
-            from_feed_order(attn_gain_term),
-            from_feed_order(ffn_gain_term),
+            attn_gain_term,
+            ffn_gain_term,
         ]
     )
     gain_terms = gain_terms.reshape(4, n_all, own_rows).transpose(1, 0, 2)
     gain_grads = jnp.sum(exchange(gain_terms, ALL), axis=0)
+
+    def row_part(z_of, *earlier):
+        rows = lax.dynamic_slice_in_dim(grad_lin, z_of * n_y * tok_count, n_y * tok_count)
+        if earlier:
+            rows = tie(rows, *earlier)
+        return dot_right_t(rows, w_heads)
+
+    grad_input = hidden_back + seq_sum(row_part, grad_w_down, grad_w_out)
+
+    grad_heads = dot_left_t(x_row, grad_lin).astype(BF16)
+    grad_heads = dp_sum(grad_heads)
+    home_g = feed_home(tie(sum_g, home_d))
+    home_u = feed_home(tie(sum_u, home_g, gain_grads, grad_w_out))
+    grad_w_gate, grad_w_up = feed_rows(home_g), feed_rows(home_u)
+    grad_heads = exchange(grad_heads.reshape(n_seq, own_rows, 3 * own_width), SEQ)
+    grad_heads = grad_heads.reshape(n_seq, own_rows, 3, own_width).transpose(2, 1, 0, 3)
+    grad_heads = grad_heads.reshape(3, own_rows, model_width).astype(F32)
 
     return (
         output[None],

time: 902 us -> 849 us (0.941)
  waiting for transfers between devices: 319 us -> 293 us
  Pallas kernels: 89.2 us -> 74 us
    ppermute x21, waiting for transfers between devices: 147 us -> 109 us  [ring_send(): return lax.ppermute(part, 'z', ring)]
    all_to_all x13, waiting for transfers between devices: 26.6 us -> 57.8 us  [exchange(): lax.all_to_all(array_in, axes, split_axis=0, concat_axis=0, tiled=True)]
    pallas_call x8, Pallas kernels: 71.4 us -> 56.2 us  [feed_step(): pl.pallas_call(kernel, grid=(feed // step,), in_specs=[part, part] + [pl....]
    ppermute x1, waiting for transfers between devices: 14.3 us -> 0.01 us  [body(): corner_g = lax.ppermute(sent_g[1], 'x', SWAP)]
    ppermute x1, waiting for transfers between devices: 28.2 us -> 15.5 us  [body(): grad_w_out = lax.ppermute(grad_w_out, ALL, home)]
    unnamed x201 -> x214, local copies, waits for them, and re-layouts: 75.5 us -> 80.8 us
  transfers between devices with their start and end apart: 83 -> 83, of which waited for: 32 -> 33; matrix products, arithmetic and copies ran while one was open for 30% -> 30% of each run, Pallas kernels for 8% -> 7%
where the time goes in v4:
time: 849 us; the launch traced here: 836 us
  waiting for transfers between devices  293 us (35%)
  local copies, waits for them, and re-layouts  202 us (24%)
  starting transfers between devices  130 us (15%)
  Pallas kernels  74 us (9%)
  other arithmetic  58.7 us (7%)
  matrix products  57.3 us (7%)
  between operations  21 us (2%)
    ppermute x21, waiting for transfers between devices, ring_send(): return lax.ppermute(part, 'z', ring)  109 us
    unnamed x214, local copies, waits for them, and re-layouts  80.8 us
    all_to_all x13, starting transfers between devices, exchange(): lax.all_to_all(array_in, axes, split_axis=0, concat_axis=0, tiled=True)  76.4 us
    all_to_all x13, waiting for transfers between devices, exchange(): lax.all_to_all(array_in, axes, split_axis=0, concat_axis=0, tiled=True)  57.8 us
    pallas_call x8, Pallas kernels, feed_step(): pl.pallas_call(kernel, grid=(feed // step,), in_specs=[part, part] + [pl....  56.2 us
    ppermute x4, waiting for transfers between devices, rest_send(): return (mine, lax.ppermute(mine, 'y', SWAP), lax.ppermute(mine, 'x', SWAP))  42.7 us
    dot_general x5, matrix products, dot_left_t(): lax.dot_general(left_mat, right_mat, (((0,), (0,)), ((), ())), preferred_...  35.9 us
    ppermute x22, starting transfers between devices, core_swap(): return lax.ppermute(array_in, 'core', SWAP)  24.8 us
  transfers between devices with their start and end apart: 83, of which 33 were waited for; matrix products, arithmetic and copies ran while one was open for 30% of the time, Pallas kernels for 7%

profile of v4, /device:TPU:25, one launch (start us, length us, event | category | flops | bytes accessed | tf_op | source)
XLA Modules:
  0.0 836.1 jit_solution(10266538765150508376)
XLA Ops:
  18.0 5.2 all-to-all-start
  42.3 6.5 all-to-all-done
  48.8 6.7 all-to-all-start.2
  62.2 14.1 %collective-permute-done.3 = bf16[192,2048]{1,0:T(8,128)(2,1)S(1)} collective-permute-done((bf16[192,2048]{1,0:T(8,128)(2,1)}, bf16[192,2048]{1,0:T(8,128)(2,1)S(1)}, u32[]{:S(2)}, u32[]{:S(2)}) %collective-permute-start.3) | collective-permute-done | bytes 786464 | tf_op jit(solution)/shard_map/ppermute | solution.py:385
  80.6 14.3 %collective-permute-done.5 = bf16[192,2048]{1,0:T(8,128)(2,1)S(1)} collective-permute-done((bf16[192,2048]{1,0:T(8,128)(2,1)S(1)}, bf16[192,2048]{1,0:T(8,128)(2,1)S(1)}, u32[]{:S(2)}, u32[]{:S(2)}) %collective-permute-start.5) | collective-permute-done | bytes 786464 | tf_op jit(solution)/shard_map/ppermute | solution.py:385
  98.1 13.4 %collective-permute-done.6 = bf16[192,2048]{1,0:T(8,128)(2,1)S(1)} collective-permute-done((bf16[192,2048]{1,0:T(8,128)(2,1)S(1)}, bf16[192,2048]{1,0:T(8,128)(2,1)S(1)}, u32[]{:S(2)}, u32[]{:S(2)}) %collective-permute-start.6) | collective-permute-done | bytes 786464 | tf_op jit(solution)/shard_map/ppermute | solution.py:398
  112.7 5.3 fusion.19.refs_0_.refs_1_.refs_2_.refs_5_.refs_6_
  119.0 5.6 all-to-all-start.1
  130.3 8.8 %all-to-all-start.3 = ((bf16[8,2,64,1024]{3,2,1,0:T(8,128)(2,1)}), bf16[8,2,64,1024]{3,2,1,0:T(8,128)(2,1)}, u32[]{:S(2)}, u32[]{:S(2)}) async-start(bf16[8,2,64,1024]{3,2,1,0:T(8,128)(2,1)} %copy.300), calls=%async_computation.3 | async-start | bytes 4194304 | tf_op jit(solution)/shard_map/all_to_all | solution.py:80
  165.9 19.7 %all-to-all-done.3 = bf16[8,2,64,1024]{3,2,1,0:T(8,128)(2,1)} async-done(((bf16[8,2,64,1024]{3,2,1,0:T(8,128)(2,1)}), bf16[8,2,64,1024]{3,2,1,0:T(8,128)(2,1)}, u32[]{:S(2)}, u32[]{:S(2)}) %all-to-all-start.3) | async-done | bytes 2097184 | tf_op jit(solution)/shard_map/all_to_all | solution.py:80
  185.6 6.8 all-to-all-start.5
  207.3 7.3 shard_map.246
  224.5 11.2 %collective-permute-done.10 = bf16[512,1024]{1,0:T(8,128)(2,1)} collective-permute-done((bf16[512,1024]{1,0:T(8,128)(2,1)}, bf16[512,1024]{1,0:T(8,128)(2,1)}, u32[]{:S(2)}, u32[]{:S(2)}) %collective-permute-start.10) | collective-permute-done | bytes 1048608 | tf_op jit(solution)/shard_map/ppermute | solution.py:447
  246.4 30.9 %collective-permute-done.17 = bf16[512,1024]{1,0:T(8,128)(2,1)} collective-permute-done((bf16[512,1024]{1,0:T(8,128)(2,1)}, bf16[512,1024]{1,0:T(8,128)(2,1)}, u32[]{:S(2)}, u32[]{:S(2)}) %collective-permute-start.17) | collective-permute-done | bytes 1048608 | tf_op jit(solution)/shard_map/ppermute | solution.py:447
  299.8 8.9 %collective-permute-done.19 = bf16[512,1024]{1,0:T(8,128)(2,1)} collective-permute-done((bf16[512,1024]{1,0:T(8,128)(2,1)}, bf16[512,1024]{1,0:T(8,128)(2,1)}, u32[]{:S(2)}, u32[]{:S(2)}) %collective-permute-start.19) | collective-permute-done | bytes 1048608 | tf_op jit(solution)/shard_map/ppermute | solution.py:515
  320.4 7.8 shard_map.247
  328.2 7.4 shard_map.248
  338.8 7.0 shard_map.249
  352.7 9.1 %collective-permute-done.29 = bf16[128,2048]{1,0:T(8,128)(2,1)S(1)} collective-permute-done((bf16[128,2048]{1,0:T(8,128)(2,1)S(1)}, bf16[128,2048]{1,0:T(8,128)(2,1)S(1)}, u32[]{:S(2)}, u32[]{:S(2)}) %collective-permute-start.29) | collective-permute-done | bytes 524320 | tf_op jit(solution)/shard_map/ppermute | solution.py:385
  362.0 6.9 shard_map.250
  379.8 12.2 %collective-permute-done.31 = bf16[128,2048]{1,0:T(8,128)(2,1)S(1)} collective-permute-done((bf16[128,2048]{1,0:T(8,128)(2,1)S(1)}, bf16[128,2048]{1,0:T(8,128)(2,1)S(1)}, u32[]{:S(2)}, u32[]{:S(2)}) %collective-permute-start.31) | collective-permute-done | bytes 524320 | tf_op jit(solution)/shard_map/ppermute | solution.py:385
  400.0 7.0 collective-permute-done.32
  412.0 10.9 %collective-permute-done.35.part = bf16[128,2048]{1,0:T(8,128)(2,1)S(1)} collective-permute-done((bf16[128,2048]{1,0:T(8,128)(2,1)S(1)}, bf16[128,2048]{1,0:T(8,128)(2,1)S(1)}, u32[]{:S(2)}, u32[]{:S(2)}) %collective-permute-start.35) | collective-permute-done | bytes 524320 | tf_op jit(solution)/shard_map/ppermute | solution.py:385
  427.7 6.8 shard_map.251
  435.6 6.8 shard_map.252
  445.1 6.8 shard_map.253
  458.7 9.9 %collective-permute-done.43 = bf16[128,2048]{1,0:T(8,128)(2,1)S(1)} collective-permute-done((bf16[128,2048]{1,0:T(8,128)(2,1)S(1)}, bf16[128,2048]{1,0:T(8,128)(2,1)S(1)}, u32[]{:S(2)}, u32[]{:S(2)}) %collective-permute-start.43) | collective-permute-done | bytes 524320 | tf_op jit(solution)/shard_map/ppermute | solution.py:385
  469.6 6.9 shard_map.254
  480.9 6.1 convolution_convert_fusion
  487.1 9.5 %convolution_convert_fusion.2 = bf16[2048,1024]{1,0:T(8,128)(2,1)} fusion(bf16[1024,2048]{1,0:T(8,128)(2,1)} %copy-done.7, bf16[1024,1024]{1,0:T(8,128)(2,1)} %copy-done.10), kind=kOutput, calls=%fused_computation.2 | convolution fusion | flops 4297064448 | bytes 10485760 | tf_op jit(solution)/shard_map/dot_general | solution.py:40
  505.3 7.8 collective-permute-done.45
  516.1 11.7 %collective-permute-done.46 = bf16[128,2048]{1,0:T(8,128)(2,1)S(1)} collective-permute-done((bf16[128,2048]{1,0:T(8,128)(2,1)S(1)}, bf16[128,2048]{1,0:T(8,128)(2,1)S(1)}, u32[]{:S(2)}, u32[]{:S(2)}) %collective-permute-start.46) | collective-permute-done | bytes 524320 | tf_op jit(solution)/shard_map/ppermute | solution.py:385
  530.6 7.2 convolution_convert_fusion.5
  549.5 10.1 %convolution_convert_fusion.1 = bf16[2048,1024]{1,0:T(8,128)(2,1)} fusion(bf16[1024,2048]{1,0:T(8,128)(2,1)} %copy-done.7, bf16[1024,1024]{1,0:T(8,128)(2,1)} %copy-done.11), kind=kOutput, calls=%fused_computation.1 | convolution fusion | flops 4297064448 | bytes 10485760 | tf_op jit(solution)/shard_map/dot_general | solution.py:40
  584.5 10.5 %shard_map.255 = (f32[1024,256]{1,0:T(8,128)S(1)}, f32[1024,256]{1,0:T(8,128)S(1)}, bf16[1024,256]{1,0:T(8,128)(2,1)S(1)}, f32[2,1024,1]{2,1,0:T(8,128)S(1)}, f32[2,1024,1]{2,1,0:T(8,128)S(1)}) custom-call(bf16[1024,256]{1,0:T(8,128)(2,1)S(1)} %copy-done.35, bf16[1024,256]{1,0:T(8,128)(2,1)S(1)} %copy-done.37, bf16[1024,256]{1,0:T(8,128)(2,1)S(1)} %copy-done.39, ...), custom_call_target="tpu_custom_call" | custom-call | flops 1879048192 | bytes 6291456 | tf_op jit(solution)/shard_map/pallas_call | solution.py:241
  608.2 15.3 %collective-permute-done.51 = bf16[128,2048]{0,1:T(8,128)(2,1)S(1)} collective-permute-done((bf16[128,2048]{0,1:T(8,128)(2,1)}, bf16[128,2048]{0,1:T(8,128)(2,1)S(1)}, u32[]{:S(2)}, u32[]{:S(2)}) %collective-permute-start.51) | collective-permute-done | bytes 524320 | tf_op jit(solution)/shard_map/ppermute | solution.py:390
  626.4 8.8 %collective-permute-done.53 = bf16[128,2048]{0,1:T(8,128)(2,1)S(1)} collective-permute-done((bf16[128,2048]{0,1:T(8,128)(2,1)}, bf16[128,2048]{0,1:T(8,128)(2,1)S(1)}, u32[]{:S(2)}, u32[]{:S(2)}) %collective-permute-start.53) | collective-permute-done | bytes 524320 | tf_op jit(solution)/shard_map/ppermute | solution.py:390
  658.7 6.2 convolution_convert_fusion.3
  669.6 5.7 all-to-all-start.8
  685.9 13.4 %all-to-all-done.8 = bf16[8,64,1024]{2,1,0:T(8,128)(2,1)} async-done(((bf16[8,64,1024]{2,1,0:T(8,128)(2,1)}), bf16[8,64,1024]{2,1,0:T(8,128)(2,1)}, u32[]{:S(2)}, u32[]{:S(2)}) %all-to-all-start.8) | async-done | bytes 1048608 | tf_op jit(solution)/shard_map/all_to_all | solution.py:80
  699.3 5.6 all-to-all-start.10
  707.4 8.4 %all-to-all-done.10 = f32[32,1,256]{2,1,0:T(1,128)} async-done(((f32[32,1,256]{2,1,0:T(1,128)}), f32[32,1,256]{2,1,0:T(1,128)}, u32[]{:S(2)}, u32[]{:S(2)}) %all-to-all-start.10) | async-done | bytes 32800 | tf_op jit(solution)/shard_map/all_to_all | solution.py:80
  715.8 5.2 all-to-all-start.11
  730.2 12.2 %collective-permute-done.65 = bf16[512,768]{1,0:T(8,128)(2,1)S(1)} collective-permute-done((bf16[512,768]{1,0:T(8,128)(2,1)S(1)}, bf16[512,768]{1,0:T(8,128)(2,1)S(1)}, u32[]{:S(2)}, u32[]{:S(2)}) %collective-permute-start.65) | collective-permute-done | bytes 786464 | tf_op jit(solution)/shard_map/ppermute | solution.py:579
  745.0 6.0 all-to-all-start.9
  770.3 15.5 %collective-permute-done.56 = bf16[64,2048]{1,0:T(8,128)(2,1)} collective-permute-done((bf16[64,2048]{1,0:T(8,128)(2,1)}, bf16[64,2048]{1,0:T(8,128)(2,1)}, u32[]{:S(2)}, u32[]{:S(2)}) %collective-permute-start.56) | collective-permute-done | bytes 262176 | tf_op jit(solution)/shard_map/ppermute | solution.py:615
  793.1 6.3 all-to-all-start.12
  820.3 5.8 all-to-all-done.12
  (528 shorter events, 367.8 us)
Async XLA Ops:
  11.6 28.8 %collective-permute-start = (bf16[192,2048]{1,0:T(8,128)(2,1)}, bf16[192,2048]{1,0:T(8,128)(2,1)}, u32[]{:S(2)}, u32[]{:S(2)}) collective-permute-start(bf16[192,2048]{1,0:T(8,128)(2,1)} %pad_maximum_fusion.2), channel_id=1, source_target_pairs={{0,1},{1,0},{2,3},{3,2},{4,5},{5,4},{6,7},{7,6},{8,9},{9,8},{10,11... | collective-permute-start | bytes 2359304 | tf_op jit(solution)/shard_map/ppermute | solution.py:398
  12.8 26.3 %collective-permute-start.1 = (bf16[192,2048]{1,0:T(8,128)(2,1)}, bf16[192,2048]{1,0:T(8,128)(2,1)}, u32[]{:S(2)}, u32[]{:S(2)}) collective-permute-start(bf16[192,2048]{1,0:T(8,128)(2,1)} %pad_maximum_fusion.2), channel_id=1, source_target_pairs={{0,2},{2,6},{6,4},{4,0},{1,3},{3,7},{7,5},{5,1},{8,10},{10,14},{14... | collective-permute-start | bytes 2359304 | tf_op jit(solution)/shard_map/ppermute | solution.py:385
  18.0 30.8 %all-to-all-start = ((bf16[8,64,768]{2,1,0:T(8,128)(2,1)}), bf16[8,64,768]{2,1,0:T(8,128)(2,1)}, u32[]{:S(2)}, u32[]{:S(2)}) async-start(bf16[8,64,768]{2,1,0:T(8,128)(2,1)} %reshape.349), calls=%async_computation | async-start | bytes 1572864 | tf_op jit(solution)/shard_map/all_to_all | solution.py:80
  39.2 22.1 %collective-permute-start.2 = (bf16[192,2048]{1,0:T(8,128)(2,1)}, bf16[192,2048]{1,0:T(8,128)(2,1)S(1)}, u32[]{:S(2)}, u32[]{:S(2)}) collective-permute-start(bf16[192,2048]{1,0:T(8,128)(2,1)} %collective-permute-done.1), channel_id=1, source_target_pairs={{0,1},{1,0},{2,3},{3,2},{4,5},{5,4},{6,7},{7,6},{8,9},{9,8},{10,11... | collective-permute-start | bytes 2359304 | tf_op jit(solution)/shard_map/ppermute | solution.py:398
  48.8 69.6 %all-to-all-start.2 = ((bf16[32,2,128]{2,1,0:T(2,128)(2,1)}), bf16[32,2,128]{2,1,0:T(2,128)(2,1)S(1)}, u32[]{:S(2)}, u32[]{:S(2)}) async-start(bf16[32,2,128]{2,1,0:T(2,128)(2,1)} %reshape.387), calls=%async_computation.2 | async-start | bytes 32768 | tf_op jit(solution)/shard_map/all_to_all | solution.py:80
  55.5 22.3 %collective-permute-start.8 = (bf16[512,768]{1,0:T(8,128)(2,1)}, bf16[512,768]{1,0:T(8,128)(2,1)S(1)}, u32[]{:S(2)}, u32[]{:S(2)}) collective-permute-start(bf16[512,768]{1,0:T(8,128)(2,1)} %bitcast.8), channel_id=1, source_target_pairs={{0,16},{16,0},{1,17},{17,1},{2,18},{18,2},{3,19},{19,3},{4,20},{20... | collective-permute-start | bytes 2359304 | tf_op jit(solution)/shard_map/ppermute | solution.py:415
  58.9 21.5 %collective-permute-start.7 = (bf16[512,768]{1,0:T(8,128)(2,1)}, bf16[512,768]{1,0:T(8,128)(2,1)S(1)}, u32[]{:S(2)}, u32[]{:S(2)}) collective-permute-start(bf16[512,768]{1,0:T(8,128)(2,1)} %bitcast.8), channel_id=1, source_target_pairs={{0,8},{8,0},{1,9},{9,1},{2,10},{10,2},{3,11},{11,3},{4,12},{12,4},... | collective-permute-start | bytes 2359304 | tf_op jit(solution)/shard_map/ppermute | solution.py:97
  76.5 19.6 %collective-permute-start.4 = (bf16[192,2048]{1,0:T(8,128)(2,1)S(1)}, bf16[192,2048]{1,0:T(8,128)(2,1)S(1)}, u32[]{:S(2)}, u32[]{:S(2)}) collective-permute-start(bf16[192,2048]{1,0:T(8,128)(2,1)S(1)} %collective-permute-done.3), channel_id=1, source_target_pairs={{0,1},{1,0},{2,3},{3,2},{4,5},{5,4},{6,7},{7,6},{8,9},{9,8},{10,11... | collective-permute-start | bytes 2359304 | tf_op jit(solution)/shard_map/ppermute | solution.py:398
  130.3 55.3 %all-to-all-start.3 = ((bf16[8,2,64,1024]{3,2,1,0:T(8,128)(2,1)}), bf16[8,2,64,1024]{3,2,1,0:T(8,128)(2,1)}, u32[]{:S(2)}, u32[]{:S(2)}) async-start(bf16[8,2,64,1024]{3,2,1,0:T(8,128)(2,1)} %copy.300), calls=%async_computation.3 | async-start | bytes 4194304 | tf_op jit(solution)/shard_map/all_to_all | solution.py:80
  149.2 50.0 %collective-permute-start.13 = (bf16[512,2048]{1,0:T(8,128)(2,1)}, bf16[512,2048]{1,0:T(8,128)(2,1)}, u32[]{:S(2)}, u32[]{:S(2)}) collective-permute-start(bf16[512,2048]{1,0:T(8,128)(2,1)} %slice_dynamic-update-slice_fusion.7), channel_id=1, source_target_pairs={{0,16},{16,0},{1,17},{17,1},{2,18},{18,2},{3,19},{19,3},{4,20},{20... | collective-permute-start | bytes 6291464 | tf_op jit(solution)/shard_map/ppermute | solution.py:415
  161.4 59.5 %collective-permute-start.12 = (bf16[512,2048]{1,0:T(8,128)(2,1)}, bf16[512,2048]{1,0:T(8,128)(2,1)}, u32[]{:S(2)}, u32[]{:S(2)}) collective-permute-start(bf16[512,2048]{1,0:T(8,128)(2,1)} %slice_dynamic-update-slice_fusion.7), channel_id=1, source_target_pairs={{0,8},{8,0},{1,9},{9,1},{2,10},{10,2},{3,11},{11,3},{4,12},{12,4},... | collective-permute-start | bytes 6291464 | tf_op jit(solution)/shard_map/ppermute | solution.py:97
  185.6 34.0 %all-to-all-start.5 = ((bf16[8,1,64,1024]{3,2,1,0:T(8,128)(2,1)}), bf16[8,1,64,1024]{3,2,1,0:T(8,128)(2,1)}, u32[]{:S(2)}, u32[]{:S(2)}) async-start(bf16[8,1,64,1024]{3,2,1,0:T(8,128)(2,1)} %copy.304), calls=%async_computation.5 | async-start | bytes 2097152 | tf_op jit(solution)/shard_map/all_to_all | solution.py:80
  192.4 123.7 %all-gather.2.cloned.1.call-start = ((), (), s32[]{:S(2)}) async-start(), calls=%async_computation.16 | async-start | bytes 5242880 | tf_op jit(solution)/shard_map/all_gather | solution.py:506
  199.2 78.3 %collective-permute-start.14 = (bf16[512,2048]{1,0:T(8,128)(2,1)}, bf16[512,2048]{1,0:T(8,128)(2,1)}, u32[]{:S(2)}, u32[]{:S(2)}) collective-permute-start(bf16[512,2048]{1,0:T(8,128)(2,1)} %collective-permute-done.13), channel_id=1, source_target_pairs={{0,8},{8,0},{1,9},{9,1},{2,10},{10,2},{3,11},{11,3},{4,12},{12,4},... | collective-permute-start | bytes 6291464 | tf_op jit(solution)/shard_map/ppermute | solution.py:97
  199.5 36.2 %collective-permute-start.10 = (bf16[512,1024]{1,0:T(8,128)(2,1)}, bf16[512,1024]{1,0:T(8,128)(2,1)}, u32[]{:S(2)}, u32[]{:S(2)}) collective-permute-start(bf16[512,1024]{1,0:T(8,128)(2,1)} %bitcast.284), channel_id=1, source_target_pairs={{0,1},{1,0},{2,3},{3,2},{4,5},{5,4},{6,7},{7,6},{8,9},{9,8},{10,11... | collective-permute-start | bytes 3145736 | tf_op jit(solution)/shard_map/ppermute | solution.py:447
  200.4 35.8 %collective-permute-start.11 = (bf16[512,1024]{1,0:T(8,128)(2,1)}, bf16[512,1024]{1,0:T(8,128)(2,1)}, u32[]{:S(2)}, u32[]{:S(2)}) collective-permute-start(bf16[512,1024]{1,0:T(8,128)(2,1)} %bitcast.285), channel_id=1, source_target_pairs={{0,16},{16,0},{1,17},{17,1},{2,18},{18,2},{3,19},{19,3},{4,20},{20... | collective-permute-start | bytes 3145736 | tf_op jit(solution)/shard_map/ppermute | solution.py:447
  219.7 57.6 %collective-permute-start.17 = (bf16[512,1024]{1,0:T(8,128)(2,1)}, bf16[512,1024]{1,0:T(8,128)(2,1)}, u32[]{:S(2)}, u32[]{:S(2)}) collective-permute-start(bf16[512,1024]{1,0:T(8,128)(2,1)} %bitcast.48), channel_id=1, source_target_pairs={{0,16},{16,0},{1,17},{17,1},{2,18},{18,2},{3,19},{19,3},{4,20},{20... | collective-permute-start | bytes 3145736 | tf_op jit(solution)/shard_map/ppermute | solution.py:447
  220.9 77.6 %collective-permute-start.18 = (bf16[512,1024]{1,0:T(8,128)(2,1)}, bf16[512,1024]{1,0:T(8,128)(2,1)}, u32[]{:S(2)}, u32[]{:S(2)}) collective-permute-start(bf16[512,1024]{1,0:T(8,128)(2,1)} %bitcast.48), channel_id=1, source_target_pairs={{0,1},{1,0},{2,3},{3,2},{4,5},{5,4},{6,7},{7,6},{8,9},{9,8},{10,11... | collective-permute-start | bytes 3145736 | tf_op jit(solution)/shard_map/ppermute | solution.py:447
  238.3 44.9 %all-to-all-start.4 = ((bf16[8,128,256]{1,2,0:T(8,128)(2,1)}), bf16[8,128,256]{1,2,0:T(8,128)(2,1)}, u32[]{:S(2)}, u32[]{:S(2)}) async-start(bf16[8,128,256]{1,2,0:T(8,128)(2,1)} %copy.301), calls=%async_computation.4 | async-start | bytes 1048576 | tf_op jit(solution)/shard_map/all_to_all | solution.py:80
  243.1 426.4 %reduce-scatter.4.cloned.1.call-start = ((), (), s32[]{:S(2)}) async-start(), calls=%async_computation.17 | async-start | bytes 5242880 | tf_op jit(solution)/shard_map/reduce_scatter | solution.py:560
  277.2 31.5 %collective-permute-start.19 = (bf16[512,1024]{1,0:T(8,128)(2,1)}, bf16[512,1024]{1,0:T(8,128)(2,1)}, u32[]{:S(2)}, u32[]{:S(2)}) collective-permute-start(bf16[512,1024]{1,0:T(8,128)(2,1)} %collective-permute-done.17), channel_id=1, source_target_pairs={{0,1},{1,0},{2,3},{3,2},{4,5},{5,4},{6,7},{7,6},{8,9},{9,8},{10,11... | collective-permute-start | bytes 3145736 | tf_op jit(solution)/shard_map/ppermute | solution.py:515
  277.3 33.9 %collective-permute-start.16 = (bf16[512,1024]{1,0:T(8,128)(2,1)}, bf16[512,1024]{1,0:T(8,128)(2,1)}, u32[]{:S(2)}, u32[]{:S(2)}) collective-permute-start(bf16[512,1024]{1,0:T(8,128)(2,1)} %collective-permute-done.10), channel_id=1, source_target_pairs={{0,16},{16,0},{1,17},{17,1},{2,18},{18,2},{3,19},{19,3},{4,20},{20... | collective-permute-start | bytes 3145736 | tf_op jit(solution)/shard_map/ppermute | solution.py:512
  288.4 21.6 %collective-permute-start.21 = (bf16[128,2048]{1,0:T(8,128)(2,1)S(1)}, bf16[128,2048]{1,0:T(8,128)(2,1)}, u32[]{:S(2)}, u32[]{:S(2)}) collective-permute-start(bf16[128,2048]{1,0:T(8,128)(2,1)S(1)} %fusion.15.part), channel_id=1, source_target_pairs={{0,2},{2,6},{6,4},{4,0},{1,3},{3,7},{7,5},{5,1},{8,10},{10,14},{14... | collective-permute-start | bytes 1572872 | tf_op jit(solution)/shard_map/ppermute | solution.py:385
  289.2 26.2 %collective-permute-start.15 = (bf16[128,2048]{1,0:T(8,128)(2,1)S(1)}, bf16[128,2048]{1,0:T(8,128)(2,1)S(1)}, u32[]{:S(2)}, u32[]{:S(2)}) collective-permute-start(bf16[128,2048]{1,0:T(8,128)(2,1)S(1)} %fusion.15.part), channel_id=1, source_target_pairs={{0,8},{8,0},{1,9},{9,1},{2,10},{10,2},{3,11},{11,3},{4,12},{12,4},... | collective-permute-start | bytes 1572872 | tf_op jit(solution)/shard_map/ppermute | solution.py:97
  314.9 21.5 %collective-permute-start.22 = (bf16[128,2048]{1,0:T(8,128)(2,1)}, bf16[128,2048]{1,0:T(8,128)(2,1)}, u32[]{:S(2)}, u32[]{:S(2)}) collective-permute-start(bf16[128,2048]{1,0:T(8,128)(2,1)} %collective-permute-done.21.part), channel_id=1, source_target_pairs={{0,2},{2,6},{6,4},{4,0},{1,3},{3,7},{7,5},{5,1},{8,10},{10,14},{14... | collective-permute-start | bytes 1572872 | tf_op jit(solution)/shard_map/ppermute | solution.py:385
  377.6 22.4 %collective-permute-start.20 = (bf16[128,2048]{1,0:T(8,128)(2,1)}, bf16[128,2048]{1,0:T(8,128)(2,1)}, u32[]{:S(2)}, u32[]{:S(2)}) collective-permute-start(bf16[128,2048]{1,0:T(8,128)(2,1)} %get-tuple-element.102), channel_id=1, source_target_pairs={{0,8},{8,0},{1,9},{9,1},{2,10},{10,2},{3,11},{11,3},{4,12},{12,4},... | collective-permute-start | bytes 1572872 | tf_op jit(solution)/shard_map/ppermute | solution.py:97
  487.1 220.3 %reduce-scatter.6.cloned.1.call-start = ((), (), s32[]{:S(2)}) async-start(), calls=%async_computation.18 | async-start | bytes 5242880 | tf_op jit(solution)/shard_map/reduce_scatter | solution.py:560
  541.6 26.6 %collective-permute-start.47 = (bf16[128,2048]{0,1:T(8,128)(2,1)}, bf16[128,2048]{0,1:T(8,128)(2,1)}, u32[]{:S(2)}, u32[]{:S(2)}) collective-permute-start(bf16[128,2048]{0,1:T(8,128)(2,1)} %bitcast.72), channel_id=1, source_target_pairs={{0,1},{1,0},{2,3},{3,2},{4,5},{5,4},{6,7},{7,6},{8,9},{9,8},{10,11... | collective-permute-start | bytes 1572872 | tf_op jit(solution)/shard_map/ppermute | solution.py:390
  544.4 27.7 %all-to-all-start.6 = ((bf16[8,128,256]{2,1,0:T(8,128)(2,1)}), bf16[8,128,256]{2,1,0:T(8,128)(2,1)}, u32[]{:S(2)}, u32[]{:S(2)}) async-start(bf16[8,128,256]{2,1,0:T(8,128)(2,1)} %bitcast.294), calls=%async_computation.6 | async-start | bytes 1048576 | tf_op jit(solution)/shard_map/all_to_all | solution.py:80
  549.5 243.5 %reduce-scatter.8.cloned.1.call-start = ((), (), s32[]{:S(2)}) async-start(), calls=%async_computation.19 | async-start | bytes 5242880 | tf_op jit(solution)/shard_map/reduce_scatter | solution.py:560
  567.0 36.5 %collective-permute-start.49 = (bf16[128,2048]{0,1:T(8,128)(2,1)}, bf16[128,2048]{0,1:T(8,128)(2,1)}, u32[]{:S(2)}, u32[]{:S(2)}) collective-permute-start(bf16[128,2048]{0,1:T(8,128)(2,1)} %collective-permute-done.48), channel_id=1, source_target_pairs={{0,1},{1,0},{2,3},{3,2},{4,5},{5,4},{6,7},{7,6},{8,9},{9,8},{10,11... | collective-permute-start | bytes 1572872 | tf_op jit(solution)/shard_map/ppermute | solution.py:390
  576.8 28.6 %collective-permute-start.52 = (bf16[128,2048]{0,1:T(8,128)(2,1)}, bf16[128,2048]{0,1:T(8,128)(2,1)}, u32[]{:S(2)}, u32[]{:S(2)}) collective-permute-start(bf16[128,2048]{0,1:T(8,128)(2,1)} %collective-permute-done.50), channel_id=1, source_target_pairs={{0,2},{2,6},{6,4},{4,0},{1,3},{3,7},{7,5},{5,1},{8,10},{10,14},{14... | collective-permute-start | bytes 1572872 | tf_op jit(solution)/shard_map/ppermute | solution.py:385
  602.7 20.8 %collective-permute-start.51 = (bf16[128,2048]{0,1:T(8,128)(2,1)}, bf16[128,2048]{0,1:T(8,128)(2,1)S(1)}, u32[]{:S(2)}, u32[]{:S(2)}) collective-permute-start(bf16[128,2048]{0,1:T(8,128)(2,1)} %collective-permute-done.50), channel_id=1, source_target_pairs={{0,1},{1,0},{2,3},{3,2},{4,5},{5,4},{6,7},{7,6},{8,9},{9,8},{10,11... | collective-permute-start | bytes 1572872 | tf_op jit(solution)/shard_map/ppermute | solution.py:390
  605.4 29.8 %collective-permute-start.53 = (bf16[128,2048]{0,1:T(8,128)(2,1)}, bf16[128,2048]{0,1:T(8,128)(2,1)S(1)}, u32[]{:S(2)}, u32[]{:S(2)}) collective-permute-start(bf16[128,2048]{0,1:T(8,128)(2,1)} %collective-permute-done.52), channel_id=1, source_target_pairs={{0,1},{1,0},{2,3},{3,2},{4,5},{5,4},{6,7},{7,6},{8,9},{9,8},{10,11... | collective-permute-start | bytes 1572872 | tf_op jit(solution)/shard_map/ppermute | solution.py:390
  647.0 77.8 %collective-permute-start.54 = (bf16[128,2048]{1,0:T(8,128)(2,1)}, bf16[128,2048]{1,0:T(8,128)(2,1)}, u32[]{:S(2)}, u32[]{:S(2)}) collective-permute-start(bf16[128,2048]{1,0:T(8,128)(2,1)} %pad_maximum_fusion.5), channel_id=1, source_target_pairs={{0,8},{8,0},{1,9},{9,1},{2,10},{10,2},{3,11},{11,3},{4,12},{12,4},... | collective-permute-start | bytes 1572872 | tf_op jit(solution)/shard_map/ppermute | solution.py:97
  667.7 53.3 %collective-permute-start.64 = (bf16[1024,768]{1,0:T(8,128)(2,1)}, bf16[1024,768]{1,0:T(8,128)(2,1)}, u32[]{:S(2)}, u32[]{:S(2)}) collective-permute-start(bf16[1024,768]{1,0:T(8,128)(2,1)} %pad_maximum_fusion.1), channel_id=1, source_target_pairs={{0,8},{8,0},{1,9},{9,1},{2,10},{10,2},{3,11},{11,3},{4,12},{12,4},... | collective-permute-start | bytes 4718600 | tf_op jit(solution)/shard_map/ppermute | solution.py:97
  669.6 29.7 %all-to-all-start.8 = ((bf16[8,64,1024]{2,1,0:T(8,128)(2,1)}), bf16[8,64,1024]{2,1,0:T(8,128)(2,1)}, u32[]{:S(2)}, u32[]{:S(2)}) async-start(bf16[8,64,1024]{2,1,0:T(8,128)(2,1)} %bitcast.313), calls=%async_computation.9 | async-start | bytes 2097152 | tf_op jit(solution)/shard_map/all_to_all | solution.py:80
  678.7 108.8 %collective-permute-start.58 = (bf16[128,2048]{1,0:T(8,128)(2,1)}, bf16[128,2048]{1,0:T(8,128)(2,1)}, u32[]{:S(2)}, u32[]{:S(2)}) collective-permute-start(bf16[128,2048]{1,0:T(8,128)(2,1)} %fusion.11), channel_id=1, source_target_pairs={{0,1},{1,0},{2,3},{3,2},{4,5},{5,4},{6,7},{7,6},{8,9},{9,8},{10,11... | collective-permute-start | bytes 1572872 | tf_op jit(solution)/shard_map/ppermute | solution.py:434
  681.2 23.6 %collective-permute-start.60 = (bf16[128,2048]{1,0:T(8,128)(2,1)}, bf16[128,2048]{1,0:T(8,128)(2,1)}, u32[]{:S(2)}, u32[]{:S(2)}) collective-permute-start(bf16[128,2048]{1,0:T(8,128)(2,1)} %fusion.13), channel_id=1, source_target_pairs={{0,1},{1,0},{2,3},{3,2},{4,5},{5,4},{6,7},{7,6},{8,9},{9,8},{10,11... | collective-permute-start | bytes 1572872 | tf_op jit(solution)/shard_map/ppermute | solution.py:434
  685.4 42.3 %collective-permute-start.59 = (bf16[128,2048]{1,0:T(8,128)(2,1)}, bf16[128,2048]{1,0:T(8,128)(2,1)}, u32[]{:S(2)}, u32[]{:S(2)}) collective-permute-start(bf16[128,2048]{1,0:T(8,128)(2,1)} %fusion.12), channel_id=1, source_target_pairs={{0,1},{1,0},{2,3},{3,2},{4,5},{5,4},{6,7},{7,6},{8,9},{9,8},{10,11... | collective-permute-start | bytes 1572872 | tf_op jit(solution)/shard_map/ppermute | solution.py:434
  707.1 20.6 %collective-permute-start.61 = (bf16[128,2048]{1,0:T(8,128)(2,1)}, bf16[128,2048]{1,0:T(8,128)(2,1)}, u32[]{:S(2)}, u32[]{:S(2)}) collective-permute-start(bf16[128,2048]{1,0:T(8,128)(2,1)} %fusion), channel_id=1, source_target_pairs={{0,2},{2,6},{6,4},{4,0},{1,3},{3,7},{7,5},{5,1},{8,10},{10,14},{14... | collective-permute-start | bytes 1572872 | tf_op jit(solution)/shard_map/ppermute | solution.py:385
  715.8 29.2 %all-to-all-start.11 = ((bf16[8,64,1024]{2,1,0:T(8,128)(2,1)}), bf16[8,64,1024]{2,1,0:T(8,128)(2,1)}, u32[]{:S(2)}, u32[]{:S(2)}) async-start(bf16[8,64,1024]{2,1,0:T(8,128)(2,1)} %bitcast.312), calls=%async_computation.13 | async-start | bytes 2097152 | tf_op jit(solution)/shard_map/all_to_all | solution.py:80
  727.5 23.5 %collective-permute-start.55 = (bf16[64,2048]{1,0:T(8,128)(2,1)}, bf16[64,2048]{1,0:T(8,128)(2,1)}, u32[]{:S(2)}, u32[]{:S(2)}) collective-permute-start(bf16[64,2048]{1,0:T(8,128)(2,1)} %constant_dynamic-slice_fusion.8), channel_id=1, source_target_pairs={{0,16},{16,0},{1,17},{17,1},{2,18},{18,2},{3,19},{19,3},{4,20},{20... | collective-permute-start | bytes 786440 | tf_op jit(solution)/shard_map/ppermute | solution.py:579
  729.9 57.7 %collective-permute-start.62 = (bf16[128,2048]{1,0:T(8,128)(2,1)}, bf16[128,2048]{1,0:T(8,128)(2,1)}, u32[]{:S(2)}, u32[]{:S(2)}) collective-permute-start(bf16[128,2048]{1,0:T(8,128)(2,1)} %fusion.2), channel_id=1, source_target_pairs={{0,2},{2,6},{6,4},{4,0},{1,3},{3,7},{7,5},{5,1},{8,10},{10,14},{14... | collective-permute-start | bytes 1572872 | tf_op jit(solution)/shard_map/ppermute | solution.py:385
  745.0 48.0 %all-to-all-start.9 = ((bf16[8,64,768]{2,1,0:T(8,128)(2,1)}), bf16[8,64,768]{2,1,0:T(8,128)(2,1)}, u32[]{:S(2)}, u32[]{:S(2)}) async-start(bf16[8,64,768]{2,1,0:T(8,128)(2,1)} %bitcast.287), calls=%async_computation.10 | async-start | bytes 1572864 | tf_op jit(solution)/shard_map/all_to_all | solution.py:80
  752.8 33.0 %collective-permute-start.56 = (bf16[64,2048]{1,0:T(8,128)(2,1)}, bf16[64,2048]{1,0:T(8,128)(2,1)}, u32[]{:S(2)}, u32[]{:S(2)}) collective-permute-start(bf16[64,2048]{1,0:T(8,128)(2,1)} %add_convert_fusion.6), channel_id=1, source_target_pairs={{0,0},{1,4},{2,8},{3,12},{4,16},{5,20},{6,24},{7,28},{8,1},{9,5},{... | collective-permute-start | bytes 786440 | tf_op jit(solution)/shard_map/ppermute | solution.py:615
  790.1 20.3 %collective-permute-start.63 = (bf16[128,2048]{1,0:T(8,128)(2,1)}, bf16[128,2048]{1,0:T(8,128)(2,1)}, u32[]{:S(2)}, u32[]{:S(2)}) collective-permute-start(bf16[128,2048]{1,0:T(8,128)(2,1)} %fusion.4), channel_id=1, source_target_pairs={{0,2},{2,6},{6,4},{4,0},{1,3},{3,7},{7,5},{5,1},{8,10},{10,14},{14... | collective-permute-start | bytes 1572872 | tf_op jit(solution)/shard_map/ppermute | solution.py:385
  793.1 33.0 %all-to-all-start.12 = ((bf16[8,64,1024]{2,1,0:T(8,128)(2,1)}), bf16[8,64,1024]{2,1,0:T(8,128)(2,1)}, u32[]{:S(2)}, u32[]{:S(2)}) async-start(bf16[8,64,1024]{2,1,0:T(8,128)(2,1)} %bitcast.314), calls=%async_computation.15 | async-start | bytes 2097152 | tf_op jit(solution)/shard_map/all_to_all | solution.py:80
  (127 other events, 970.4 us)
Sparse Core Ops, SparseCore 0:
  199.0 90.4 all-gather.1
  487.2 52.5 reduce-scatter.3
  543.1 78.0 reduce-scatter.5
  624.0 56.5 reduce-scatter.7

commit v5 on v4

--- a/solution.py
+++ b/solution.py
@@ -222,7 +222,7 @@
         + doc_specs,
         out_specs=[part(0), part(0), part(0), each, part(0)],
         out_shape=[low, low, low, jax.ShapeDtypeStruct((heads, length, 1), F32), low],
-        compiler_params=pltpu.CompilerParams(vmem_limit_bytes=24 * 1024 * 1024),
+        compiler_params=pltpu.CompilerParams(vmem_limit_bytes=58 * 1024 * 1024),
         cost_estimate=pl.CostEstimate(
             flops=3 * pairs, bytes_accessed=qkv.size * 6, transcendentals=heads * length * length
         ),
@@ -247,7 +247,7 @@
         out_specs=[part(0), part(0), part(0), each, each],
         out_shape=[flat, flat, low, line, line],
         scratch_shapes=[pltpu.VMEM((length, HEAD_DIM), F32)] * 2,
-        compiler_params=pltpu.CompilerParams(vmem_limit_bytes=24 * 1024 * 1024),
+        compiler_params=pltpu.CompilerParams(vmem_limit_bytes=58 * 1024 * 1024),
         cost_estimate=pl.CostEstimate(
             flops=7 * pairs, bytes_accessed=qkv.size * 8, transcendentals=heads * length * length
         ),
@@ -580,7 +580,7 @@
         return (of(term, x_at).astype(F32) + away.astype(F32)).astype(BF16)
 
     (g_res, g_gate, g_up), grad_ffn = feed_pass(
-        grad_result.astype(BF16), (gate, upward), feed_back_kernel, (BF16, BF16)
+        grad_result.astype(BF16), (gate, upward), feed_back_kernel, (BF16, BF16), (output,)
     )
     grad_hidden = grad_top + grad_ffn
     term_d = token_sum(g_res, active)

time: 849 us -> 843 us (level)
  local copies, waits for them, and re-layouts: 202 us -> 181 us
  waiting for transfers between devices: 293 us -> 304 us
    unnamed x214 -> x184, local copies, waits for them, and re-layouts: 80.8 us -> 61.8 us
  transfers between devices with their start and end apart: 83 -> 83, of which waited for: 33 -> 34; matrix products, arithmetic and copies ran while one was open for 30% -> 30% of each run, Pallas kernels for 7% -> 8%
where the time goes in v5:
time: 843 us; the launch traced here: 831 us
  waiting for transfers between devices  304 us (36%)
  local copies, waits for them, and re-layouts  181 us (21%)
  starting transfers between devices  133 us (16%)
  Pallas kernels  78.8 us (9%)
  other arithmetic  58.8 us (7%)
  matrix products  54.6 us (6%)
  between operations  21 us (2%)
    ppermute x21, waiting for transfers between devices, ring_send(): return lax.ppermute(part, 'z', ring)  109 us
    all_to_all x13, starting transfers between devices, exchange(): lax.all_to_all(array_in, axes, split_axis=0, concat_axis=0, tiled=True)  78 us
    unnamed x184, local copies, waits for them, and re-layouts  61.8 us
    all_to_all x13, waiting for transfers between devices, exchange(): lax.all_to_all(array_in, axes, split_axis=0, concat_axis=0, tiled=True)  57.5 us
    pallas_call x8, Pallas kernels, feed_step(): pl.pallas_call(kernel, grid=(feed // step,), in_specs=[part, part] + [pl....  56 us
    ppermute x4, waiting for transfers between devices, rest_send(): return (mine, lax.ppermute(mine, 'y', SWAP), lax.ppermute(mine, 'x', SWAP))  45 us
    dot_general x5, matrix products, dot_left_t(): lax.dot_general(left_mat, right_mat, (((0,), (0,)), ((), ())), preferred_...  33.3 us
    ppermute x22, starting transfers between devices, core_swap(): return lax.ppermute(array_in, 'core', SWAP)  25.8 us
  transfers between devices with their start and end apart: 83, of which 34 were waited for; matrix products, arithmetic and copies ran while one was open for 30% of the time, Pallas kernels for 8%

profile of v5, /device:TPU:25, one launch (start us, length us, event | category | flops | bytes accessed | tf_op | source)
XLA Modules:
  0.0 830.9 jit_solution(17828349835970065994)
XLA Ops:
  42.7 6.0 all-to-all-done
  48.7 6.7 all-to-all-start.2
  61.0 15.3 %collective-permute-done.3 = bf16[192,2048]{1,0:T(8,128)(2,1)S(1)} collective-permute-done((bf16[192,2048]{1,0:T(8,128)(2,1)}, bf16[192,2048]{1,0:T(8,128)(2,1)S(1)}, u32[]{:S(2)}, u32[]{:S(2)}) %collective-permute-start.3) | collective-permute-done | bytes 786464 | tf_op jit(solution)/shard_map/ppermute | solution.py:385
  80.5 14.4 %collective-permute-done.5 = bf16[192,2048]{1,0:T(8,128)(2,1)S(1)} collective-permute-done((bf16[192,2048]{1,0:T(8,128)(2,1)S(1)}, bf16[192,2048]{1,0:T(8,128)(2,1)S(1)}, u32[]{:S(2)}, u32[]{:S(2)}) %collective-permute-start.5) | collective-permute-done | bytes 786464 | tf_op jit(solution)/shard_map/ppermute | solution.py:385
  98.1 13.4 %collective-permute-done.6 = bf16[192,2048]{1,0:T(8,128)(2,1)S(1)} collective-permute-done((bf16[192,2048]{1,0:T(8,128)(2,1)S(1)}, bf16[192,2048]{1,0:T(8,128)(2,1)S(1)}, u32[]{:S(2)}, u32[]{:S(2)}) %collective-permute-start.6) | collective-permute-done | bytes 786464 | tf_op jit(solution)/shard_map/ppermute | solution.py:398
  119.3 5.7 all-to-all-start.1
  130.7 8.6 %all-to-all-start.3 = ((bf16[8,2,64,1024]{3,2,1,0:T(8,128)(2,1)}), bf16[8,2,64,1024]{3,2,1,0:T(8,128)(2,1)S(1)}, u32[]{:S(2)}, u32[]{:S(2)}) async-start(bf16[8,2,64,1024]{3,2,1,0:T(8,128)(2,1)} %copy.300), calls=%async_computation.3 | async-start | bytes 4194304 | tf_op jit(solution)/shard_map/all_to_all | solution.py:80
  165.5 20.3 %all-to-all-done.3 = bf16[8,2,64,1024]{3,2,1,0:T(8,128)(2,1)S(1)} async-done(((bf16[8,2,64,1024]{3,2,1,0:T(8,128)(2,1)}), bf16[8,2,64,1024]{3,2,1,0:T(8,128)(2,1)S(1)}, u32[]{:S(2)}, u32[]{:S(2)}) %all-to-all-start.3) | async-done | bytes 2097184 | tf_op jit(solution)/shard_map/all_to_all | solution.py:80
  185.7 6.8 all-to-all-start.5
  208.9 9.8 %shard_map.246 = (bf16[1024,256]{1,0:T(8,128)(2,1)}, bf16[1024,256]{1,0:T(8,128)(2,1)}, bf16[1024,256]{1,0:T(8,128)(2,1)}, f32[2,1024,1]{2,1,0:T(8,128)}, bf16[1024,256]{1,0:T(8,128)(2,1)}) custom-call(f32[1024,768]{1,0:T(8,128)} %copy-done.23, f32[1024,768]{1,0:T(8,128)} %copy-done.23, f32[1024,768]{1,0:T(8,128)} %copy-done.23, ...), custom_call_target="tpu_custom_call" | custom-call | flops 805306368 | bytes 4718592 | tf_op jit(solution)/shard_map/pallas_call | solution.py:217
  223.4 11.4 %collective-permute-done.10 = bf16[512,1024]{1,0:T(8,128)(2,1)} collective-permute-done((bf16[512,1024]{1,0:T(8,128)(2,1)}, bf16[512,1024]{1,0:T(8,128)(2,1)}, u32[]{:S(2)}, u32[]{:S(2)}) %collective-permute-start.10) | collective-permute-done | bytes 1048608 | tf_op jit(solution)/shard_map/ppermute | solution.py:447
  244.6 32.7 %collective-permute-done.17 = bf16[512,1024]{1,0:T(8,128)(2,1)} collective-permute-done((bf16[512,1024]{1,0:T(8,128)(2,1)}, bf16[512,1024]{1,0:T(8,128)(2,1)}, u32[]{:S(2)}, u32[]{:S(2)}) %collective-permute-start.17) | collective-permute-done | bytes 1048608 | tf_op jit(solution)/shard_map/ppermute | solution.py:447
  297.7 10.1 %collective-permute-done.19 = bf16[512,1024]{1,0:T(8,128)(2,1)} collective-permute-done((bf16[512,1024]{1,0:T(8,128)(2,1)}, bf16[512,1024]{1,0:T(8,128)(2,1)}, u32[]{:S(2)}, u32[]{:S(2)}) %collective-permute-start.19) | collective-permute-done | bytes 1048608 | tf_op jit(solution)/shard_map/ppermute | solution.py:515
  318.4 7.8 shard_map.247
  326.2 7.2 shard_map.248
  336.7 7.0 shard_map.249
  350.7 9.1 %collective-permute-done.29 = bf16[128,2048]{1,0:T(8,128)(2,1)S(1)} collective-permute-done((bf16[128,2048]{1,0:T(8,128)(2,1)S(1)}, bf16[128,2048]{1,0:T(8,128)(2,1)S(1)}, u32[]{:S(2)}, u32[]{:S(2)}) %collective-permute-start.29) | collective-permute-done | bytes 524320 | tf_op jit(solution)/shard_map/ppermute | solution.py:385
  360.0 6.9 shard_map.250
  376.5 12.2 %collective-permute-done.31 = bf16[128,2048]{1,0:T(8,128)(2,1)S(1)} collective-permute-done((bf16[128,2048]{1,0:T(8,128)(2,1)S(1)}, bf16[128,2048]{1,0:T(8,128)(2,1)S(1)}, u32[]{:S(2)}, u32[]{:S(2)}) %collective-permute-start.31) | collective-permute-done | bytes 524320 | tf_op jit(solution)/shard_map/ppermute | solution.py:385
  395.7 7.9 collective-permute-done.32
  407.9 10.9 %collective-permute-done.35.part = bf16[128,2048]{1,0:T(8,128)(2,1)S(1)} collective-permute-done((bf16[128,2048]{1,0:T(8,128)(2,1)S(1)}, bf16[128,2048]{1,0:T(8,128)(2,1)S(1)}, u32[]{:S(2)}, u32[]{:S(2)}) %collective-permute-start.35) | collective-permute-done | bytes 524320 | tf_op jit(solution)/shard_map/ppermute | solution.py:385
  423.6 6.8 shard_map.251
  431.4 6.8 shard_map.252
  440.9 6.8 shard_map.253
  454.5 9.9 %collective-permute-done.43 = bf16[128,2048]{1,0:T(8,128)(2,1)S(1)} collective-permute-done((bf16[128,2048]{1,0:T(8,128)(2,1)S(1)}, bf16[128,2048]{1,0:T(8,128)(2,1)S(1)}, u32[]{:S(2)}, u32[]{:S(2)}) %collective-permute-start.43) | collective-permute-done | bytes 524320 | tf_op jit(solution)/shard_map/ppermute | solution.py:385
  465.4 6.8 shard_map.254
  475.6 6.1 convolution_convert_fusion
  483.3 8.3 %convolution_convert_fusion.2 = bf16[2048,1024]{1,0:T(8,128)(2,1)} fusion(bf16[1024,2048]{1,0:T(8,128)(2,1)} %copy-done.7, bf16[1024,1024]{1,0:T(8,128)(2,1)S(1)} %copy-done.9), kind=kOutput, calls=%fused_computation.2 | convolution fusion | flops 4297064448 | bytes 10485760 | tf_op jit(solution)/shard_map/dot_general | solution.py:40
  502.5 5.8 collective-permute-done.45
  516.6 5.9 collective-permute-done.46
  525.4 7.2 convolution_convert_fusion.5
  544.8 8.8 %convolution_convert_fusion.1 = bf16[2048,1024]{1,0:T(8,128)(2,1)} fusion(bf16[1024,2048]{1,0:T(8,128)(2,1)} %copy-done.7, bf16[1024,1024]{1,0:T(8,128)(2,1)S(1)} %copy-done.11), kind=kOutput, calls=%fused_computation.1 | convolution fusion | flops 4297064448 | bytes 10485760 | tf_op jit(solution)/shard_map/dot_general | solution.py:40
  562.7 9.3 %collective-permute-done.50 = bf16[128,2048]{0,1:T(8,128)(2,1)S(1)} collective-permute-done((bf16[128,2048]{0,1:T(8,128)(2,1)}, bf16[128,2048]{0,1:T(8,128)(2,1)S(1)}, u32[]{:S(2)}, u32[]{:S(2)}) %collective-permute-start.50) | collective-permute-done | bytes 524320 | tf_op jit(solution)/shard_map/ppermute | solution.py:385
  571.9 13.0 %shard_map.255 = (f32[1024,256]{1,0:T(8,128)}, f32[1024,256]{1,0:T(8,128)}, bf16[1024,256]{1,0:T(8,128)(2,1)}, f32[2,1024,1]{2,1,0:T(8,128)}, f32[2,1024,1]{2,1,0:T(8,128)}) custom-call(bf16[1024,256]{1,0:T(8,128)(2,1)} %get-tuple-element.150.refs_0_, bf16[1024,256]{1,0:T(8,128)(2,1)} %get-tuple-element.151.refs_1_, ...), custom_call_target="tpu_custom_call" | custom-call | flops 1879048192 | bytes 6291456 | tf_op jit(solution)/shard_map/pallas_call | solution.py:241
  591.2 6.3 collective-permute-done.51
  599.3 19.0 %collective-permute-done.53 = bf16[128,2048]{0,1:T(8,128)(2,1)S(1)} collective-permute-done((bf16[128,2048]{0,1:T(8,128)(2,1)S(1)}, bf16[128,2048]{0,1:T(8,128)(2,1)S(1)}, u32[]{:S(2)}, u32[]{:S(2)}) %collective-permute-start.53) | collective-permute-done | bytes 524320 | tf_op jit(solution)/shard_map/ppermute | solution.py:390
  620.0 6.4 all-to-all-start.7
  631.9 6.0 collective-permute-start.54
  644.8 6.4 convolution_convert_fusion.3
  673.3 11.8 %all-to-all-done.8 = bf16[8,64,1024]{2,1,0:T(8,128)(2,1)} async-done(((bf16[8,64,1024]{2,1,0:T(8,128)(2,1)}), bf16[8,64,1024]{2,1,0:T(8,128)(2,1)}, u32[]{:S(2)}, u32[]{:S(2)}) %all-to-all-start.8) | async-done | bytes 1048608 | tf_op jit(solution)/shard_map/all_to_all | solution.py:80
  685.1 5.6 all-to-all-start.10
  690.7 8.5 %collective-permute-done.60 = bf16[128,2048]{1,0:T(8,128)(2,1)} collective-permute-done((bf16[128,2048]{1,0:T(8,128)(2,1)}, bf16[128,2048]{1,0:T(8,128)(2,1)}, u32[]{:S(2)}, u32[]{:S(2)}) %collective-permute-start.60) | collective-permute-done | bytes 524320 | tf_op jit(solution)/shard_map/ppermute | solution.py:434
  701.8 9.0 %all-to-all-done.10 = f32[32,1,256]{2,1,0:T(1,128)} async-done(((f32[32,1,256]{2,1,0:T(1,128)}), f32[32,1,256]{2,1,0:T(1,128)}, u32[]{:S(2)}, u32[]{:S(2)}) %all-to-all-start.10) | async-done | bytes 32800 | tf_op jit(solution)/shard_map/all_to_all | solution.py:80
  725.1 12.2 %collective-permute-done.65 = bf16[512,768]{1,0:T(8,128)(2,1)S(1)} collective-permute-done((bf16[512,768]{1,0:T(8,128)(2,1)S(1)}, bf16[512,768]{1,0:T(8,128)(2,1)S(1)}, u32[]{:S(2)}, u32[]{:S(2)}) %collective-permute-start.65) | collective-permute-done | bytes 786464 | tf_op jit(solution)/shard_map/ppermute | solution.py:579
  740.0 6.2 all-to-all-start.9
  765.4 14.6 %collective-permute-done.56 = bf16[64,2048]{1,0:T(8,128)(2,1)} collective-permute-done((bf16[64,2048]{1,0:T(8,128)(2,1)}, bf16[64,2048]{1,0:T(8,128)(2,1)}, u32[]{:S(2)}, u32[]{:S(2)}) %collective-permute-start.56) | collective-permute-done | bytes 262176 | tf_op jit(solution)/shard_map/ppermute | solution.py:615
  787.3 7.0 all-to-all-start.12
  814.0 7.1 all-to-all-done.12
  (498 shorter events, 352.1 us)
Async XLA Ops:
  11.7 29.1 %collective-permute-start = (bf16[192,2048]{1,0:T(8,128)(2,1)}, bf16[192,2048]{1,0:T(8,128)(2,1)}, u32[]{:S(2)}, u32[]{:S(2)}) collective-permute-start(bf16[192,2048]{1,0:T(8,128)(2,1)} %pad_maximum_fusion.2), channel_id=1, source_target_pairs={{0,1},{1,0},{2,3},{3,2},{4,5},{5,4},{6,7},{7,6},{8,9},{9,8},{10,11... | collective-permute-start | bytes 2359304 | tf_op jit(solution)/shard_map/ppermute | solution.py:398
  12.9 26.7 %collective-permute-start.1 = (bf16[192,2048]{1,0:T(8,128)(2,1)}, bf16[192,2048]{1,0:T(8,128)(2,1)}, u32[]{:S(2)}, u32[]{:S(2)}) collective-permute-start(bf16[192,2048]{1,0:T(8,128)(2,1)} %pad_maximum_fusion.2), channel_id=1, source_target_pairs={{0,2},{2,6},{6,4},{4,0},{1,3},{3,7},{7,5},{5,1},{8,10},{10,14},{14... | collective-permute-start | bytes 2359304 | tf_op jit(solution)/shard_map/ppermute | solution.py:385
  18.1 30.7 %all-to-all-start = ((bf16[8,64,768]{2,1,0:T(8,128)(2,1)}), bf16[8,64,768]{2,1,0:T(8,128)(2,1)S(1)}, u32[]{:S(2)}, u32[]{:S(2)}) async-start(bf16[8,64,768]{2,1,0:T(8,128)(2,1)} %reshape.350), calls=%async_computation | async-start | bytes 1572864 | tf_op jit(solution)/shard_map/all_to_all | solution.py:80
  39.7 20.4 %collective-permute-start.2 = (bf16[192,2048]{1,0:T(8,128)(2,1)}, bf16[192,2048]{1,0:T(8,128)(2,1)S(1)}, u32[]{:S(2)}, u32[]{:S(2)}) collective-permute-start(bf16[192,2048]{1,0:T(8,128)(2,1)} %collective-permute-done.1), channel_id=1, source_target_pairs={{0,1},{1,0},{2,3},{3,2},{4,5},{5,4},{6,7},{7,6},{8,9},{9,8},{10,11... | collective-permute-start | bytes 2359304 | tf_op jit(solution)/shard_map/ppermute | solution.py:398
  48.7 69.5 %all-to-all-start.2 = ((bf16[32,2,128]{2,1,0:T(2,128)(2,1)}), bf16[32,2,128]{2,1,0:T(2,128)(2,1)S(1)}, u32[]{:S(2)}, u32[]{:S(2)}) async-start(bf16[32,2,128]{2,1,0:T(2,128)(2,1)} %reshape.388), calls=%async_computation.2 | async-start | bytes 32768 | tf_op jit(solution)/shard_map/all_to_all | solution.py:80
  55.5 22.3 %collective-permute-start.8 = (bf16[512,768]{1,0:T(8,128)(2,1)S(1)}, bf16[512,768]{1,0:T(8,128)(2,1)S(1)}, u32[]{:S(2)}, u32[]{:S(2)}) collective-permute-start(bf16[512,768]{1,0:T(8,128)(2,1)S(1)} %bitcast.281), channel_id=1, source_target_pairs={{0,16},{16,0},{1,17},{17,1},{2,18},{18,2},{3,19},{19,3},{4,20},{20... | collective-permute-start | bytes 2359304 | tf_op jit(solution)/shard_map/ppermute | solution.py:415
  56.7 19.6 %collective-permute-start.3 = (bf16[192,2048]{1,0:T(8,128)(2,1)}, bf16[192,2048]{1,0:T(8,128)(2,1)S(1)}, u32[]{:S(2)}, u32[]{:S(2)}) collective-permute-start(bf16[192,2048]{1,0:T(8,128)(2,1)} %collective-permute-done.1), channel_id=1, source_target_pairs={{0,2},{2,6},{6,4},{4,0},{1,3},{3,7},{7,5},{5,1},{8,10},{10,14},{14... | collective-permute-start | bytes 2359304 | tf_op jit(solution)/shard_map/ppermute | solution.py:385
  58.9 21.5 %collective-permute-start.7 = (bf16[512,768]{1,0:T(8,128)(2,1)S(1)}, bf16[512,768]{1,0:T(8,128)(2,1)S(1)}, u32[]{:S(2)}, u32[]{:S(2)}) collective-permute-start(bf16[512,768]{1,0:T(8,128)(2,1)S(1)} %bitcast.282), channel_id=1, source_target_pairs={{0,8},{8,0},{1,9},{9,1},{2,10},{10,2},{3,11},{11,3},{4,12},{12,4},... | collective-permute-start | bytes 2359304 | tf_op jit(solution)/shard_map/ppermute | solution.py:97
  76.5 19.6 %collective-permute-start.4 = (bf16[192,2048]{1,0:T(8,128)(2,1)S(1)}, bf16[192,2048]{1,0:T(8,128)(2,1)S(1)}, u32[]{:S(2)}, u32[]{:S(2)}) collective-permute-start(bf16[192,2048]{1,0:T(8,128)(2,1)S(1)} %collective-permute-done.3), channel_id=1, source_target_pairs={{0,1},{1,0},{2,3},{3,2},{4,5},{5,4},{6,7},{7,6},{8,9},{9,8},{10,11... | collective-permute-start | bytes 2359304 | tf_op jit(solution)/shard_map/ppermute | solution.py:398
  130.7 55.0 %all-to-all-start.3 = ((bf16[8,2,64,1024]{3,2,1,0:T(8,128)(2,1)}), bf16[8,2,64,1024]{3,2,1,0:T(8,128)(2,1)S(1)}, u32[]{:S(2)}, u32[]{:S(2)}) async-start(bf16[8,2,64,1024]{3,2,1,0:T(8,128)(2,1)} %copy.300), calls=%async_computation.3 | async-start | bytes 4194304 | tf_op jit(solution)/shard_map/all_to_all | solution.py:80
  149.3 48.4 %collective-permute-start.13 = (bf16[512,2048]{1,0:T(8,128)(2,1)}, bf16[512,2048]{1,0:T(8,128)(2,1)}, u32[]{:S(2)}, u32[]{:S(2)}) collective-permute-start(bf16[512,2048]{1,0:T(8,128)(2,1)} %slice_dynamic-update-slice_fusion.7), channel_id=1, source_target_pairs={{0,16},{16,0},{1,17},{17,1},{2,18},{18,2},{3,19},{19,3},{4,20},{20... | collective-permute-start | bytes 6291464 | tf_op jit(solution)/shard_map/ppermute | solution.py:415
  161.0 59.1 %collective-permute-start.12 = (bf16[512,2048]{1,0:T(8,128)(2,1)}, bf16[512,2048]{1,0:T(8,128)(2,1)}, u32[]{:S(2)}, u32[]{:S(2)}) collective-permute-start(bf16[512,2048]{1,0:T(8,128)(2,1)} %slice_dynamic-update-slice_fusion.7), channel_id=1, source_target_pairs={{0,8},{8,0},{1,9},{9,1},{2,10},{10,2},{3,11},{11,3},{4,12},{12,4},... | collective-permute-start | bytes 6291464 | tf_op jit(solution)/shard_map/ppermute | solution.py:97
  185.7 33.0 %all-to-all-start.5 = ((bf16[8,1,64,1024]{3,2,1,0:T(8,128)(2,1)}), bf16[8,1,64,1024]{3,2,1,0:T(8,128)(2,1)}, u32[]{:S(2)}, u32[]{:S(2)}) async-start(bf16[8,1,64,1024]{3,2,1,0:T(8,128)(2,1)} %copy.304), calls=%async_computation.5 | async-start | bytes 2097152 | tf_op jit(solution)/shard_map/all_to_all | solution.py:80
  192.5 122.7 %all-gather.2.cloned.1.call-start = ((), (), s32[]{:S(2)}) async-start(), calls=%async_computation.16 | async-start | bytes 5242880 | tf_op jit(solution)/shard_map/all_gather | solution.py:506
  197.7 79.8 %collective-permute-start.14 = (bf16[512,2048]{1,0:T(8,128)(2,1)}, bf16[512,2048]{1,0:T(8,128)(2,1)}, u32[]{:S(2)}, u32[]{:S(2)}) collective-permute-start(bf16[512,2048]{1,0:T(8,128)(2,1)} %collective-permute-done.13), channel_id=1, source_target_pairs={{0,8},{8,0},{1,9},{9,1},{2,10},{10,2},{3,11},{11,3},{4,12},{12,4},... | collective-permute-start | bytes 6291464 | tf_op jit(solution)/shard_map/ppermute | solution.py:97
  198.7 36.2 %collective-permute-start.10 = (bf16[512,1024]{1,0:T(8,128)(2,1)}, bf16[512,1024]{1,0:T(8,128)(2,1)}, u32[]{:S(2)}, u32[]{:S(2)}) collective-permute-start(bf16[512,1024]{1,0:T(8,128)(2,1)} %bitcast.276), channel_id=1, source_target_pairs={{0,1},{1,0},{2,3},{3,2},{4,5},{5,4},{6,7},{7,6},{8,9},{9,8},{10,11... | collective-permute-start | bytes 3145736 | tf_op jit(solution)/shard_map/ppermute | solution.py:447
  199.9 35.8 %collective-permute-start.11 = (bf16[512,1024]{1,0:T(8,128)(2,1)}, bf16[512,1024]{1,0:T(8,128)(2,1)S(1)}, u32[]{:S(2)}, u32[]{:S(2)}) collective-permute-start(bf16[512,1024]{1,0:T(8,128)(2,1)} %bitcast.277), channel_id=1, source_target_pairs={{0,16},{16,0},{1,17},{17,1},{2,18},{18,2},{3,19},{19,3},{4,20},{20... | collective-permute-start | bytes 3145736 | tf_op jit(solution)/shard_map/ppermute | solution.py:447
  218.7 58.6 %collective-permute-start.17 = (bf16[512,1024]{1,0:T(8,128)(2,1)}, bf16[512,1024]{1,0:T(8,128)(2,1)}, u32[]{:S(2)}, u32[]{:S(2)}) collective-permute-start(bf16[512,1024]{1,0:T(8,128)(2,1)} %bitcast.48), channel_id=1, source_target_pairs={{0,16},{16,0},{1,17},{17,1},{2,18},{18,2},{3,19},{19,3},{4,20},{20... | collective-permute-start | bytes 3145736 | tf_op jit(solution)/shard_map/ppermute | solution.py:447
  220.0 76.3 %collective-permute-start.18 = (bf16[512,1024]{1,0:T(8,128)(2,1)}, bf16[512,1024]{1,0:T(8,128)(2,1)}, u32[]{:S(2)}, u32[]{:S(2)}) collective-permute-start(bf16[512,1024]{1,0:T(8,128)(2,1)} %bitcast.48), channel_id=1, source_target_pairs={{0,1},{1,0},{2,3},{3,2},{4,5},{5,4},{6,7},{7,6},{8,9},{9,8},{10,11... | collective-permute-start | bytes 3145736 | tf_op jit(solution)/shard_map/ppermute | solution.py:447
  236.9 45.7 %all-to-all-start.4 = ((bf16[8,128,256]{1,2,0:T(8,128)(2,1)}), bf16[8,128,256]{1,2,0:T(8,128)(2,1)S(1)}, u32[]{:S(2)}, u32[]{:S(2)}) async-start(bf16[8,128,256]{1,2,0:T(8,128)(2,1)} %copy.301), calls=%async_computation.4 | async-start | bytes 1048576 | tf_op jit(solution)/shard_map/all_to_all | solution.py:80
  241.4 414.3 %reduce-scatter.4.cloned.1.call-start = ((), (), s32[]{:S(2)}) async-start(), calls=%async_computation.17 | async-start | bytes 5242880 | tf_op jit(solution)/shard_map/reduce_scatter | solution.py:560
  277.3 30.6 %collective-permute-start.19 = (bf16[512,1024]{1,0:T(8,128)(2,1)}, bf16[512,1024]{1,0:T(8,128)(2,1)}, u32[]{:S(2)}, u32[]{:S(2)}) collective-permute-start(bf16[512,1024]{1,0:T(8,128)(2,1)} %collective-permute-done.17), channel_id=1, source_target_pairs={{0,1},{1,0},{2,3},{3,2},{4,5},{5,4},{6,7},{7,6},{8,9},{9,8},{10,11... | collective-permute-start | bytes 3145736 | tf_op jit(solution)/shard_map/ppermute | solution.py:515
  277.3 33.0 %collective-permute-start.16 = (bf16[512,1024]{1,0:T(8,128)(2,1)}, bf16[512,1024]{1,0:T(8,128)(2,1)}, u32[]{:S(2)}, u32[]{:S(2)}) collective-permute-start(bf16[512,1024]{1,0:T(8,128)(2,1)} %collective-permute-done.10), channel_id=1, source_target_pairs={{0,16},{16,0},{1,17},{17,1},{2,18},{18,2},{3,19},{19,3},{4,20},{20... | collective-permute-start | bytes 3145736 | tf_op jit(solution)/shard_map/ppermute | solution.py:512
  287.6 21.6 %collective-permute-start.21 = (bf16[128,2048]{1,0:T(8,128)(2,1)S(1)}, bf16[128,2048]{1,0:T(8,128)(2,1)S(1)}, u32[]{:S(2)}, u32[]{:S(2)}) collective-permute-start(bf16[128,2048]{1,0:T(8,128)(2,1)S(1)} %fusion.15.part), channel_id=1, source_target_pairs={{0,2},{2,6},{6,4},{4,0},{1,3},{3,7},{7,5},{5,1},{8,10},{10,14},{14... | collective-permute-start | bytes 1572872 | tf_op jit(solution)/shard_map/ppermute | solution.py:385
  288.3 26.1 %collective-permute-start.15 = (bf16[128,2048]{1,0:T(8,128)(2,1)S(1)}, bf16[128,2048]{1,0:T(8,128)(2,1)S(1)}, u32[]{:S(2)}, u32[]{:S(2)}) collective-permute-start(bf16[128,2048]{1,0:T(8,128)(2,1)S(1)} %fusion.15.part), channel_id=1, source_target_pairs={{0,8},{8,0},{1,9},{9,1},{2,10},{10,2},{3,11},{11,3},{4,12},{12,4},... | collective-permute-start | bytes 1572872 | tf_op jit(solution)/shard_map/ppermute | solution.py:97
  314.0 20.3 %collective-permute-start.22 = (bf16[128,2048]{1,0:T(8,128)(2,1)S(1)}, bf16[128,2048]{1,0:T(8,128)(2,1)}, u32[]{:S(2)}, u32[]{:S(2)}) collective-permute-start(bf16[128,2048]{1,0:T(8,128)(2,1)S(1)} %collective-permute-done.21.part), channel_id=1, source_target_pairs={{0,2},{2,6},{6,4},{4,0},{1,3},{3,7},{7,5},{5,1},{8,10},{10,14},{14... | collective-permute-start | bytes 1572872 | tf_op jit(solution)/shard_map/ppermute | solution.py:385
  374.3 21.5 %collective-permute-start.20 = (bf16[128,2048]{1,0:T(8,128)(2,1)}, bf16[128,2048]{1,0:T(8,128)(2,1)}, u32[]{:S(2)}, u32[]{:S(2)}) collective-permute-start(bf16[128,2048]{1,0:T(8,128)(2,1)} %get-tuple-element.102), channel_id=1, source_target_pairs={{0,8},{8,0},{1,9},{9,1},{2,10},{10,2},{3,11},{11,3},{4,12},{12,4},... | collective-permute-start | bytes 1572872 | tf_op jit(solution)/shard_map/ppermute | solution.py:97
  481.8 220.0 %reduce-scatter.6.cloned.1.call-start = ((), (), s32[]{:S(2)}) async-start(), calls=%async_computation.18 | async-start | bytes 5242880 | tf_op jit(solution)/shard_map/reduce_scatter | solution.py:560
  536.6 22.1 %collective-permute-start.47 = (bf16[128,2048]{0,1:T(8,128)(2,1)}, bf16[128,2048]{0,1:T(8,128)(2,1)}, u32[]{:S(2)}, u32[]{:S(2)}) collective-permute-start(bf16[128,2048]{0,1:T(8,128)(2,1)} %bitcast.72), channel_id=1, source_target_pairs={{0,1},{1,0},{2,3},{3,2},{4,5},{5,4},{6,7},{7,6},{8,9},{9,8},{10,11... | collective-permute-start | bytes 1572872 | tf_op jit(solution)/shard_map/ppermute | solution.py:390
  539.7 23.0 %all-to-all-start.6 = ((bf16[8,128,256]{2,1,0:T(8,128)(2,1)}), bf16[8,128,256]{2,1,0:T(8,128)(2,1)}, u32[]{:S(2)}, u32[]{:S(2)}) async-start(bf16[8,128,256]{2,1,0:T(8,128)(2,1)} %bitcast.291), calls=%async_computation.6 | async-start | bytes 1048576 | tf_op jit(solution)/shard_map/all_to_all | solution.py:80
  544.8 242.5 %reduce-scatter.8.cloned.1.call-start = ((), (), s32[]{:S(2)}) async-start(), calls=%async_computation.19 | async-start | bytes 5242880 | tf_op jit(solution)/shard_map/reduce_scatter | solution.py:560
  557.5 30.9 %collective-permute-start.49 = (bf16[128,2048]{0,1:T(8,128)(2,1)}, bf16[128,2048]{0,1:T(8,128)(2,1)S(1)}, u32[]{:S(2)}, u32[]{:S(2)}) collective-permute-start(bf16[128,2048]{0,1:T(8,128)(2,1)} %collective-permute-done.48), channel_id=1, source_target_pairs={{0,1},{1,0},{2,3},{3,2},{4,5},{5,4},{6,7},{7,6},{8,9},{9,8},{10,11... | collective-permute-start | bytes 1572872 | tf_op jit(solution)/shard_map/ppermute | solution.py:390
  589.3 29.1 %collective-permute-start.53 = (bf16[128,2048]{0,1:T(8,128)(2,1)S(1)}, bf16[128,2048]{0,1:T(8,128)(2,1)S(1)}, u32[]{:S(2)}, u32[]{:S(2)}) collective-permute-start(bf16[128,2048]{0,1:T(8,128)(2,1)S(1)} %collective-permute-done.52), channel_id=1, source_target_pairs={{0,1},{1,0},{2,3},{3,2},{4,5},{5,4},{6,7},{7,6},{8,9},{9,8},{10,11... | collective-permute-start | bytes 1572872 | tf_op jit(solution)/shard_map/ppermute | solution.py:390
  631.9 87.8 %collective-permute-start.54 = (bf16[128,2048]{1,0:T(8,128)(2,1)}, bf16[128,2048]{1,0:T(8,128)(2,1)}, u32[]{:S(2)}, u32[]{:S(2)}) collective-permute-start(bf16[128,2048]{1,0:T(8,128)(2,1)} %pad_maximum_fusion.5), channel_id=1, source_target_pairs={{0,8},{8,0},{1,9},{9,1},{2,10},{10,2},{3,11},{11,3},{4,12},{12,4},... | collective-permute-start | bytes 1572872 | tf_op jit(solution)/shard_map/ppermute | solution.py:97
  653.9 62.0 %collective-permute-start.64 = (bf16[1024,768]{1,0:T(8,128)(2,1)}, bf16[1024,768]{1,0:T(8,128)(2,1)}, u32[]{:S(2)}, u32[]{:S(2)}) collective-permute-start(bf16[1024,768]{1,0:T(8,128)(2,1)} %pad_maximum_fusion.1), channel_id=1, source_target_pairs={{0,8},{8,0},{1,9},{9,1},{2,10},{10,2},{3,11},{11,3},{4,12},{12,4},... | collective-permute-start | bytes 4718600 | tf_op jit(solution)/shard_map/ppermute | solution.py:97
  655.8 29.3 %all-to-all-start.8 = ((bf16[8,64,1024]{2,1,0:T(8,128)(2,1)}), bf16[8,64,1024]{2,1,0:T(8,128)(2,1)}, u32[]{:S(2)}, u32[]{:S(2)}) async-start(bf16[8,64,1024]{2,1,0:T(8,128)(2,1)} %bitcast.310), calls=%async_computation.9 | async-start | bytes 2097152 | tf_op jit(solution)/shard_map/all_to_all | solution.py:80
  665.7 116.1 %collective-permute-start.58 = (bf16[128,2048]{1,0:T(8,128)(2,1)}, bf16[128,2048]{1,0:T(8,128)(2,1)}, u32[]{:S(2)}, u32[]{:S(2)}) collective-permute-start(bf16[128,2048]{1,0:T(8,128)(2,1)} %fusion.11), channel_id=1, source_target_pairs={{0,1},{1,0},{2,3},{3,2},{4,5},{5,4},{6,7},{7,6},{8,9},{9,8},{10,11... | collective-permute-start | bytes 1572872 | tf_op jit(solution)/shard_map/ppermute | solution.py:434
  668.6 30.5 %collective-permute-start.60 = (bf16[128,2048]{1,0:T(8,128)(2,1)}, bf16[128,2048]{1,0:T(8,128)(2,1)}, u32[]{:S(2)}, u32[]{:S(2)}) collective-permute-start(bf16[128,2048]{1,0:T(8,128)(2,1)} %fusion.13), channel_id=1, source_target_pairs={{0,1},{1,0},{2,3},{3,2},{4,5},{5,4},{6,7},{7,6},{8,9},{9,8},{10,11... | collective-permute-start | bytes 1572872 | tf_op jit(solution)/shard_map/ppermute | solution.py:434
  672.4 50.2 %collective-permute-start.59 = (bf16[128,2048]{1,0:T(8,128)(2,1)}, bf16[128,2048]{1,0:T(8,128)(2,1)}, u32[]{:S(2)}, u32[]{:S(2)}) collective-permute-start(bf16[128,2048]{1,0:T(8,128)(2,1)} %fusion.12), channel_id=1, source_target_pairs={{0,1},{1,0},{2,3},{3,2},{4,5},{5,4},{6,7},{7,6},{8,9},{9,8},{10,11... | collective-permute-start | bytes 1572872 | tf_op jit(solution)/shard_map/ppermute | solution.py:434
  685.1 25.6 %all-to-all-start.10 = ((f32[32,1,256]{2,1,0:T(1,128)}), f32[32,1,256]{2,1,0:T(1,128)}, u32[]{:S(2)}, u32[]{:S(2)}) async-start(f32[32,1,256]{2,1,0:T(1,128)} %reshape.390), calls=%async_computation.11 | async-start | bytes 65536 | tf_op jit(solution)/shard_map/all_to_all | solution.py:80
  701.5 21.2 %collective-permute-start.61 = (bf16[128,2048]{1,0:T(8,128)(2,1)}, bf16[128,2048]{1,0:T(8,128)(2,1)}, u32[]{:S(2)}, u32[]{:S(2)}) collective-permute-start(bf16[128,2048]{1,0:T(8,128)(2,1)} %fusion), channel_id=1, source_target_pairs={{0,2},{2,6},{6,4},{4,0},{1,3},{3,7},{7,5},{5,1},{8,10},{10,14},{14... | collective-permute-start | bytes 1572872 | tf_op jit(solution)/shard_map/ppermute | solution.py:385
  710.7 29.2 %all-to-all-start.11 = ((bf16[8,64,1024]{2,1,0:T(8,128)(2,1)}), bf16[8,64,1024]{2,1,0:T(8,128)(2,1)}, u32[]{:S(2)}, u32[]{:S(2)}) async-start(bf16[8,64,1024]{2,1,0:T(8,128)(2,1)} %bitcast.309), calls=%async_computation.13 | async-start | bytes 2097152 | tf_op jit(solution)/shard_map/all_to_all | solution.py:80
  722.4 23.9 %collective-permute-start.55 = (bf16[64,2048]{1,0:T(8,128)(2,1)}, bf16[64,2048]{1,0:T(8,128)(2,1)}, u32[]{:S(2)}, u32[]{:S(2)}) collective-permute-start(bf16[64,2048]{1,0:T(8,128)(2,1)} %constant_dynamic-slice_fusion.8), channel_id=1, source_target_pairs={{0,16},{16,0},{1,17},{17,1},{2,18},{18,2},{3,19},{19,3},{4,20},{20... | collective-permute-start | bytes 786440 | tf_op jit(solution)/shard_map/ppermute | solution.py:579
  724.9 57.0 %collective-permute-start.62 = (bf16[128,2048]{1,0:T(8,128)(2,1)}, bf16[128,2048]{1,0:T(8,128)(2,1)}, u32[]{:S(2)}, u32[]{:S(2)}) collective-permute-start(bf16[128,2048]{1,0:T(8,128)(2,1)} %fusion.2), channel_id=1, source_target_pairs={{0,2},{2,6},{6,4},{4,0},{1,3},{3,7},{7,5},{5,1},{8,10},{10,14},{14... | collective-permute-start | bytes 1572872 | tf_op jit(solution)/shard_map/ppermute | solution.py:385
  740.0 47.3 %all-to-all-start.9 = ((bf16[8,64,768]{2,1,0:T(8,128)(2,1)}), bf16[8,64,768]{2,1,0:T(8,128)(2,1)}, u32[]{:S(2)}, u32[]{:S(2)}) async-start(bf16[8,64,768]{2,1,0:T(8,128)(2,1)} %bitcast.280), calls=%async_computation.10 | async-start | bytes 1572864 | tf_op jit(solution)/shard_map/all_to_all | solution.py:80
  748.0 32.0 %collective-permute-start.56 = (bf16[64,2048]{1,0:T(8,128)(2,1)}, bf16[64,2048]{1,0:T(8,128)(2,1)}, u32[]{:S(2)}, u32[]{:S(2)}) collective-permute-start(bf16[64,2048]{1,0:T(8,128)(2,1)} %add_convert_fusion.6), channel_id=1, source_target_pairs={{0,0},{1,4},{2,8},{3,12},{4,16},{5,20},{6,24},{7,28},{8,1},{9,5},{... | collective-permute-start | bytes 786440 | tf_op jit(solution)/shard_map/ppermute | solution.py:615
  784.4 20.6 %collective-permute-start.63 = (bf16[128,2048]{1,0:T(8,128)(2,1)}, bf16[128,2048]{1,0:T(8,128)(2,1)}, u32[]{:S(2)}, u32[]{:S(2)}) collective-permute-start(bf16[128,2048]{1,0:T(8,128)(2,1)} %fusion.4), channel_id=1, source_target_pairs={{0,2},{2,6},{6,4},{4,0},{1,3},{3,7},{7,5},{5,1},{8,10},{10,14},{14... | collective-permute-start | bytes 1572872 | tf_op jit(solution)/shard_map/ppermute | solution.py:385
  787.3 33.7 %all-to-all-start.12 = ((bf16[8,64,1024]{2,1,0:T(8,128)(2,1)}), bf16[8,64,1024]{2,1,0:T(8,128)(2,1)}, u32[]{:S(2)}, u32[]{:S(2)}) async-start(bf16[8,64,1024]{2,1,0:T(8,128)(2,1)} %bitcast.311), calls=%async_computation.15 | async-start | bytes 2097152 | tf_op jit(solution)/shard_map/all_to_all | solution.py:80
  (112 other events, 1185.0 us)
Sparse Core Ops, SparseCore 0:
  197.6 90.7 all-gather.1
  481.9 52.8 reduce-scatter.3
  538.1 84.1 reduce-scatter.5
  625.1 60.1 reduce-scatter.7

commit v6 on v5

--- a/solution.py
+++ b/solution.py
@@ -528,7 +528,7 @@
             pair = (rows, core_swap(rows))
             if at < n_z - 1:
                 rows = ring_send(tie(rows, *gate) if gate and at == 1 else rows)
-            if at > 1:
+            if at > 2:
                 pair = tie(pair, total)
             *held, mine, away = feed_step(
                 at, n_z, pair, (w_g, w_u, w_d), saved, held, kernel, dtypes

time: 843 us -> 828 us (0.982)
  waiting for transfers between devices: 304 us -> 281 us
    ppermute x4, waiting for transfers between devices: 12.2 us -> 3.73 us  [seq_sum(): away = lax.ppermute(pick(part, 1 - y_at).astype(BF16), 'y', SWAP)]
    unnamed x184 -> x180, local copies, waits for them, and re-layouts: 61.8 us -> 61.7 us
  transfers between devices with their start and end apart: 83 -> 83, of which waited for: 34 -> 32; matrix products, arithmetic and copies ran while one was open for 30% -> 32% of each run, Pallas kernels for 8% -> 9%
where the time goes in v6:
time: 828 us; the launch traced here: 815 us
  waiting for transfers between devices  281 us (34%)
  local copies, waits for them, and re-layouts  188 us (23%)
  starting transfers between devices  131 us (16%)
  Pallas kernels  78.9 us (10%)
  other arithmetic  58.7 us (7%)
  matrix products  57.2 us (7%)
  between operations  21 us (3%)
    ppermute x21, waiting for transfers between devices, ring_send(): return lax.ppermute(part, 'z', ring)  102 us
    all_to_all x13, starting transfers between devices, exchange(): lax.all_to_all(array_in, axes, split_axis=0, concat_axis=0, tiled=True)  78.6 us
    unnamed x180, local copies, waits for them, and re-layouts  61.7 us
    pallas_call x8, Pallas kernels, feed_step(): pl.pallas_call(kernel, grid=(feed // step,), in_specs=[part, part] + [pl....  56.2 us
    all_to_all x13, waiting for transfers between devices, exchange(): lax.all_to_all(array_in, axes, split_axis=0, concat_axis=0, tiled=True)  52 us
    ppermute x4, waiting for transfers between devices, rest_send(): return (mine, lax.ppermute(mine, 'y', SWAP), lax.ppermute(mine, 'x', SWAP))  45 us
    dot_general x5, matrix products, dot_left_t(): lax.dot_general(left_mat, right_mat, (((0,), (0,)), ((), ())), preferred_...  34.6 us
    ppermute x4, waiting for transfers between devices, seq_gather(): chunks += [held, lax.ppermute(held, 'y', SWAP)]  25.6 us
  transfers between devices with their start and end apart: 83, of which 32 were waited for; matrix products, arithmetic and copies ran while one was open for 32% of the time, Pallas kernels for 9%

profile of v6, /device:TPU:25, one launch (start us, length us, event | category | flops | bytes accessed | tf_op | source)
XLA Modules:
  0.0 815.1 jit_solution(15215674004050411012)
XLA Ops:
  41.6 7.0 all-to-all-done
  48.6 6.7 all-to-all-start.2
  61.8 14.4 %collective-permute-done.3 = bf16[192,2048]{1,0:T(8,128)(2,1)S(1)} collective-permute-done((bf16[192,2048]{1,0:T(8,128)(2,1)}, bf16[192,2048]{1,0:T(8,128)(2,1)S(1)}, u32[]{:S(2)}, u32[]{:S(2)}) %collective-permute-start.3) | collective-permute-done | bytes 786464 | tf_op jit(solution)/shard_map/ppermute | solution.py:385
  80.5 14.3 %collective-permute-done.5 = bf16[192,2048]{1,0:T(8,128)(2,1)S(1)} collective-permute-done((bf16[192,2048]{1,0:T(8,128)(2,1)S(1)}, bf16[192,2048]{1,0:T(8,128)(2,1)S(1)}, u32[]{:S(2)}, u32[]{:S(2)}) %collective-permute-start.5) | collective-permute-done | bytes 786464 | tf_op jit(solution)/shard_map/ppermute | solution.py:385
  98.1 13.4 %collective-permute-done.6 = bf16[192,2048]{1,0:T(8,128)(2,1)S(1)} collective-permute-done((bf16[192,2048]{1,0:T(8,128)(2,1)S(1)}, bf16[192,2048]{1,0:T(8,128)(2,1)S(1)}, u32[]{:S(2)}, u32[]{:S(2)}) %collective-permute-start.6) | collective-permute-done | bytes 786464 | tf_op jit(solution)/shard_map/ppermute | solution.py:398
  112.5 5.3 fusion.19.refs_0_.refs_1_.refs_2_.refs_5_.refs_6_
  119.3 5.7 all-to-all-start.1
  130.7 8.6 %all-to-all-start.3 = ((bf16[8,2,64,1024]{3,2,1,0:T(8,128)(2,1)}), bf16[8,2,64,1024]{3,2,1,0:T(8,128)(2,1)S(1)}, u32[]{:S(2)}, u32[]{:S(2)}) async-start(bf16[8,2,64,1024]{3,2,1,0:T(8,128)(2,1)} %copy.300), calls=%async_computation.3 | async-start | bytes 4194304 | tf_op jit(solution)/shard_map/all_to_all | solution.py:80
  165.5 20.3 %all-to-all-done.3 = bf16[8,2,64,1024]{3,2,1,0:T(8,128)(2,1)S(1)} async-done(((bf16[8,2,64,1024]{3,2,1,0:T(8,128)(2,1)}), bf16[8,2,64,1024]{3,2,1,0:T(8,128)(2,1)S(1)}, u32[]{:S(2)}, u32[]{:S(2)}) %all-to-all-start.3) | async-done | bytes 2097184 | tf_op jit(solution)/shard_map/all_to_all | solution.py:80
  185.7 6.8 all-to-all-start.5
  209.1 9.8 %shard_map.246 = (bf16[1024,256]{1,0:T(8,128)(2,1)}, bf16[1024,256]{1,0:T(8,128)(2,1)}, bf16[1024,256]{1,0:T(8,128)(2,1)}, f32[2,1024,1]{2,1,0:T(8,128)}, bf16[1024,256]{1,0:T(8,128)(2,1)}) custom-call(f32[1024,768]{1,0:T(8,128)} %copy-done.23, f32[1024,768]{1,0:T(8,128)} %copy-done.23, f32[1024,768]{1,0:T(8,128)} %copy-done.23, ...), custom_call_target="tpu_custom_call" | custom-call | flops 805306368 | bytes 4718592 | tf_op jit(solution)/shard_map/pallas_call | solution.py:217
  223.6 11.4 %collective-permute-done.10 = bf16[512,1024]{1,0:T(8,128)(2,1)} collective-permute-done((bf16[512,1024]{1,0:T(8,128)(2,1)}, bf16[512,1024]{1,0:T(8,128)(2,1)}, u32[]{:S(2)}, u32[]{:S(2)}) %collective-permute-start.10) | collective-permute-done | bytes 1048608 | tf_op jit(solution)/shard_map/ppermute | solution.py:447
  244.8 32.7 %collective-permute-done.17 = bf16[512,1024]{1,0:T(8,128)(2,1)} collective-permute-done((bf16[512,1024]{1,0:T(8,128)(2,1)}, bf16[512,1024]{1,0:T(8,128)(2,1)}, u32[]{:S(2)}, u32[]{:S(2)}) %collective-permute-start.17) | collective-permute-done | bytes 1048608 | tf_op jit(solution)/shard_map/ppermute | solution.py:447
  299.8 8.2 %collective-permute-done.19 = bf16[512,1024]{1,0:T(8,128)(2,1)} collective-permute-done((bf16[512,1024]{1,0:T(8,128)(2,1)}, bf16[512,1024]{1,0:T(8,128)(2,1)}, u32[]{:S(2)}, u32[]{:S(2)}) %collective-permute-start.19) | collective-permute-done | bytes 1048608 | tf_op jit(solution)/shard_map/ppermute | solution.py:515
  319.3 7.8 shard_map.247
  327.1 7.4 shard_map.248
  334.7 7.0 shard_map.249
  342.7 5.9 collective-permute-done.23.part
  350.8 9.1 %collective-permute-done.29 = bf16[128,2048]{1,0:T(8,128)(2,1)S(1)} collective-permute-done((bf16[128,2048]{1,0:T(8,128)(2,1)S(1)}, bf16[128,2048]{1,0:T(8,128)(2,1)S(1)}, u32[]{:S(2)}, u32[]{:S(2)}) %collective-permute-start.29) | collective-permute-done | bytes 524320 | tf_op jit(solution)/shard_map/ppermute | solution.py:385
  360.1 6.9 shard_map.250
  384.2 8.5 %collective-permute-done.32 = bf16[128,2048]{1,0:T(8,128)(2,1)} collective-permute-done((bf16[128,2048]{1,0:T(8,128)(2,1)}, bf16[128,2048]{1,0:T(8,128)(2,1)}, u32[]{:S(2)}, u32[]{:S(2)}) %collective-permute-start.32) | collective-permute-done | bytes 524320 | tf_op jit(solution)/shard_map/ppermute | solution.py:385
  395.9 12.5 %collective-permute-done.35.part = bf16[128,2048]{1,0:T(8,128)(2,1)S(1)} collective-permute-done((bf16[128,2048]{1,0:T(8,128)(2,1)S(1)}, bf16[128,2048]{1,0:T(8,128)(2,1)S(1)}, u32[]{:S(2)}, u32[]{:S(2)}) %collective-permute-start.35) | collective-permute-done | bytes 524320 | tf_op jit(solution)/shard_map/ppermute | solution.py:385
  412.4 6.8 shard_map.251
  420.2 6.8 shard_map.252
  429.9 6.8 shard_map.253
  443.3 9.9 %collective-permute-done.43 = bf16[128,2048]{1,0:T(8,128)(2,1)S(1)} collective-permute-done((bf16[128,2048]{1,0:T(8,128)(2,1)S(1)}, bf16[128,2048]{1,0:T(8,128)(2,1)S(1)}, u32[]{:S(2)}, u32[]{:S(2)}) %collective-permute-start.43) | collective-permute-done | bytes 524320 | tf_op jit(solution)/shard_map/ppermute | solution.py:385
  454.2 6.8 shard_map.254
  464.4 6.1 convolution_convert_fusion
  472.1 8.3 %convolution_convert_fusion.2 = bf16[2048,1024]{1,0:T(8,128)(2,1)} fusion(bf16[1024,2048]{1,0:T(8,128)(2,1)} %copy-done.7, bf16[1024,1024]{1,0:T(8,128)(2,1)S(1)} %copy-done.9), kind=kOutput, calls=%fused_computation.2 | convolution fusion | flops 4297064448 | bytes 10485760 | tf_op jit(solution)/shard_map/dot_general | solution.py:40
  491.0 6.0 collective-permute-done.45
  505.3 5.9 collective-permute-done.46
  514.0 7.2 convolution_convert_fusion.5
  534.2 9.0 %convolution_convert_fusion.1 = bf16[2048,1024]{1,0:T(8,128)(2,1)} fusion(bf16[1024,2048]{1,0:T(8,128)(2,1)} %copy-done.7, bf16[1024,1024]{1,0:T(8,128)(2,1)S(1)} %copy-done.11), kind=kOutput, calls=%fused_computation.1 | convolution fusion | flops 4297064448 | bytes 10485760 | tf_op jit(solution)/shard_map/dot_general | solution.py:40
  552.7 8.8 %collective-permute-done.50 = bf16[128,2048]{0,1:T(8,128)(2,1)S(1)} collective-permute-done((bf16[128,2048]{0,1:T(8,128)(2,1)}, bf16[128,2048]{0,1:T(8,128)(2,1)S(1)}, u32[]{:S(2)}, u32[]{:S(2)}) %collective-permute-start.50) | collective-permute-done | bytes 524320 | tf_op jit(solution)/shard_map/ppermute | solution.py:385
  561.6 13.0 %shard_map.255 = (f32[1024,256]{1,0:T(8,128)}, f32[1024,256]{1,0:T(8,128)}, bf16[1024,256]{1,0:T(8,128)(2,1)}, f32[2,1024,1]{2,1,0:T(8,128)}, f32[2,1024,1]{2,1,0:T(8,128)}) custom-call(bf16[1024,256]{1,0:T(8,128)(2,1)} %get-tuple-element.142.refs_0_, bf16[1024,256]{1,0:T(8,128)(2,1)} %get-tuple-element.143.refs_1_, ...), custom_call_target="tpu_custom_call" | custom-call | flops 1879048192 | bytes 6291456 | tf_op jit(solution)/shard_map/pallas_call | solution.py:241
  580.8 6.2 collective-permute-done.51
  588.9 19.4 %collective-permute-done.53 = bf16[128,2048]{0,1:T(8,128)(2,1)S(1)} collective-permute-done((bf16[128,2048]{0,1:T(8,128)(2,1)S(1)}, bf16[128,2048]{0,1:T(8,128)(2,1)S(1)}, u32[]{:S(2)}, u32[]{:S(2)}) %collective-permute-start.53) | collective-permute-done | bytes 524320 | tf_op jit(solution)/shard_map/ppermute | solution.py:390
  609.8 6.8 all-to-all-start.7
  639.4 7.5 convolution_convert_fusion.3
  646.9 5.2 all-to-all-start.8
  676.2 5.6 all-to-all-start.10
  684.3 10.7 %all-to-all-done.10 = f32[32,1,256]{2,1,0:T(1,128)} async-done(((f32[32,1,256]{2,1,0:T(1,128)}), f32[32,1,256]{2,1,0:T(1,128)}, u32[]{:S(2)}, u32[]{:S(2)}) %all-to-all-start.10) | async-done | bytes 32800 | tf_op jit(solution)/shard_map/all_to_all | solution.py:80
  695.0 5.2 all-to-all-start.11
  709.4 12.2 %collective-permute-done.65 = bf16[512,768]{1,0:T(8,128)(2,1)S(1)} collective-permute-done((bf16[512,768]{1,0:T(8,128)(2,1)S(1)}, bf16[512,768]{1,0:T(8,128)(2,1)S(1)}, u32[]{:S(2)}, u32[]{:S(2)}) %collective-permute-start.65) | collective-permute-done | bytes 786464 | tf_op jit(solution)/shard_map/ppermute | solution.py:579
  724.2 6.2 all-to-all-start.9
  748.4 15.0 %collective-permute-done.56 = bf16[64,2048]{1,0:T(8,128)(2,1)} collective-permute-done((bf16[64,2048]{1,0:T(8,128)(2,1)}, bf16[64,2048]{1,0:T(8,128)(2,1)}, u32[]{:S(2)}, u32[]{:S(2)}) %collective-permute-start.56) | collective-permute-done | bytes 262176 | tf_op jit(solution)/shard_map/ppermute | solution.py:615
  770.8 7.7 all-to-all-start.12
  798.2 7.0 all-to-all-done.12
  (494 shorter events, 348.3 us)
Async XLA Ops:
  11.6 28.2 %collective-permute-start = (bf16[192,2048]{1,0:T(8,128)(2,1)}, bf16[192,2048]{1,0:T(8,128)(2,1)}, u32[]{:S(2)}, u32[]{:S(2)}) collective-permute-start(bf16[192,2048]{1,0:T(8,128)(2,1)} %pad_maximum_fusion.2), channel_id=1, source_target_pairs={{0,1},{1,0},{2,3},{3,2},{4,5},{5,4},{6,7},{7,6},{8,9},{9,8},{10,11... | collective-permute-start | bytes 2359304 | tf_op jit(solution)/shard_map/ppermute | solution.py:398
  12.8 25.7 %collective-permute-start.1 = (bf16[192,2048]{1,0:T(8,128)(2,1)}, bf16[192,2048]{1,0:T(8,128)(2,1)}, u32[]{:S(2)}, u32[]{:S(2)}) collective-permute-start(bf16[192,2048]{1,0:T(8,128)(2,1)} %pad_maximum_fusion.2), channel_id=1, source_target_pairs={{0,2},{2,6},{6,4},{4,0},{1,3},{3,7},{7,5},{5,1},{8,10},{10,14},{14... | collective-permute-start | bytes 2359304 | tf_op jit(solution)/shard_map/ppermute | solution.py:385
  18.0 30.7 %all-to-all-start = ((bf16[8,64,768]{2,1,0:T(8,128)(2,1)}), bf16[8,64,768]{2,1,0:T(8,128)(2,1)S(1)}, u32[]{:S(2)}, u32[]{:S(2)}) async-start(bf16[8,64,768]{2,1,0:T(8,128)(2,1)} %reshape.350), calls=%async_computation | async-start | bytes 1572864 | tf_op jit(solution)/shard_map/all_to_all | solution.py:80
  38.6 22.3 %collective-permute-start.2 = (bf16[192,2048]{1,0:T(8,128)(2,1)}, bf16[192,2048]{1,0:T(8,128)(2,1)S(1)}, u32[]{:S(2)}, u32[]{:S(2)}) collective-permute-start(bf16[192,2048]{1,0:T(8,128)(2,1)} %collective-permute-done.1), channel_id=1, source_target_pairs={{0,1},{1,0},{2,3},{3,2},{4,5},{5,4},{6,7},{7,6},{8,9},{9,8},{10,11... | collective-permute-start | bytes 2359304 | tf_op jit(solution)/shard_map/ppermute | solution.py:398
  48.6 69.6 %all-to-all-start.2 = ((bf16[32,2,128]{2,1,0:T(2,128)(2,1)}), bf16[32,2,128]{2,1,0:T(2,128)(2,1)S(1)}, u32[]{:S(2)}, u32[]{:S(2)}) async-start(bf16[32,2,128]{2,1,0:T(2,128)(2,1)} %reshape.388), calls=%async_computation.2 | async-start | bytes 32768 | tf_op jit(solution)/shard_map/all_to_all | solution.py:80
  55.4 22.4 %collective-permute-start.8 = (bf16[512,768]{1,0:T(8,128)(2,1)S(1)}, bf16[512,768]{1,0:T(8,128)(2,1)S(1)}, u32[]{:S(2)}, u32[]{:S(2)}) collective-permute-start(bf16[512,768]{1,0:T(8,128)(2,1)S(1)} %bitcast.281), channel_id=1, source_target_pairs={{0,16},{16,0},{1,17},{17,1},{2,18},{18,2},{3,19},{19,3},{4,20},{20... | collective-permute-start | bytes 2359304 | tf_op jit(solution)/shard_map/ppermute | solution.py:415
  56.6 19.6 %collective-permute-start.3 = (bf16[192,2048]{1,0:T(8,128)(2,1)}, bf16[192,2048]{1,0:T(8,128)(2,1)S(1)}, u32[]{:S(2)}, u32[]{:S(2)}) collective-permute-start(bf16[192,2048]{1,0:T(8,128)(2,1)} %collective-permute-done.1), channel_id=1, source_target_pairs={{0,2},{2,6},{6,4},{4,0},{1,3},{3,7},{7,5},{5,1},{8,10},{10,14},{14... | collective-permute-start | bytes 2359304 | tf_op jit(solution)/shard_map/ppermute | solution.py:385
  58.8 21.6 %collective-permute-start.7 = (bf16[512,768]{1,0:T(8,128)(2,1)S(1)}, bf16[512,768]{1,0:T(8,128)(2,1)S(1)}, u32[]{:S(2)}, u32[]{:S(2)}) collective-permute-start(bf16[512,768]{1,0:T(8,128)(2,1)S(1)} %bitcast.282), channel_id=1, source_target_pairs={{0,8},{8,0},{1,9},{9,1},{2,10},{10,2},{3,11},{11,3},{4,12},{12,4},... | collective-permute-start | bytes 2359304 | tf_op jit(solution)/shard_map/ppermute | solution.py:97
  76.5 19.6 %collective-permute-start.4 = (bf16[192,2048]{1,0:T(8,128)(2,1)S(1)}, bf16[192,2048]{1,0:T(8,128)(2,1)S(1)}, u32[]{:S(2)}, u32[]{:S(2)}) collective-permute-start(bf16[192,2048]{1,0:T(8,128)(2,1)S(1)} %collective-permute-done.3), channel_id=1, source_target_pairs={{0,1},{1,0},{2,3},{3,2},{4,5},{5,4},{6,7},{7,6},{8,9},{9,8},{10,11... | collective-permute-start | bytes 2359304 | tf_op jit(solution)/shard_map/ppermute | solution.py:398
  77.8 19.3 %collective-permute-start.9 = (bf16[512,768]{1,0:T(8,128)(2,1)S(1)}, bf16[512,768]{1,0:T(8,128)(2,1)S(1)}, u32[]{:S(2)}, u32[]{:S(2)}) collective-permute-start(bf16[512,768]{1,0:T(8,128)(2,1)S(1)} %collective-permute-done.8), channel_id=1, source_target_pairs={{0,8},{8,0},{1,9},{9,1},{2,10},{10,2},{3,11},{11,3},{4,12},{12,4},... | collective-permute-start | bytes 2359304 | tf_op jit(solution)/shard_map/ppermute | solution.py:97
  130.7 55.0 %all-to-all-start.3 = ((bf16[8,2,64,1024]{3,2,1,0:T(8,128)(2,1)}), bf16[8,2,64,1024]{3,2,1,0:T(8,128)(2,1)S(1)}, u32[]{:S(2)}, u32[]{:S(2)}) async-start(bf16[8,2,64,1024]{3,2,1,0:T(8,128)(2,1)} %copy.300), calls=%async_computation.3 | async-start | bytes 4194304 | tf_op jit(solution)/shard_map/all_to_all | solution.py:80
  149.3 48.6 %collective-permute-start.13 = (bf16[512,2048]{1,0:T(8,128)(2,1)}, bf16[512,2048]{1,0:T(8,128)(2,1)}, u32[]{:S(2)}, u32[]{:S(2)}) collective-permute-start(bf16[512,2048]{1,0:T(8,128)(2,1)} %slice_dynamic-update-slice_fusion.7), channel_id=1, source_target_pairs={{0,16},{16,0},{1,17},{17,1},{2,18},{18,2},{3,19},{19,3},{4,20},{20... | collective-permute-start | bytes 6291464 | tf_op jit(solution)/shard_map/ppermute | solution.py:415
  161.0 59.2 %collective-permute-start.12 = (bf16[512,2048]{1,0:T(8,128)(2,1)}, bf16[512,2048]{1,0:T(8,128)(2,1)}, u32[]{:S(2)}, u32[]{:S(2)}) collective-permute-start(bf16[512,2048]{1,0:T(8,128)(2,1)} %slice_dynamic-update-slice_fusion.7), channel_id=1, source_target_pairs={{0,8},{8,0},{1,9},{9,1},{2,10},{10,2},{3,11},{11,3},{4,12},{12,4},... | collective-permute-start | bytes 6291464 | tf_op jit(solution)/shard_map/ppermute | solution.py:97
  185.7 33.1 %all-to-all-start.5 = ((bf16[8,1,64,1024]{3,2,1,0:T(8,128)(2,1)}), bf16[8,1,64,1024]{3,2,1,0:T(8,128)(2,1)}, u32[]{:S(2)}, u32[]{:S(2)}) async-start(bf16[8,1,64,1024]{3,2,1,0:T(8,128)(2,1)} %copy.304), calls=%async_computation.5 | async-start | bytes 2097152 | tf_op jit(solution)/shard_map/all_to_all | solution.py:80
  192.5 123.6 %all-gather.2.cloned.1.call-start = ((), (), s32[]{:S(2)}) async-start(), calls=%async_computation.16 | async-start | bytes 5242880 | tf_op jit(solution)/shard_map/all_gather | solution.py:506
  197.9 79.9 %collective-permute-start.14 = (bf16[512,2048]{1,0:T(8,128)(2,1)}, bf16[512,2048]{1,0:T(8,128)(2,1)}, u32[]{:S(2)}, u32[]{:S(2)}) collective-permute-start(bf16[512,2048]{1,0:T(8,128)(2,1)} %collective-permute-done.13), channel_id=1, source_target_pairs={{0,8},{8,0},{1,9},{9,1},{2,10},{10,2},{3,11},{11,3},{4,12},{12,4},... | collective-permute-start | bytes 6291464 | tf_op jit(solution)/shard_map/ppermute | solution.py:97
  198.8 36.2 %collective-permute-start.10 = (bf16[512,1024]{1,0:T(8,128)(2,1)}, bf16[512,1024]{1,0:T(8,128)(2,1)}, u32[]{:S(2)}, u32[]{:S(2)}) collective-permute-start(bf16[512,1024]{1,0:T(8,128)(2,1)} %bitcast.276), channel_id=1, source_target_pairs={{0,1},{1,0},{2,3},{3,2},{4,5},{5,4},{6,7},{7,6},{8,9},{9,8},{10,11... | collective-permute-start | bytes 3145736 | tf_op jit(solution)/shard_map/ppermute | solution.py:447
  200.0 35.8 %collective-permute-start.11 = (bf16[512,1024]{1,0:T(8,128)(2,1)}, bf16[512,1024]{1,0:T(8,128)(2,1)S(1)}, u32[]{:S(2)}, u32[]{:S(2)}) collective-permute-start(bf16[512,1024]{1,0:T(8,128)(2,1)} %bitcast.277), channel_id=1, source_target_pairs={{0,16},{16,0},{1,17},{17,1},{2,18},{18,2},{3,19},{19,3},{4,20},{20... | collective-permute-start | bytes 3145736 | tf_op jit(solution)/shard_map/ppermute | solution.py:447
  218.9 58.6 %collective-permute-start.17 = (bf16[512,1024]{1,0:T(8,128)(2,1)}, bf16[512,1024]{1,0:T(8,128)(2,1)}, u32[]{:S(2)}, u32[]{:S(2)}) collective-permute-start(bf16[512,1024]{1,0:T(8,128)(2,1)} %bitcast.48), channel_id=1, source_target_pairs={{0,16},{16,0},{1,17},{17,1},{2,18},{18,2},{3,19},{19,3},{4,20},{20... | collective-permute-start | bytes 3145736 | tf_op jit(solution)/shard_map/ppermute | solution.py:447
  220.2 76.2 %collective-permute-start.18 = (bf16[512,1024]{1,0:T(8,128)(2,1)}, bf16[512,1024]{1,0:T(8,128)(2,1)}, u32[]{:S(2)}, u32[]{:S(2)}) collective-permute-start(bf16[512,1024]{1,0:T(8,128)(2,1)} %bitcast.48), channel_id=1, source_target_pairs={{0,1},{1,0},{2,3},{3,2},{4,5},{5,4},{6,7},{7,6},{8,9},{9,8},{10,11... | collective-permute-start | bytes 3145736 | tf_op jit(solution)/shard_map/ppermute | solution.py:447
  237.0 45.8 %all-to-all-start.4 = ((bf16[8,128,256]{1,2,0:T(8,128)(2,1)}), bf16[8,128,256]{1,2,0:T(8,128)(2,1)S(1)}, u32[]{:S(2)}, u32[]{:S(2)}) async-start(bf16[8,128,256]{1,2,0:T(8,128)(2,1)} %copy.301), calls=%async_computation.4 | async-start | bytes 1048576 | tf_op jit(solution)/shard_map/all_to_all | solution.py:80
  241.6 405.3 %reduce-scatter.4.cloned.1.call-start = ((), (), s32[]{:S(2)}) async-start(), calls=%async_computation.17 | async-start | bytes 5242880 | tf_op jit(solution)/shard_map/reduce_scatter | solution.py:560
  277.5 30.6 %collective-permute-start.19 = (bf16[512,1024]{1,0:T(8,128)(2,1)}, bf16[512,1024]{1,0:T(8,128)(2,1)}, u32[]{:S(2)}, u32[]{:S(2)}) collective-permute-start(bf16[512,1024]{1,0:T(8,128)(2,1)} %collective-permute-done.17), channel_id=1, source_target_pairs={{0,1},{1,0},{2,3},{3,2},{4,5},{5,4},{6,7},{7,6},{8,9},{9,8},{10,11... | collective-permute-start | bytes 3145736 | tf_op jit(solution)/shard_map/ppermute | solution.py:515
  277.5 32.9 %collective-permute-start.16 = (bf16[512,1024]{1,0:T(8,128)(2,1)}, bf16[512,1024]{1,0:T(8,128)(2,1)}, u32[]{:S(2)}, u32[]{:S(2)}) collective-permute-start(bf16[512,1024]{1,0:T(8,128)(2,1)} %collective-permute-done.10), channel_id=1, source_target_pairs={{0,16},{16,0},{1,17},{17,1},{2,18},{18,2},{3,19},{19,3},{4,20},{20... | collective-permute-start | bytes 3145736 | tf_op jit(solution)/shard_map/ppermute | solution.py:512
  288.5 26.8 %collective-permute-start.15 = (bf16[128,2048]{1,0:T(8,128)(2,1)S(1)}, bf16[128,2048]{1,0:T(8,128)(2,1)S(1)}, u32[]{:S(2)}, u32[]{:S(2)}) collective-permute-start(bf16[128,2048]{1,0:T(8,128)(2,1)S(1)} %fusion.15.part), channel_id=1, source_target_pairs={{0,8},{8,0},{1,9},{9,1},{2,10},{10,2},{3,11},{11,3},{4,12},{12,4},... | collective-permute-start | bytes 1572872 | tf_op jit(solution)/shard_map/ppermute | solution.py:97
  314.2 20.5 %collective-permute-start.25 = (bf16[128,2048]{1,0:T(8,128)(2,1)S(1)}, bf16[128,2048]{1,0:T(8,128)(2,1)}, u32[]{:S(2)}, u32[]{:S(2)}) collective-permute-start(bf16[128,2048]{1,0:T(8,128)(2,1)S(1)} %collective-permute-done.22.part), channel_id=1, source_target_pairs={{0,8},{8,0},{1,9},{9,1},{2,10},{10,2},{3,11},{11,3},{4,12},{12,4},... | collective-permute-start | bytes 1572872 | tf_op jit(solution)/shard_map/ppermute | solution.py:97
  429.1 24.1 %collective-permute-start.43 = (bf16[128,2048]{1,0:T(8,128)(2,1)S(1)}, bf16[128,2048]{1,0:T(8,128)(2,1)S(1)}, u32[]{:S(2)}, u32[]{:S(2)}) collective-permute-start(bf16[128,2048]{1,0:T(8,128)(2,1)S(1)} %add_convert_fusion.4), channel_id=1, source_target_pairs={{0,2},{2,6},{6,4},{4,0},{1,3},{3,7},{7,5},{5,1},{8,10},{10,14},{14... | collective-permute-start | bytes 1572872 | tf_op jit(solution)/shard_map/ppermute | solution.py:385
  470.5 213.8 %reduce-scatter.6.cloned.1.call-start = ((), (), s32[]{:S(2)}) async-start(), calls=%async_computation.18 | async-start | bytes 5242880 | tf_op jit(solution)/shard_map/reduce_scatter | solution.py:560
  525.3 23.5 %collective-permute-start.47 = (bf16[128,2048]{0,1:T(8,128)(2,1)}, bf16[128,2048]{0,1:T(8,128)(2,1)}, u32[]{:S(2)}, u32[]{:S(2)}) collective-permute-start(bf16[128,2048]{0,1:T(8,128)(2,1)} %bitcast.72), channel_id=1, source_target_pairs={{0,1},{1,0},{2,3},{3,2},{4,5},{5,4},{6,7},{7,6},{8,9},{9,8},{10,11... | collective-permute-start | bytes 1572872 | tf_op jit(solution)/shard_map/ppermute | solution.py:390
  529.4 23.4 %all-to-all-start.6 = ((bf16[8,128,256]{2,1,0:T(8,128)(2,1)}), bf16[8,128,256]{2,1,0:T(8,128)(2,1)}, u32[]{:S(2)}, u32[]{:S(2)}) async-start(bf16[8,128,256]{2,1,0:T(8,128)(2,1)} %bitcast.291), calls=%async_computation.6 | async-start | bytes 1048576 | tf_op jit(solution)/shard_map/all_to_all | solution.py:80
  534.2 236.7 %reduce-scatter.8.cloned.1.call-start = ((), (), s32[]{:S(2)}) async-start(), calls=%async_computation.19 | async-start | bytes 5242880 | tf_op jit(solution)/shard_map/reduce_scatter | solution.py:560
  547.6 30.4 %collective-permute-start.49 = (bf16[128,2048]{0,1:T(8,128)(2,1)}, bf16[128,2048]{0,1:T(8,128)(2,1)S(1)}, u32[]{:S(2)}, u32[]{:S(2)}) collective-permute-start(bf16[128,2048]{0,1:T(8,128)(2,1)} %collective-permute-done.48), channel_id=1, source_target_pairs={{0,1},{1,0},{2,3},{3,2},{4,5},{5,4},{6,7},{7,6},{8,9},{9,8},{10,11... | collective-permute-start | bytes 1572872 | tf_op jit(solution)/shard_map/ppermute | solution.py:390
  578.9 29.3 %collective-permute-start.53 = (bf16[128,2048]{0,1:T(8,128)(2,1)S(1)}, bf16[128,2048]{0,1:T(8,128)(2,1)S(1)}, u32[]{:S(2)}, u32[]{:S(2)}) collective-permute-start(bf16[128,2048]{0,1:T(8,128)(2,1)S(1)} %collective-permute-done.52), channel_id=1, source_target_pairs={{0,1},{1,0},{2,3},{3,2},{4,5},{5,4},{6,7},{7,6},{8,9},{9,8},{10,11... | collective-permute-start | bytes 1572872 | tf_op jit(solution)/shard_map/ppermute | solution.py:390
  622.1 80.7 %collective-permute-start.54 = (bf16[128,2048]{1,0:T(8,128)(2,1)}, bf16[128,2048]{1,0:T(8,128)(2,1)}, u32[]{:S(2)}, u32[]{:S(2)}) collective-permute-start(bf16[128,2048]{1,0:T(8,128)(2,1)} %pad_maximum_fusion.5), channel_id=1, source_target_pairs={{0,8},{8,0},{1,9},{9,1},{2,10},{10,2},{3,11},{11,3},{4,12},{12,4},... | collective-permute-start | bytes 1572872 | tf_op jit(solution)/shard_map/ppermute | solution.py:97
  638.3 43.5 %collective-permute-start.60 = (bf16[128,2048]{1,0:T(8,128)(2,1)}, bf16[128,2048]{1,0:T(8,128)(2,1)}, u32[]{:S(2)}, u32[]{:S(2)}) collective-permute-start(bf16[128,2048]{1,0:T(8,128)(2,1)} %fusion.13), channel_id=1, source_target_pairs={{0,1},{1,0},{2,3},{3,2},{4,5},{5,4},{6,7},{7,6},{8,9},{9,8},{10,11... | collective-permute-start | bytes 1572872 | tf_op jit(solution)/shard_map/ppermute | solution.py:434
  646.9 29.3 %all-to-all-start.8 = ((bf16[8,64,1024]{2,1,0:T(8,128)(2,1)}), bf16[8,64,1024]{2,1,0:T(8,128)(2,1)}, u32[]{:S(2)}, u32[]{:S(2)}) async-start(bf16[8,64,1024]{2,1,0:T(8,128)(2,1)} %bitcast.310), calls=%async_computation.9 | async-start | bytes 2097152 | tf_op jit(solution)/shard_map/all_to_all | solution.py:80
  656.7 43.5 %collective-permute-start.64 = (bf16[1024,768]{1,0:T(8,128)(2,1)}, bf16[1024,768]{1,0:T(8,128)(2,1)}, u32[]{:S(2)}, u32[]{:S(2)}) collective-permute-start(bf16[1024,768]{1,0:T(8,128)(2,1)} %pad_maximum_fusion.1), channel_id=1, source_target_pairs={{0,8},{8,0},{1,9},{9,1},{2,10},{10,2},{3,11},{11,3},{4,12},{12,4},... | collective-permute-start | bytes 4718600 | tf_op jit(solution)/shard_map/ppermute | solution.py:97
  659.0 47.9 %collective-permute-start.59 = (bf16[128,2048]{1,0:T(8,128)(2,1)}, bf16[128,2048]{1,0:T(8,128)(2,1)}, u32[]{:S(2)}, u32[]{:S(2)}) collective-permute-start(bf16[128,2048]{1,0:T(8,128)(2,1)} %fusion.12), channel_id=1, source_target_pairs={{0,1},{1,0},{2,3},{3,2},{4,5},{5,4},{6,7},{7,6},{8,9},{9,8},{10,11... | collective-permute-start | bytes 1572872 | tf_op jit(solution)/shard_map/ppermute | solution.py:434
  664.1 101.1 %collective-permute-start.58 = (bf16[128,2048]{1,0:T(8,128)(2,1)}, bf16[128,2048]{1,0:T(8,128)(2,1)}, u32[]{:S(2)}, u32[]{:S(2)}) collective-permute-start(bf16[128,2048]{1,0:T(8,128)(2,1)} %fusion.11), channel_id=1, source_target_pairs={{0,1},{1,0},{2,3},{3,2},{4,5},{5,4},{6,7},{7,6},{8,9},{9,8},{10,11... | collective-permute-start | bytes 1572872 | tf_op jit(solution)/shard_map/ppermute | solution.py:434
  684.1 22.8 %collective-permute-start.61 = (bf16[128,2048]{1,0:T(8,128)(2,1)}, bf16[128,2048]{1,0:T(8,128)(2,1)}, u32[]{:S(2)}, u32[]{:S(2)}) collective-permute-start(bf16[128,2048]{1,0:T(8,128)(2,1)} %fusion), channel_id=1, source_target_pairs={{0,2},{2,6},{6,4},{4,0},{1,3},{3,7},{7,5},{5,1},{8,10},{10,14},{14... | collective-permute-start | bytes 1572872 | tf_op jit(solution)/shard_map/ppermute | solution.py:385
  695.0 29.2 %all-to-all-start.11 = ((bf16[8,64,1024]{2,1,0:T(8,128)(2,1)}), bf16[8,64,1024]{2,1,0:T(8,128)(2,1)}, u32[]{:S(2)}, u32[]{:S(2)}) async-start(bf16[8,64,1024]{2,1,0:T(8,128)(2,1)} %bitcast.309), calls=%async_computation.13 | async-start | bytes 2097152 | tf_op jit(solution)/shard_map/all_to_all | solution.py:80
  702.7 18.9 %collective-permute-start.65 = (bf16[512,768]{1,0:T(8,128)(2,1)S(1)}, bf16[512,768]{1,0:T(8,128)(2,1)S(1)}, u32[]{:S(2)}, u32[]{:S(2)}) collective-permute-start(bf16[512,768]{1,0:T(8,128)(2,1)S(1)} %constant_dynamic-slice_fusion), channel_id=1, source_target_pairs={{0,16},{16,0},{1,17},{17,1},{2,18},{18,2},{3,19},{19,3},{4,20},{20... | collective-permute-start | bytes 2359304 | tf_op jit(solution)/shard_map/ppermute | solution.py:579
  705.5 25.0 %collective-permute-start.55 = (bf16[64,2048]{1,0:T(8,128)(2,1)}, bf16[64,2048]{1,0:T(8,128)(2,1)}, u32[]{:S(2)}, u32[]{:S(2)}) collective-permute-start(bf16[64,2048]{1,0:T(8,128)(2,1)} %constant_dynamic-slice_fusion.8), channel_id=1, source_target_pairs={{0,16},{16,0},{1,17},{17,1},{2,18},{18,2},{3,19},{19,3},{4,20},{20... | collective-permute-start | bytes 786440 | tf_op jit(solution)/shard_map/ppermute | solution.py:579
  709.1 56.1 %collective-permute-start.62 = (bf16[128,2048]{1,0:T(8,128)(2,1)}, bf16[128,2048]{1,0:T(8,128)(2,1)}, u32[]{:S(2)}, u32[]{:S(2)}) collective-permute-start(bf16[128,2048]{1,0:T(8,128)(2,1)} %fusion.2), channel_id=1, source_target_pairs={{0,2},{2,6},{6,4},{4,0},{1,3},{3,7},{7,5},{5,1},{8,10},{10,14},{14... | collective-permute-start | bytes 1572872 | tf_op jit(solution)/shard_map/ppermute | solution.py:385
  724.2 46.6 %all-to-all-start.9 = ((bf16[8,64,768]{2,1,0:T(8,128)(2,1)}), bf16[8,64,768]{2,1,0:T(8,128)(2,1)}, u32[]{:S(2)}, u32[]{:S(2)}) async-start(bf16[8,64,768]{2,1,0:T(8,128)(2,1)} %bitcast.280), calls=%async_computation.10 | async-start | bytes 1572864 | tf_op jit(solution)/shard_map/all_to_all | solution.py:80
  732.3 31.2 %collective-permute-start.56 = (bf16[64,2048]{1,0:T(8,128)(2,1)}, bf16[64,2048]{1,0:T(8,128)(2,1)}, u32[]{:S(2)}, u32[]{:S(2)}) collective-permute-start(bf16[64,2048]{1,0:T(8,128)(2,1)} %add_convert_fusion.8), channel_id=1, source_target_pairs={{0,0},{1,4},{2,8},{3,12},{4,16},{5,20},{6,24},{7,28},{8,1},{9,5},{... | collective-permute-start | bytes 786440 | tf_op jit(solution)/shard_map/ppermute | solution.py:615
  767.7 21.5 %collective-permute-start.63 = (bf16[128,2048]{1,0:T(8,128)(2,1)}, bf16[128,2048]{1,0:T(8,128)(2,1)}, u32[]{:S(2)}, u32[]{:S(2)}) collective-permute-start(bf16[128,2048]{1,0:T(8,128)(2,1)} %fusion.4), channel_id=1, source_target_pairs={{0,2},{2,6},{6,4},{4,0},{1,3},{3,7},{7,5},{5,1},{8,10},{10,14},{14... | collective-permute-start | bytes 1572872 | tf_op jit(solution)/shard_map/ppermute | solution.py:385
  770.8 34.4 %all-to-all-start.12 = ((bf16[8,64,1024]{2,1,0:T(8,128)(2,1)}), bf16[8,64,1024]{2,1,0:T(8,128)(2,1)}, u32[]{:S(2)}, u32[]{:S(2)}) async-start(bf16[8,64,1024]{2,1,0:T(8,128)(2,1)} %bitcast.311), calls=%async_computation.15 | async-start | bytes 2097152 | tf_op jit(solution)/shard_map/all_to_all | solution.py:80
  (110 other events, 1191.1 us)
Sparse Core Ops, SparseCore 0:
  197.7 90.7 all-gather.1
  470.7 53.7 reduce-scatter.3
  527.7 84.0 reduce-scatter.5
  614.6 68.5 reduce-scatter.7
